TPU v7x, 32 devices: a whole 2x2x4 slice. The times are simulated.
32 devices in a mesh: ctx: 8 (over y, x, core), fsdp: 4 (over z).
Axes of the slice: x: 2, y: 2, z: 4, core: 2. Of those that a mesh axis runs over, the one named last changes fastest.
Arguments:
- tokens: bfloat16 [4, 1024, 2048], P('fsdp', 'ctx'), may hold values from -6 to 6
- doc_lengths: int32 [4, 4], P('fsdp'), may hold values from 1 to 896, as said below
- norm1_gain: float32 [2048], P(('ctx', 'fsdp')), may hold values from 0.5 to 1.5
- w_query: bfloat16 [2048, 2048], P(('ctx', 'fsdp')), may hold values from -0.125 to 0.125
- w_key: bfloat16 [2048, 2048], P(('ctx', 'fsdp')), may hold values from -0.125 to 0.125
- w_value: bfloat16 [2048, 2048], P(('ctx', 'fsdp')), may hold values from -0.125 to 0.125
- w_out: bfloat16 [2048, 2048], P(('ctx', 'fsdp')), may hold values from -2 to 2
- norm2_gain: float32 [2048], P(('ctx', 'fsdp')), may hold values from 0.5 to 1.5
- w_gate: bfloat16 [2048, 8192], P(('ctx', 'fsdp')), may hold values from -0.125 to 0.125
- w_up: bfloat16 [2048, 8192], P(('ctx', 'fsdp')), may hold values from -0.125 to 0.125
- w_down: bfloat16 [8192, 2048], P(('ctx', 'fsdp')), may hold values from -0.0625 to 0.0625
- cotangent: bfloat16 [4, 1024, 2048], P('fsdp', 'ctx'), may hold values from -6 to 6
Outputs:
- layer_out: bfloat16 [4, 1024, 2048], P('fsdp', 'ctx')
- grad_tokens: float32 [4, 1024, 2048], P('fsdp', 'ctx')
- grad_norm1_gain: float32 [2048], P(('ctx', 'fsdp'))
- grad_query: float32 [2048, 2048], P(('ctx', 'fsdp'))
- grad_key: float32 [2048, 2048], P(('ctx', 'fsdp'))
- grad_value: float32 [2048, 2048], P(('ctx', 'fsdp'))
- grad_out: float32 [2048, 2048], P(('ctx', 'fsdp'))
- grad_norm2_gain: float32 [2048], P(('ctx', 'fsdp'))
- grad_gate: float32 [2048, 8192], P(('ctx', 'fsdp'))
- grad_up: float32 [2048, 8192], P(('ctx', 'fsdp'))
- grad_down: float32 [8192, 2048], P(('ctx', 'fsdp'))
Inputs may be any that keep to these rules, and one draw needn't show every extreme that they name: `doc_lengths`: each row holds 4 document lengths that sum to 1024; the first is more than half of 1024.
All inputs are finite; a program needn't handle non-finite values.
Results may differ from a plain program's by a relative error of at most 0.015.
Values may be sent and summed in bfloat16 or wider, within the bound.
No kernel may reach another device: no remote copies, remote signals or barrier semaphores. Data moves between devices by JAX's collectives and lax.ppermute only.
A program may use at most 704 MiB of HBM per device.

v0:
```python
import math

import jax
import jax.numpy as jnp
from jax import lax
from jax.sharding import PartitionSpec as P

HEAD_DIM = 64


EPSILON = 1e-05
THETA = 130000.0
MASKED = -1e30


def norm_apply(values, gain_row):
    inverse = lax.rsqrt(jnp.mean(values * values, axis=-1, keepdims=True) + EPSILON)
    return (values * inverse * gain_row, inverse)


def norm_back(values, inverse, gain_row, upstream):
    scaled = upstream * gain_row
    inner_sum = jnp.mean(scaled * values, axis=-1, keepdims=True)
    inward = inverse * scaled - values * (inverse * inverse * inverse) * inner_sum
    gain_term = jnp.sum(upstream * values * inverse, axis=0)
    return (inward, gain_term)


def dealt_place(owner_rank, within, block_len, block_count):
    return jnp.where(
        within < block_len,
        owner_rank * block_len + within,
        (block_count - 1 - owner_rank) * block_len + within - block_len,
    )


def doc_tables(token_place, lengths, doc_count):
    doc_ends = jnp.cumsum(lengths)
    passed = (token_place[:, None] >= doc_ends[None, : doc_count - 1]).astype(jnp.int32)
    doc_index = jnp.sum(passed, axis=1)
    start_place = jnp.sum(passed * lengths[None, : doc_count - 1], axis=1)
    return (doc_index, token_place - start_place)


def rope_tables(rope_place, head_size):
    half_dim = head_size // 2
    frequency = jnp.power(THETA, -2.0 * jnp.arange(half_dim, dtype=jnp.float32) / head_size)
    angles = rope_place.astype(jnp.float32)[:, None] * frequency[None, :]
    return (jnp.cos(angles)[:, None, :], jnp.sin(angles)[:, None, :])


def rope_turn(values, cosine_table, sine_table, head_count, direction):
    row_count = values.shape[0]
    shaped = values.reshape(row_count, head_count, -1)
    half_dim = shaped.shape[2] // 2
    first_half = shaped[:, :, :half_dim]
    second_half = shaped[:, :, half_dim:]
    turned = jnp.concatenate(
        [
            first_half * cosine_table - direction * second_half * sine_table,
            second_half * cosine_table + direction * first_half * sine_table,
        ],
        axis=2,
    )
    return turned.reshape(row_count, -1)


def local(
    tokens,
    doc_lengths,
    norm1_gain,
    w_query,
    w_key,
    w_value,
    w_out,
    norm2_gain,
    w_gate,
    w_up,
    w_down,
    cotangent,
):
    ctx_count = lax.axis_size("ctx")
    ctx_rank = lax.axis_index("ctx")
    local_rows = tokens.shape[1]
    block_len = local_rows // 2
    model_width = tokens.shape[2]
    ff_width = w_gate.shape[1]
    head_size = HEAD_DIM
    head_count = model_width // head_size
    group_size = min(4, head_count)
    group_width = group_size * head_size
    group_total = head_count // group_size
    score_scale = 1.0 / math.sqrt(head_size)
    seq_rows = local_rows * ctx_count
    lengths = doc_lengths[0]
    doc_count = lengths.shape[0]
    row_ids = jnp.arange(local_rows, dtype=jnp.int32)
    query_place = dealt_place(ctx_rank, row_ids, block_len, 2 * ctx_count)
    key_ids = jnp.arange(seq_rows, dtype=jnp.int32)
    key_place = dealt_place(key_ids // local_rows, key_ids % local_rows, block_len, 2 * ctx_count)
    query_doc, query_rope = doc_tables(query_place, lengths, doc_count)
    key_doc = doc_tables(key_place, lengths, doc_count)[0]
    allowed = (key_place[None, :] <= query_place[:, None]) & (
        key_doc[None, :] == query_doc[:, None]
    )
    cosine_table, sine_table = rope_tables(query_rope, head_size)
    token_rows = tokens[0].astype(jnp.float32)
    attn_weights = (
        lax.all_gather(w_query, ("ctx", "fsdp"), axis=0, tiled=True),
        lax.all_gather(w_key, ("ctx", "fsdp"), axis=0, tiled=True),
        lax.all_gather(w_value, ("ctx", "fsdp"), axis=0, tiled=True),
        lax.all_gather(w_out, ("ctx", "fsdp"), axis=0, tiled=True),
    )
    gains = (
        lax.all_gather(norm1_gain, ("ctx", "fsdp"), axis=0, tiled=True),
        lax.all_gather(norm2_gain, ("ctx", "fsdp"), axis=0, tiled=True),
    )
    normed1, inverse1 = norm_apply(token_rows, gains[0])
    attn_in = normed1.astype(jnp.bfloat16)
    query_rows = rope_turn(
        jnp.dot(attn_in, attn_weights[0], preferred_element_type=jnp.float32),
        cosine_table,
        sine_table,
        head_count,
        1.0,
    ).astype(jnp.bfloat16)
    key_rows = rope_turn(
        jnp.dot(attn_in, attn_weights[1], preferred_element_type=jnp.float32),
        cosine_table,
        sine_table,
        head_count,
        1.0,
    ).astype(jnp.bfloat16)
    value_rows = jnp.dot(attn_in, attn_weights[2], preferred_element_type=jnp.float32).astype(
        jnp.bfloat16
    )
    all_keys, all_values = (
        lax.all_gather(key_rows, "ctx", axis=0, tiled=True),
        lax.all_gather(value_rows, "ctx", axis=0, tiled=True),
    )

    def group_slices(group_index):
        offset = group_index * group_width
        query_part = lax.dynamic_slice_in_dim(query_rows, offset, group_width, 1).reshape(
            local_rows, group_size, head_size
        )
        key_part = lax.dynamic_slice_in_dim(all_keys, offset, group_width, 1).reshape(
            seq_rows, group_size, head_size
        )
        value_part = lax.dynamic_slice_in_dim(all_values, offset, group_width, 1).reshape(
            seq_rows, group_size, head_size
        )
        scores = (
            jnp.einsum("qhd,khd->hqk", query_part, key_part, preferred_element_type=jnp.float32)
            * score_scale
        )
        scores = jnp.where(allowed[None], scores, MASKED)
        return (offset, query_part, key_part, value_part, scores)

    def forward_group(group_index, carried):
        mixed_acc, lse_acc = carried
        offset, query_part, key_part, value_part, scores = group_slices(group_index)
        row_max = jnp.max(scores, axis=-1, keepdims=True)
        exp_scores = jnp.where(allowed[None], jnp.exp(scores - row_max), 0.0)
        row_total = jnp.sum(exp_scores, axis=-1, keepdims=True)
        prob_low = (exp_scores / row_total).astype(jnp.bfloat16)
        mixed_part = jnp.einsum(
            "hqk,khd->qhd", prob_low, value_part, preferred_element_type=jnp.float32
        )
        mixed_acc = lax.dynamic_update_slice_in_dim(
            mixed_acc, mixed_part.reshape(local_rows, group_width), offset, 1
        )
        lse_acc = lax.dynamic_update_slice_in_dim(
            lse_acc, (row_max + jnp.log(row_total))[..., 0], group_index * group_size, 0
        )
        return (mixed_acc, lse_acc)

    mixed_acc, log_totals = lax.fori_loop(
        0,
        group_total,
        forward_group,
        (
            jnp.zeros((local_rows, model_width), jnp.float32),
            jnp.zeros((head_count, local_rows), jnp.float32),
        ),
    )
    mixed = mixed_acc.astype(jnp.bfloat16)
    hidden1 = token_rows + jnp.dot(mixed, attn_weights[3], preferred_element_type=jnp.float32)
    normed2, inverse2 = norm_apply(hidden1, gains[1])
    mlp_in = normed2.astype(jnp.bfloat16)
    pieces = (
        lax.all_gather(w_gate, ("ctx", "fsdp"), axis=0, tiled=True),
        lax.all_gather(w_up, ("ctx", "fsdp"), axis=0, tiled=True),
    )
    columns = mlp_in
    gate_proj = jnp.dot(columns, pieces[0], preferred_element_type=jnp.float32)
    up_proj = jnp.dot(columns, pieces[1], preferred_element_type=jnp.float32)
    sigmoid_gate = jax.nn.sigmoid(gate_proj)
    silu_gate = gate_proj * sigmoid_gate
    activation = (silu_gate * up_proj).astype(jnp.bfloat16)
    columns = activation
    layer_out = hidden1 + jnp.dot(
        columns,
        lax.all_gather(w_down, ("ctx", "fsdp"), axis=0, tiled=True),
        preferred_element_type=jnp.float32,
    )
    upstream = cotangent[0]
    columns = activation
    down_grad = lax.psum_scatter(
        jnp.einsum("tf,td->fd", columns, upstream, preferred_element_type=jnp.float32),
        ("ctx", "fsdp"),
        scatter_dimension=0,
        tiled=True,
    )
    act_grad = jnp.einsum(
        "td,fd->tf",
        upstream,
        lax.all_gather(w_down, ("ctx", "fsdp"), axis=0, tiled=True),
        preferred_element_type=jnp.float32,
    )
    gate_low = (
        act_grad * up_proj * sigmoid_gate * (1.0 + gate_proj * (1.0 - sigmoid_gate))
    ).astype(jnp.bfloat16)
    up_low = (act_grad * silu_gate).astype(jnp.bfloat16)
    columns = mlp_in
    gate_up_grad = lax.psum_scatter(
        jnp.concatenate(
            [
                jnp.einsum("td,tf->df", columns, gate_low, preferred_element_type=jnp.float32),
                jnp.einsum("td,tf->df", columns, up_low, preferred_element_type=jnp.float32),
            ],
            axis=1,
        ),
        ("ctx", "fsdp"),
        scatter_dimension=0,
        tiled=True,
    )
    gate_grad = gate_up_grad[:, :ff_width]
    up_grad = gate_up_grad[:, ff_width:]
    pieces = (
        lax.all_gather(w_gate, ("ctx", "fsdp"), axis=0, tiled=True),
        lax.all_gather(w_up, ("ctx", "fsdp"), axis=0, tiled=True),
    )
    part = jnp.einsum(
        "tf,df->td", gate_low, pieces[0], preferred_element_type=jnp.float32
    ) + jnp.einsum("tf,df->td", up_low, pieces[1], preferred_element_type=jnp.float32)
    hidden_back, gain2_term = norm_back(hidden1, inverse2, gains[1], part)
    hidden1_grad = upstream.astype(jnp.float32) + hidden_back
    hidden_low = hidden1_grad.astype(jnp.bfloat16)
    back_attn = (
        lax.all_gather(w_query, ("ctx", "fsdp"), axis=0, tiled=True),
        lax.all_gather(w_key, ("ctx", "fsdp"), axis=0, tiled=True),
        lax.all_gather(w_value, ("ctx", "fsdp"), axis=0, tiled=True),
        lax.all_gather(w_out, ("ctx", "fsdp"), axis=0, tiled=True),
    )
    mixed_low = jnp.einsum(
        "te,de->td", hidden_low, back_attn[3], preferred_element_type=jnp.float32
    ).astype(jnp.bfloat16)

    def backward_group(group_index, carried):
        query_acc, key_acc, value_acc = carried
        offset, query_part, key_part, value_part, scores = group_slices(group_index)
        mixed_part = lax.dynamic_slice_in_dim(mixed_low, offset, group_width, 1).reshape(
            local_rows, group_size, head_size
        )
        lse_part = lax.dynamic_slice_in_dim(log_totals, group_index * group_size, group_size, 0)[
            ..., None
        ]
        probs = jnp.where(allowed[None], jnp.exp(scores - lse_part), 0.0)
        prob_grad = jnp.einsum(
            "qhd,khd->hqk", mixed_part, value_part, preferred_element_type=jnp.float32
        )
        inner_sum = jnp.sum(probs * prob_grad, axis=-1, keepdims=True)
        score_low = (probs * (prob_grad - inner_sum) * score_scale).astype(jnp.bfloat16)
        query_part_grad = jnp.einsum(
            "hqk,khd->qhd", score_low, key_part, preferred_element_type=jnp.float32
        )
        key_part_grad = jnp.einsum(
            "hqk,qhd->khd", score_low, query_part, preferred_element_type=jnp.float32
        )
        value_part_grad = jnp.einsum(
            "hqk,qhd->khd",
            probs.astype(jnp.bfloat16),
            mixed_part,
            preferred_element_type=jnp.float32,
        )
        query_acc = lax.dynamic_update_slice_in_dim(
            query_acc, query_part_grad.reshape(local_rows, group_width), offset, 1
        )
        key_acc = lax.dynamic_update_slice_in_dim(
            key_acc, key_part_grad.reshape(seq_rows, group_width), offset, 1
        )
        value_acc = lax.dynamic_update_slice_in_dim(
            value_acc, value_part_grad.reshape(seq_rows, group_width), offset, 1
        )
        return (query_acc, key_acc, value_acc)

    query_acc, key_acc, value_acc = lax.fori_loop(
        0,
        group_total,
        backward_group,
        (
            jnp.zeros((local_rows, model_width), jnp.float32),
            jnp.zeros((seq_rows, model_width), jnp.float32),
            jnp.zeros((seq_rows, model_width), jnp.float32),
        ),
    )
    key_sum, value_sum = (
        lax.psum_scatter(
            key_acc.astype(jnp.bfloat16), "ctx", scatter_dimension=0, tiled=True
        ).astype(jnp.float32),
        lax.psum_scatter(
            value_acc.astype(jnp.bfloat16), "ctx", scatter_dimension=0, tiled=True
        ).astype(jnp.float32),
    )
    query_low = rope_turn(query_acc, cosine_table, sine_table, head_count, -1.0).astype(
        jnp.bfloat16
    )
    key_low = rope_turn(key_sum, cosine_table, sine_table, head_count, -1.0).astype(jnp.bfloat16)
    value_low = value_sum.astype(jnp.bfloat16)
    columns = attn_in
    attn_grads = lax.psum_scatter(
        jnp.concatenate(
            [
                jnp.einsum("td,te->de", columns, query_low, preferred_element_type=jnp.float32),
                jnp.einsum("td,te->de", columns, key_low, preferred_element_type=jnp.float32),
                jnp.einsum("td,te->de", columns, value_low, preferred_element_type=jnp.float32),
                jnp.einsum("td,te->de", mixed, hidden_low, preferred_element_type=jnp.float32),
            ],
            axis=1,
        ),
        ("ctx", "fsdp"),
        scatter_dimension=0,
        tiled=True,
    )
    in_grad = (
        jnp.einsum("te,de->td", query_low, back_attn[0], preferred_element_type=jnp.float32)
        + jnp.einsum("te,de->td", key_low, back_attn[1], preferred_element_type=jnp.float32)
        + jnp.einsum("te,de->td", value_low, back_attn[2], preferred_element_type=jnp.float32)
    )
    token_back, gain1_term = norm_back(token_rows, inverse1, gains[0], in_grad)
    gain1_grad, gain2_grad = (
        lax.psum_scatter(gain1_term, ("ctx", "fsdp"), scatter_dimension=0, tiled=True),
        lax.psum_scatter(gain2_term, ("ctx", "fsdp"), scatter_dimension=0, tiled=True),
    )
    token_grad = hidden1_grad + token_back
    return (
        layer_out.astype(jnp.bfloat16)[None],
        token_grad[None],
        gain1_grad,
        attn_grads[:, :model_width],
        attn_grads[:, model_width : 2 * model_width],
        attn_grads[:, 2 * model_width : 3 * model_width],
        attn_grads[:, 3 * model_width :],
        gain2_grad,
        gate_grad,
        up_grad,
        down_grad,
    )


def solution(mesh):
    placed = (
        P("fsdp", "ctx", None),
        P("fsdp", None),
        P(("ctx", "fsdp")),
        P(("ctx", "fsdp"), None),
        P(("ctx", "fsdp"), None),
        P(("ctx", "fsdp"), None),
        P(("ctx", "fsdp"), None),
        P(("ctx", "fsdp")),
        P(("ctx", "fsdp"), None),
        P(("ctx", "fsdp"), None),
        P(("ctx", "fsdp"), None),
        P("fsdp", "ctx", None),
    )
    return jax.shard_map(
        local,
        mesh=mesh,
        in_specs=placed,
        out_specs=(
            P("fsdp", "ctx", None),
            P("fsdp", "ctx", None),
            P(("ctx", "fsdp")),
            P(("ctx", "fsdp"), None),
            P(("ctx", "fsdp"), None),
            P(("ctx", "fsdp"), None),
            P(("ctx", "fsdp"), None),
            P(("ctx", "fsdp")),
            P(("ctx", "fsdp"), None),
            P(("ctx", "fsdp"), None),
            P(("ctx", "fsdp"), None),
        ),
        check_vma=False,
    )
```

profile of v0, /device:TPU:0, one launch (start us, length us, event | category | flops | bytes accessed | tf_op | source)
XLA Modules:
  0.0 6058.3 jit_solution(12525693602919006422)
XLA Ops:
  11.2 43.3 all-reduce.6
  56.2 35.0 all-gather.10.cloned.1.call-done
  91.3 5.7 convolution_convert_fusion.1
  98.1 72.1 %all-gather.16.cloned.1.call-done = bf16[2048,2048]{1,0:T(8,128)(2,1)} async-done(((bf16[64,2048]{1,0:T(8,128)(2,1)}), bf16[2048,2048]{1,0:T(8,128)(2,1)}) %all-gather.16.cloned.1.call-update) | async-done | bytes 8388624 | tf_op jit(solution)/shard_map/all_gather | solution.py:110
  170.2 12.3 copy.42
  182.6 66.6 %all-gather.14.cloned.1.call-done = bf16[2048,2048]{1,0:T(8,128)(2,1)} async-done(((bf16[64,2048]{1,0:T(8,128)(2,1)}), bf16[2048,2048]{1,0:T(8,128)(2,1)}) %all-gather.14.cloned.1.call-update) | async-done | bytes 8388624 | tf_op jit(solution)/shard_map/all_gather | solution.py:109
  249.2 12.4 copy.41
  261.6 6.0 fusion.52
  275.2 11.7 all-gather.12.cloned.1.call-done
  286.8 6.4 copy.43
  293.3 33.3 all-gather.18.cloned.1.call-done
  326.6 36.9 while.34
  363.5 43.4 all-gather.20.cloned.1.call-done
  406.9 4.7 multiply_reduce_fusion.3
  411.8 191.4 %all-gather.22.cloned.1.call-done = bf16[2048,8192]{1,0:T(8,128)(2,1)} async-done(((bf16[64,8192]{1,0:T(8,128)(2,1)}), bf16[2048,8192]{1,0:T(8,128)(2,1)}) %all-gather.22.cloned.1.call-update) | async-done | bytes 33554448 | tf_op jit(solution)/shard_map/all_gather | solution.py:192
  603.2 17.8 fusion.92
  621.0 178.1 %all-gather.24.cloned.1.call-done = bf16[2048,8192]{1,0:T(8,128)(2,1)} async-done(((bf16[64,8192]{1,0:T(8,128)(2,1)}), bf16[2048,8192]{1,0:T(8,128)(2,1)}) %all-gather.24.cloned.1.call-update) | async-done | bytes 33554448 | tf_op jit(solution)/shard_map/all_gather | solution.py:193
  799.1 17.8 fusion.93
  816.9 178.2 %all-gather.26.cloned.1.call-done = bf16[8192,2048]{1,0:T(8,128)(2,1)} async-done(((bf16[256,2048]{1,0:T(8,128)(2,1)}), bf16[8192,2048]{1,0:T(8,128)(2,1)}) %all-gather.26.cloned.1.call-update) | async-done | bytes 33554448 | tf_op jit(solution)/shard_map/all_gather | solution.py:204
  995.1 21.3 multiply_convert_fusion.1
  1016.4 17.4 fusion.94
  1033.8 17.0 multiply_reduce_fusion.1
  1052.2 7.5 convolution_convert_fusion
  1060.7 2.5 broadcast.351
  1063.3 2.6 broadcast.351.clone
  1065.8 131.7 %while.35 = (s32[]{:T(128)}, f32[128,2048]{0,1:T(8,128)}, bf16[1024,2048]{0,1:T(8,128)(2,1)}, bf16[1024,2048]{0,1:T(8,128)(2,1)}, bf16[1024,2048]{0,1:T(8,128)(2...) while((s32[]{:T(128)}, f32[128,2048]{0,1:T(8,128)}, ...), condition=%wide.region_13.14_spmd.clone, body=%wide.region_11.13_spmd.clone.sunk | while | flops 343804928 | bytes 22822188 | solution.py:298
  1072.9 2.9 fusion.177
  1076.7 3.6 fusion.179
  1089.3 2.9 fusion.177
  1093.1 3.6 fusion.179
  1105.7 2.9 fusion.177
  1109.6 3.6 fusion.179
  1122.1 2.9 fusion.177
  1126.0 3.6 fusion.179
  1138.6 2.9 fusion.177
  1142.4 3.6 fusion.179
  1155.0 2.9 fusion.177
  1158.8 3.6 fusion.179
  1171.4 2.9 fusion.177
  1175.2 3.6 fusion.179
  1187.8 2.9 fusion.177
  1191.7 3.6 fusion.179
  1197.5 6.5 copy.50
  1204.1 6.7 copy.52
  1210.8 24.5 fusion.97
  1235.3 23.7 fusion.96
  1259.1 89.0 %pad_maximum_fusion = f32[2048,16384]{1,0:T(8,128)} fusion(f32[2048,8192]{1,0:T(8,128)} %fusion.97, f32[2048,8192]{1,0:T(8,128)} %fusion.96), kind=kLoop, calls=%fused_computation.41 | loop fusion | flops 33554432 | bytes 268435456 | tf_op jit(solution)/shard_map/concatenate | solution.py:227
  1349.5 8.9 fusion.60
  1360.5 8.2 fusion.58
  1368.7 8.5 fusion.56
  1377.2 11.0 fusion.65
  1388.2 41.6 pad_maximum_fusion.1
  1429.8 61.4 %copy.54 = f32[2048,8192]{1,0:T(8,128)} copy(f32[2048,8192]{0,1:T(8,128)} %pad_maximum_fusion.1) | data formatting | bytes 134217728
  1493.0 25.9 fusion.48
  1520.2 14.3 fusion.30
  1534.5 6.6 fusion.95
  1541.1 6.6 convolution_add_fusion.3
  1547.9 3.1 fusion.45
  1550.9 42.3 all-reduce.5
  1595.8 1629.8 %all-reduce.9.cloned.1.call-done = f32[2048,16384]{1,0:T(8,128)} async-done(((f32[2048,16384]{1,0:T(8,128)}), f32[2048,16384]{1,0:T(8,128)}) %all-reduce.9.cloned.1.call-update) | async-done | bytes 134217744
  3225.6 4.9 fusion.89
  3230.5 1407.4 %reduce-scatter.17.cloned.1.call-done = f32[64,8192]{1,0:T(8,128)} async-done(((f32[2048,8192]{1,0:T(8,128)}), f32[64,8192]{1,0:T(8,128)}) %reduce-scatter.17.cloned.1.call-update) | async-done | bytes 2097168
  4637.9 2.9 fusion.90
  4640.7 1410.6 %reduce-scatter.11.cloned.1.call-done = f32[256,2048]{1,0:T(8,128)} async-done(((f32[8192,2048]{1,0:T(8,128)}), f32[256,2048]{1,0:T(8,128)}) %reduce-scatter.11.cloned.1.call-update) | async-done | bytes 2097168 | tf_op jit(solution)/shard_map/reduce_scatter | solution.py:209
  (302 shorter events, 141.1 us)
Async XLA Ops:
  7.2 84.1 %all-gather.10.cloned.1.call-start = ((), (), s32[]{:S(2)}) async-start(), calls=%async_computation.4 | async-start | bytes 8650752 | tf_op jit(solution)/shard_map/all_gather | solution.py:111
  7.9 162.3 %all-gather.16.cloned.1.call-start = ((), (), s32[]{:S(2)}) async-start(), calls=%async_computation.7 | async-start | bytes 8650752 | tf_op jit(solution)/shard_map/all_gather | solution.py:110
  8.7 240.5 %all-gather.14.cloned.1.call-start = ((), (), s32[]{:S(2)}) async-start(), calls=%async_computation.6 | async-start | bytes 8650752 | tf_op jit(solution)/shard_map/all_gather | solution.py:109
  9.4 277.4 %all-gather.12.cloned.1.call-start = ((), (), s32[]{:S(2)}) async-start(), calls=%async_computation.5 | async-start | bytes 4718592 | tf_op jit(solution)/shard_map/all_gather | solution.py:139
  54.5 213.1 %copy-start.24 = (f32[2048]{0:T(1024)}, f32[2048]{0:T(1024)S(1)}, u32[]{:S(2)}) copy-start(f32[2048]{0:T(1024)S(1)} %get-tuple-element.526) | copy-start | bytes 24580
  56.2 211.4 %copy-start.30 = (f32[128]{0:T(128)}, f32[128]{0:T(128)S(1)}, u32[]{:S(2)}) copy-start(f32[128]{0:T(128)S(1)} %get-tuple-element.559) | copy-start | bytes 1540
  91.3 5.8 copy-start.35
  97.0 229.6 %all-gather.18.cloned.1.call-start = ((), (), s32[]{:S(2)}) async-start(), calls=%async_computation.8 | async-start | bytes 4718592 | tf_op jit(solution)/shard_map/all_gather | solution.py:138
  98.1 172.0 %copy-start.27 = (f32[128,32]{0,1:T(8,128)}, f32[128,32]{0,1:T(8,128)S(1)}, u32[]{:S(2)}) copy-start(f32[128,32]{0,1:T(8,128)S(1)} %get-tuple-element.557) | copy-start | bytes 49156
  249.2 12.4 copy-start.1
  261.6 6.0 copy-start.4
  271.3 135.6 %all-gather.20.cloned.1.call-start = ((), (), s32[]{:S(2)}) async-start(), calls=%async_computation.9 | async-start | bytes 8650752 | tf_op jit(solution)/shard_map/all_gather | solution.py:112
  271.9 331.3 %all-gather.22.cloned.1.call-start = ((), (), s32[]{:S(2)}) async-start(), calls=%async_computation.10 | async-start | bytes 34603008 | tf_op jit(solution)/shard_map/all_gather | solution.py:192
  272.6 526.5 %all-gather.24.cloned.1.call-start = ((), (), s32[]{:S(2)}) async-start(), calls=%async_computation.11 | async-start | bytes 34603008 | tf_op jit(solution)/shard_map/all_gather | solution.py:193
  273.4 721.7 %all-gather.26.cloned.1.call-start = ((), (), s32[]{:S(2)}) async-start(), calls=%async_computation.12 | async-start | bytes 34603008 | tf_op jit(solution)/shard_map/all_gather | solution.py:204
  274.1 1084.3 %reduce-scatter.13.cloned.1.call-start = ((), (), s32[]{:S(2)}) async-start(), calls=%async_computation.14 | async-start | bytes 4718592
  363.5 48.2 copy-start.14
  411.6 639.2 %copy-start.5 = (f32[128,2048]{1,0:T(8,128)}, f32[128,2048]{1,0:T(8,128)S(1)}, u32[]{:S(2)}) copy-start(f32[128,2048]{1,0:T(8,128)S(1)} %get-tuple-element.563) | copy-start | bytes 3145732
  621.0 374.1 %copy-start.22 = (bf16[1,128,2048]{2,1,0:T(8,128)(2,1)S(1)}, bf16[1,128,2048]{2,1,0:T(8,128)(2,1)}, u32[]{:S(2)}) copy-start(bf16[1,128,2048]{2,1,0:T(8,128)(2,1)} %param.27) | copy-start | bytes 1572868
  1016.4 17.4 copy-start.12
  1052.2 7.5 copy-start.7
  1204.0 173.2 %reduce-scatter.15.cloned.1.call-start = ((), (), s32[]{:S(2)}) async-start(), calls=%async_computation.15 | async-start | bytes 4718592
  1204.1 6.7 copy-start.13
  1210.8 24.6 copy-start.11
  1259.1 1966.5 %all-reduce.9.cloned.1.call-start = ((), (), s32[]{:S(2)}) async-start(), calls=%async_computation.17 | async-start | bytes 268435456
  1348.1 1.2 copy-start.8
  1348.2 1.4 copy-start.15
  1348.2 11.8 copy-start.20
  1348.2 11.8 copy-start.28
  1348.2 11.8 copy-start.29
  1348.2 3289.7 %reduce-scatter.17.cloned.1.call-start = ((), (), s32[]{:S(2)}) async-start(), calls=%async_computation.16 | async-start | bytes 69206016
  1358.4 2.0 copy-start.2
  1358.4 2.0 copy-start.25
  1358.5 2.0 copy-start.31
  1360.4 8.3 copy-start.18
  1360.4 8.3 copy-start.16
  1377.2 11.0 copy-start
  1491.3 1.6 copy-start.10
  1491.3 1.7 copy-start.23
  1491.3 4560.0 %reduce-scatter.11.cloned.1.call-start = ((), (), s32[]{:S(2)}) async-start(), calls=%async_computation.13 | async-start | bytes 69206016 | tf_op jit(solution)/shard_map/reduce_scatter | solution.py:209
  1518.9 1.3 copy-start.6
  1520.2 14.3 copy-start.17
  1534.5 6.6 copy-start.19
  1534.5 13.3 slice-start
  1541.1 6.7 slice-start.1
  1541.1 6.7 copy-start.3
  1541.1 6.7 copy-start.21
  1541.1 6.7 copy-start.26
  1541.1 6.7 copy-start.32
  1547.8 3.1 copy-start.33
  1547.8 46.5 copy-start.9
  1547.8 46.5 copy-start.34
Sparse Core Ops, SparseCore 0:
  10.9 80.2 all-gather.9
  94.2 75.9 all-gather.15
  173.2 75.9 all-gather.13
  251.5 35.2 all-gather.11
  289.1 37.4 all-gather.17
  329.4 77.4 all-gather.19
  409.8 193.3 all-gather.21
  606.1 192.9 all-gather.23
  802.1 192.9 all-gather.25
  1204.1 49.5 reduce-scatter.12
  1259.2 50.1 reduce-scatter.14
  1348.3 1877.2 all-reduce.8
  3227.9 1409.9 reduce-scatter.16
  4640.7 1410.6 reduce-scatter.10
where the time goes:
time: 6070 us; the launch traced here: 6060 us
  waiting for transfers between devices  5260 us (87%)
  matrix products  347 us (6%)
  local copies, waits for them, and re-layouts  199 us (3%)
  other arithmetic  148 us (2%)
  blocking collectives  85.6 us (1%)
    unnamed x18, waiting for transfers between devices  3040 us
    reduce_scatter x1, waiting for transfers between devices, local(): lax.psum_scatter(jnp.einsum('tf,td->fd', columns, upstream, preferred_ele...  1410 us
    all_gather x1, waiting for transfers between devices, local(): lax.all_gather(w_gate, ('ctx', 'fsdp'), axis=0, tiled=True)  191 us
    all_gather x1, waiting for transfers between devices, local(): lax.all_gather(w_down, ('ctx', 'fsdp'), axis=0, tiled=True)  178 us
    all_gather x1, waiting for transfers between devices, local(): lax.all_gather(w_up, ('ctx', 'fsdp'), axis=0, tiled=True)  178 us
  transfers between devices with their start and end apart: 14, of which 12 were waited for; matrix products, arithmetic and copies ran while one was open for 8% of the time, Pallas kernels for 0%

commit v1 on v0

v1 whole, which is shorter than its diff:
```python
import functools
import math

import jax
import jax.numpy as jnp
from jax import lax
from jax.experimental import pallas as pl
from jax.experimental.pallas import tpu as pltpu
from jax.sharding import Mesh
from jax.sharding import PartitionSpec as P

HEAD_DIM = 64
LANES = 128
TILE = 256


EPSILON = 1e-05
THETA = 130000.0
MASKED = -1e30
LOW = jnp.bfloat16
FULL = jnp.float32
RANKS = ("chip", "core")
EVERY = ("chip", "core", "fsdp")
VMEM_BYTES = 56 * 1024 * 1024


def norm_apply(values, gain_row):
    inverse = lax.rsqrt(jnp.mean(values * values, axis=-1, keepdims=True) + EPSILON)
    return (values * inverse * gain_row, inverse)


def norm_back(values, inverse, gain_row, upstream):
    scaled = upstream * gain_row
    inner_sum = jnp.mean(scaled * values, axis=-1, keepdims=True)
    inward = inverse * scaled - values * (inverse * inverse * inverse) * inner_sum
    gain_term = jnp.sum(upstream * values * inverse, axis=0)
    return (inward, gain_term)


def matmul(left, right, left_dim=1, right_dim=0):
    return lax.dot_general(
        left,
        right,
        (((left_dim,), (right_dim,)), ((), ())),
        preferred_element_type=FULL,
    )


def product_kernel(left_dim, right_dim, left, *refs):
    count = len(refs) // 2
    for right, out in zip(refs[:count], refs[count:]):
        out[...] = matmul(left[...], right[...], left_dim, right_dim).astype(out.dtype)


def product_rows(left, rights, left_dim, right_dim, tile, dtype=LOW):
    free = 1 - left_dim
    extent = left.shape[free]
    tile = min(tile, extent)
    shape = (tile, left.shape[1]) if free == 0 else (left.shape[0], tile)
    index = (lambda i: (i, 0)) if free == 0 else (lambda i: (0, i))
    widths = [right.shape[1 - right_dim] for right in rights]
    return pl.pallas_call(
        functools.partial(product_kernel, left_dim, right_dim),
        grid=(extent // tile,),
        in_specs=[pl.BlockSpec(shape, index)]
        + [pl.BlockSpec(right.shape, lambda i: (0, 0)) for right in rights],
        out_specs=[pl.BlockSpec((tile, width), lambda i: (i, 0)) for width in widths],
        out_shape=[jax.ShapeDtypeStruct((extent, width), dtype) for width in widths],
        compiler_params=pltpu.CompilerParams(vmem_limit_bytes=VMEM_BYTES),
    )(left, *rights)


def expand_kernel(
    near_in, far_in, near, far, gate_cols, up_cols, down_rows, rows, activation, gate_low, up_low
):
    half = near.shape[0]

    @pl.when(pl.program_id(0) == 0)
    def _():
        rows[:half, :] = near_in[...]
        rows[half:, :] = far_in[...]

    step = min(TILE, half)
    for first in range(0, 2 * half, step):
        here = slice(first, first + step)
        source = near if first < half else far
        gate = matmul(rows[here, :], gate_cols[...])
        up = matmul(rows[here, :], up_cols[...])
        act_grad = matmul(source[first % half : first % half + step, :], down_rows[...], 1, 1)
        sigmoid = 1.0 / (1.0 + jnp.exp(-gate))
        silu = gate * sigmoid
        activation[here, :] = (silu * up).astype(LOW)
        gate_low[here, :] = (act_grad * up * sigmoid * (1.0 + gate * (1.0 - sigmoid))).astype(LOW)
        up_low[here, :] = (act_grad * silu).astype(LOW)


def expand(near_in, far_in, near, far, gate_cols, up_cols, down_rows):
    half, width = near.shape
    total = 2 * half
    hidden = gate_cols.shape[1]
    tile = min(TILE, hidden)
    once = pl.BlockSpec((half, width), lambda i: (0, 0), pipeline_mode=pl.Buffered(1))
    column = pl.BlockSpec((width, tile), lambda i: (0, i))
    out = pl.BlockSpec((total, tile), lambda i: (0, i))
    return pl.pallas_call(
        expand_kernel,
        grid=(hidden // tile,),
        in_specs=[once] * 4 + [column, column, pl.BlockSpec((tile, width), lambda i: (i, 0))],
        out_specs=[pl.BlockSpec((total, width), lambda i: (0, 0))] + [out] * 3,
        out_shape=[jax.ShapeDtypeStruct((total, width), LOW)]
        + [jax.ShapeDtypeStruct((total, hidden), LOW)] * 3,
        compiler_params=pltpu.CompilerParams(vmem_limit_bytes=VMEM_BYTES),
    )(near_in, far_in, near, far, gate_cols, up_cols, down_rows)


def pair_kernel(order, left, right, gate_low, up_low, gate_out, up_out):
    del order
    gate_out[...] = matmul(left[...], gate_low[...], 0, 0).astype(LOW)
    up_out[...] = matmul(right[...], up_low[...], 0, 0).astype(LOW)


def pair_products(rows, gate_low, up_low, chip, chips, codes):
    count, width = rows.shape
    tile = width // chips
    steps = len(codes[0])
    order = chip ^ jnp.array(codes[0] + codes[1], dtype=jnp.int32)
    whole = pl.BlockSpec(gate_low.shape, lambda i, order: (0, 0))
    out = pl.BlockSpec((tile, gate_low.shape[1]), lambda i, order: (i, 0))
    return pl.pallas_call(
        pair_kernel,
        grid_spec=pltpu.PrefetchScalarGridSpec(
            num_scalar_prefetch=1,
            grid=(steps,),
            in_specs=[
                pl.BlockSpec((count, tile), lambda i, order: (0, order[i])),
                pl.BlockSpec((count, tile), lambda i, order: (0, order[steps + i])),
                whole,
                whole,
            ],
            out_specs=[out, out],
        ),
        out_shape=[jax.ShapeDtypeStruct((steps * tile, gate_low.shape[1]), LOW)] * 2,
        compiler_params=pltpu.CompilerParams(vmem_limit_bytes=VMEM_BYTES),
    )(order, rows, rows, gate_low, up_low)


def contract_kernel(left, right, left_cols, right_cols, out):
    total = matmul(left[...], left_cols[...], 1, 1) + matmul(right[...], right_cols[...], 1, 1)
    out[...] = total.astype(out.dtype)


def contract(left, right, left_cols, right_cols, part, dtype):
    count, hidden = left.shape
    width = left_cols.shape[0]
    tile = min(512, width)
    rows = pl.BlockSpec((count // 2, hidden), lambda i: (part, 0))
    cols = pl.BlockSpec((tile, hidden), lambda i: (i, 0))
    return pl.pallas_call(
        contract_kernel,
        grid=(width // tile,),
        in_specs=[rows, rows, cols, cols],
        out_specs=pl.BlockSpec((count // 2, tile), lambda i: (0, i)),
        out_shape=jax.ShapeDtypeStruct((count // 2, width), dtype),
        compiler_params=pltpu.CompilerParams(vmem_limit_bytes=VMEM_BYTES),
    )(left, right, left_cols, right_cols)


def swap_with(value, axis, code):
    count = lax.axis_size(axis)
    return lax.ppermute(value, axis, [(i, i ^ code) for i in range(count)])


def permute(value, axis, pairs):
    return lax.ppermute(value, axis, pairs)


def gather_line(value, axis, *earlier):
    count = lax.axis_size(axis)
    if count != 4:
        return [value] + [swap_with(value, axis, code) for code in range(1, count)]
    near = swap_with(value, axis, 1)
    far = after(swap_with(value, axis, 2), near, *earlier)
    middle = permute(after(value, far), axis, [(1, 2), (2, 1)])
    ends = permute(far, axis, [(2, 3), (1, 0)])
    place = lax.axis_index(axis)
    return [value, near, far, jnp.where((place == 1) | (place == 2), middle, ends)]


def scatter_line(pieces, axis):
    count = lax.axis_size(axis)
    if count != 4:
        early, late = [], [swap_with(pieces[code], axis, code) for code in range(1, count)]
    else:
        ends = permute(pieces[3], axis, [(3, 2), (0, 1)])
        middle = permute(pieces[3], axis, [(1, 2), (2, 1)])
        passed = (pieces[2].astype(FULL) + ends.astype(FULL)).astype(LOW)
        early = [middle]
        late = [swap_with(passed, axis, 2), swap_with(after(pieces[1], ends), axis, 1)]
    total = pieces[0].astype(FULL)
    for part in early + late:
        total = total + part.astype(FULL)
    return total, early, late


def gather_rows(rows, axis, *earlier):
    near = [swap_with(rows, axis, code) for code in range(1, lax.axis_size(axis))]
    near = [rows] + [after(part, *earlier) if earlier else part for part in near]
    far = [swap_with(part, "core", 1) for part in near]
    return near + far


def scatter_rows(near, far, axis):
    total = near + swap_with(far.astype(LOW), "core", 1).astype(FULL)
    return sum_rows(total.astype(LOW), axis)


def sum_rows(low, axis):
    count = lax.axis_size(axis)
    rows = low.shape[0] // count
    result = low[:rows].astype(FULL)
    for code in range(1, count):
        result = result + swap_with(low[code * rows : (code + 1) * rows], axis, code).astype(FULL)
    return result


def after(value, *earlier):
    return lax.optimization_barrier((value,) + earlier)[0]


def total_over(value, axis):
    code = 1
    while code < lax.axis_size(axis):
        value = value + swap_with(value, axis, code)
        code *= 2
    return value


def shuffle(kernel, outs, *arrays):
    whole = pl.BlockSpec(memory_space=pltpu.VMEM)
    return pl.pallas_call(
        kernel,
        in_specs=[whole] * len(arrays),
        out_specs=[whole] * len(outs),
        out_shape=outs,
        compiler_params=pltpu.CompilerParams(vmem_limit_bytes=32 * 1024 * 1024),
    )(*arrays)


def shuffle(kernel, outs, *arrays):
    whole = pl.BlockSpec(memory_space=pltpu.VMEM)
    return pl.pallas_call(
        kernel,
        in_specs=[whole] * len(arrays),
        out_specs=[whole] * len(outs),
        out_shape=outs,
        compiler_params=pltpu.CompilerParams(vmem_limit_bytes=32 * 1024 * 1024),
    )(*arrays)


def block_order(chips):
    return [2, 3, 1, 0] if chips == 4 else list(range(chips))


def gather_each(block, axis):
    copies = jnp.broadcast_to(block[None], (lax.axis_size(axis),) + block.shape)
    copies = lax.all_to_all(copies, axis, 0, 0, tiled=True)
    return copies.reshape(-1, block.shape[1])


def scatter_each(low, axis):
    count = lax.axis_size(axis)
    parts = lax.all_to_all(low.reshape(count, -1, low.shape[1]), axis, 0, 0, tiled=True)
    return jnp.sum(parts.astype(FULL), axis=0)


def gather_gains(*gains):
    packed = jnp.concatenate(gains)
    count = math.prod(lax.axis_size(axis) for axis in EVERY)
    spread = jnp.broadcast_to(packed[None], (count, packed.shape[0]))
    return lax.all_to_all(spread, EVERY, 0, 0, tiled=True)


def pack_heads_kernel(query, key, value, out):
    ranks, _, width = out.shape
    for rank in range(ranks):
        for group in range(width // (3 * LANES)):
            source = rank * (width // 3) + group * LANES
            for kind, weight in enumerate((query, key, value)):
                start = (group * 3 + kind) * LANES
                out[rank, :, start : start + LANES] = weight[:, source : source + LANES]


def unpack_heads_kernel(packed, *outs):
    ranks, _, width = packed.shape
    for rank in range(ranks):
        for group in range(width // (3 * LANES)):
            target = rank * (width // 3) + group * LANES
            for kind, out in enumerate(outs):
                start = (group * 3 + kind) * LANES
                out[:, target : target + LANES] = packed[rank, :, start : start + LANES].astype(FULL)


def pack_columns_kernel(chips, gate, up, gate_out, up_out):
    steps, _, width = gate_out.shape
    block = width // chips
    for weight, out in ((gate, gate_out), (up, up_out)):
        for step in range(steps):
            for chip in range(chips):
                start = (chip * steps + step) * block
                here = slice(chip * block, (chip + 1) * block)
                out[step, :, here] = weight[:, start : start + block]


def unpack_columns_kernel(chips, packed, out):
    steps, _, width = packed.shape
    block = width // chips
    for step in range(steps):
        for chip in range(chips):
            start = (chip * steps + step) * block
            here = slice(chip * block, (chip + 1) * block)
            out[:, start : start + block] = packed[step, :, here].astype(FULL)


def join_kernel(*refs):
    out = refs[-1]
    first = 0
    for part in refs[:-1]:
        last = first + part.shape[0]
        out[first:last, :] = part[...]
        first = last


def join_rows(parts):
    rows = sum(part.shape[0] for part in parts)
    return shuffle(join_kernel, [jax.ShapeDtypeStruct((rows, parts[0].shape[1]), LOW)], *parts)[0]


def spread_kernel(place, *refs):
    out = refs[-1]
    for code, part in enumerate(refs[:-1]):
        for rank in range(out.shape[0]):
            out[rank, place[0] ^ code] = part[rank]


def spread_shards(shard, parts):
    whole = pl.BlockSpec(memory_space=pltpu.VMEM)
    ranks, rows, width = parts[0].shape
    return pl.pallas_call(
        spread_kernel,
        in_specs=[pl.BlockSpec(memory_space=pltpu.SMEM)] + [whole] * len(parts),
        out_specs=whole,
        out_shape=jax.ShapeDtypeStruct((ranks, len(parts), rows, width), LOW),
        compiler_params=pltpu.CompilerParams(vmem_limit_bytes=32 * 1024 * 1024),
    )(jnp.reshape(shard, (1,)).astype(jnp.int32), *parts)


def place_kernel(place, *refs):
    out = refs[-1]
    for code, part in enumerate(refs[:-1]):
        rows = part.shape[0]
        first = pl.multiple_of((place[0] ^ code) * rows, rows)
        out[pl.ds(first, rows), :] = part[...]


def place_blocks(index, parts):
    whole = pl.BlockSpec(memory_space=pltpu.VMEM)
    rows, width = parts[0].shape
    return pl.pallas_call(
        place_kernel,
        in_specs=[pl.BlockSpec(memory_space=pltpu.SMEM)] + [whole] * len(parts),
        out_specs=whole,
        out_shape=jax.ShapeDtypeStruct((len(parts) * rows, width), LOW),
        compiler_params=pltpu.CompilerParams(vmem_limit_bytes=32 * 1024 * 1024),
    )(jnp.reshape(index, (1,)).astype(jnp.int32), *parts)


def place_block(buffer, block, index, dim):
    start = [0] * buffer.ndim
    start[dim] = index
    return lax.dynamic_update_slice(buffer, jnp.expand_dims(block, dim), start)


def pick_block(buffer, index, dim):
    return lax.dynamic_index_in_dim(buffer, index, dim, keepdims=False)


def natural_tables(lengths, seq_rows):
    doc_count = lengths.shape[0]
    place = jnp.arange(seq_rows, dtype=jnp.int32)
    doc_ends = jnp.cumsum(lengths)
    passed = (place[:, None] >= doc_ends[None, : doc_count - 1]).astype(jnp.int32)
    start_place = jnp.sum(passed * lengths[None, : doc_count - 1], axis=1)
    half_dim = HEAD_DIM // 2
    frequency = jnp.power(THETA, -2.0 * jnp.arange(half_dim, dtype=FULL) / HEAD_DIM)
    angles = (place - start_place).astype(FULL)[:, None] * frequency[None, :]
    cosine, sine = jnp.cos(angles), jnp.sin(angles)
    repeats = LANES // HEAD_DIM
    cosine_table = jnp.concatenate([cosine, cosine] * repeats, axis=1)
    sine_table = jnp.concatenate([-sine, sine] * repeats, axis=1)
    return start_place.reshape(1, seq_rows), cosine_table, sine_table


def half_swap(values):
    lane = lax.broadcasted_iota(jnp.int32, values.shape, 1)
    return jnp.where(
        lane % HEAD_DIM < HEAD_DIM // 2,
        pltpu.roll(values, LANES - HEAD_DIM // 2, 1),
        pltpu.roll(values, HEAD_DIM // 2, 1),
    )


def head_lanes(values, head):
    lane = lax.broadcasted_iota(jnp.int32, values.shape, 1)
    return jnp.where(lane // HEAD_DIM == head, values, jnp.zeros_like(values))


def allowed_keys(start_row, tile, chunk):
    keys = lax.broadcasted_iota(jnp.int32, (TILE, TILE), 0) + chunk * TILE
    allowed = keys >= start_row
    if chunk == tile:
        queries = lax.broadcasted_iota(jnp.int32, (TILE, TILE), 1) + tile * TILE
        allowed = allowed & (keys <= queries)
    return allowed


def forward_kernel(
    offsets, qkv, cosine, sine, starts, mixed, query_out, key_out, value_out, lse_out, value_flip, held
):
    seq_rows = query_out.shape[0]
    block = HEAD_DIM
    for n in range(seq_rows // block):
        rows = pl.ds(pl.multiple_of(offsets[n], block), block)
        here = slice(n * block, (n + 1) * block)
        cos, sin = cosine[here, :], sine[here, :]
        query = qkv[rows, 0:LANES]
        turned = (query * cos + half_swap(query) * sin).astype(LOW)
        query_out[here, :] = turned * LOW(1.0 / math.sqrt(HEAD_DIM))
        key = qkv[rows, LANES : 2 * LANES]
        key_out[here, :] = (key * cos + half_swap(key) * sin).astype(LOW)
        value_out[here, :] = qkv[rows, 2 * LANES : 3 * LANES].astype(LOW)
    value_flip[...] = value_out[...].T
    for tile in range(seq_rows // TILE):
        here = slice(tile * TILE, (tile + 1) * TILE)
        start_row = starts[:, here]
        flipped = []
        for head in range(LANES // HEAD_DIM):
            query = head_lanes(query_out[here, :], head)
            top = jnp.full((1, TILE), MASKED, FULL)
            for chunk in range(tile + 1):
                keys = slice(chunk * TILE, (chunk + 1) * TILE)
                scores = matmul(key_out[keys, :], query, 1, 1)
                scores = jnp.where(allowed_keys(start_row, tile, chunk), scores, MASKED)
                held[keys, :] = scores
                top = jnp.maximum(top, jnp.max(scores, axis=0, keepdims=True))
            total = jnp.zeros((1, TILE), FULL)
            for chunk in range(tile + 1):
                keys = slice(chunk * TILE, (chunk + 1) * TILE)
                raised = jnp.exp(held[keys, :] - top)
                held[keys, :] = raised
                total = total + jnp.sum(raised, axis=0, keepdims=True)
            inverse = 1.0 / total
            mixed_flip = jnp.zeros((HEAD_DIM, TILE), FULL)
            for chunk in range(tile + 1):
                keys = slice(chunk * TILE, (chunk + 1) * TILE)
                prob_low = (held[keys, :] * inverse).astype(LOW)
                mixed_flip = mixed_flip + matmul(
                    value_flip[head * HEAD_DIM : (head + 1) * HEAD_DIM, keys], prob_low
                )
            flipped.append(mixed_flip)
            lse_out[0, head : head + 1, here] = top + jnp.log(total)
        together = jnp.concatenate(flipped, axis=0).T.astype(LOW)
        for part in range(TILE // block):
            n = tile * (TILE // block) + part
            rows = pl.ds(pl.multiple_of(offsets[n], block), block)
            mixed[rows, :] = together[part * block : (part + 1) * block, :]


def backward_kernel(
    offsets, upstream, query_in, key_in, value_in, lse, cosine, sine, starts, out,
    ups, key_flip, prob_held, grad_held, query_sum, key_sum, value_sum,
):
    seq_rows = query_in.shape[0]
    block = HEAD_DIM
    for n in range(seq_rows // block):
        rows = pl.ds(pl.multiple_of(offsets[n], block), block)
        ups[n * block : (n + 1) * block, :] = upstream[rows, :]
    key_flip[...] = key_in[...].T
    key_sum[...] = jnp.zeros_like(key_sum)
    value_sum[...] = jnp.zeros_like(value_sum)
    for tile in range(seq_rows // TILE):
        here = slice(tile * TILE, (tile + 1) * TILE)
        start_row = starts[:, here]
        flipped = []
        for head in range(LANES // HEAD_DIM):
            query = head_lanes(query_in[here, :], head)
            up = head_lanes(ups[here, :], head)
            lse_row = lse[0, head : head + 1, here]
            inner = jnp.zeros((1, TILE), FULL)
            for chunk in range(tile + 1):
                keys = slice(chunk * TILE, (chunk + 1) * TILE)
                scores = matmul(key_in[keys, :], query, 1, 1)
                probs = jnp.where(
                    allowed_keys(start_row, tile, chunk), jnp.exp(scores - lse_row), 0.0
                )
                prob_grad = matmul(value_in[keys, :], up, 1, 1)
                inner = inner + jnp.sum(probs * prob_grad, axis=0, keepdims=True)
                prob_held[keys, :] = probs
                grad_held[keys, :] = prob_grad
                value_sum[keys, :] += matmul(probs.astype(LOW), up)
            query_flip = jnp.zeros((HEAD_DIM, TILE), FULL)
            for chunk in range(tile + 1):
                keys = slice(chunk * TILE, (chunk + 1) * TILE)
                score_low = (prob_held[keys, :] * (grad_held[keys, :] - inner)).astype(LOW)
                key_sum[keys, :] += matmul(score_low, query)
                query_flip = query_flip + matmul(
                    key_flip[head * HEAD_DIM : (head + 1) * HEAD_DIM, keys], score_low
                )
            flipped.append(query_flip)
        query_sum[here, :] = jnp.concatenate(flipped, axis=0).T * (1.0 / math.sqrt(HEAD_DIM))
    for n in range(seq_rows // block):
        rows = pl.ds(pl.multiple_of(offsets[n], block), block)
        here = slice(n * block, (n + 1) * block)
        cos, sin = cosine[here, :], sine[here, :]
        query, key = query_sum[here, :], key_sum[here, :]
        out[rows, 0:LANES] = (query * cos - half_swap(query) * sin).astype(LOW)
        out[rows, LANES : 2 * LANES] = (key * cos - half_swap(key) * sin).astype(LOW)
        out[rows, 2 * LANES : 3 * LANES] = value_sum[here, :].astype(LOW)


def attention_forward(offsets, qkv, cosine, sine, starts):
    seq_rows, width = qkv.shape
    groups = width // (3 * LANES)
    whole = lambda g, offs: (0, 0)
    column = lambda g, offs: (0, g)
    low_out = jax.ShapeDtypeStruct((seq_rows, groups * LANES), LOW)
    return pl.pallas_call(
        forward_kernel,
        grid_spec=pltpu.PrefetchScalarGridSpec(
            num_scalar_prefetch=1,
            grid=(groups,),
            in_specs=[
                pl.BlockSpec((seq_rows, 3 * LANES), column),
                pl.BlockSpec((seq_rows, LANES), whole),
                pl.BlockSpec((seq_rows, LANES), whole),
                pl.BlockSpec((1, seq_rows), whole),
            ],
            out_specs=[pl.BlockSpec((seq_rows, LANES), column)] * 4
            + [pl.BlockSpec((1, 8, seq_rows), lambda g, offs: (g, 0, 0))],
            scratch_shapes=[
                pltpu.VMEM((LANES, seq_rows), LOW),
                pltpu.VMEM((seq_rows, TILE), FULL),
            ],
        ),
        out_shape=[low_out] * 4 + [jax.ShapeDtypeStruct((groups, 8, seq_rows), FULL)],
        compiler_params=pltpu.CompilerParams(vmem_limit_bytes=40 * 1024 * 1024),
    )(offsets, qkv, cosine, sine, starts)


def attention_backward(offsets, upstream, query, key, value, lse, cosine, sine, starts):
    seq_rows, width = query.shape
    groups = width // LANES
    whole = lambda g, offs: (0, 0)
    column = lambda g, offs: (0, g)
    return pl.pallas_call(
        backward_kernel,
        grid_spec=pltpu.PrefetchScalarGridSpec(
            num_scalar_prefetch=1,
            grid=(groups,),
            in_specs=[pl.BlockSpec((seq_rows, LANES), column)] * 4
            + [pl.BlockSpec((1, 8, seq_rows), lambda g, offs: (g, 0, 0))]
            + [pl.BlockSpec((seq_rows, LANES), whole)] * 2
            + [pl.BlockSpec((1, seq_rows), whole)],
            out_specs=pl.BlockSpec((seq_rows, 3 * LANES), column),
            scratch_shapes=[
                pltpu.VMEM((seq_rows, LANES), LOW),
                pltpu.VMEM((LANES, seq_rows), LOW),
                pltpu.VMEM((seq_rows, TILE), FULL),
                pltpu.VMEM((seq_rows, TILE), FULL),
                pltpu.VMEM((seq_rows, LANES), FULL),
                pltpu.VMEM((seq_rows, LANES), FULL),
                pltpu.VMEM((seq_rows, LANES), FULL),
            ],
        ),
        out_shape=jax.ShapeDtypeStruct((seq_rows, groups * 3 * LANES), LOW),
        compiler_params=pltpu.CompilerParams(vmem_limit_bytes=40 * 1024 * 1024),
    )(offsets, upstream, query, key, value, lse, cosine, sine, starts)


def local(
    tokens,
    doc_lengths,
    norm1_gain,
    w_query,
    w_key,
    w_value,
    w_out,
    norm2_gain,
    w_gate,
    w_up,
    w_down,
    cotangent,
):
    chips, cores, shards = (lax.axis_size(name) for name in EVERY)
    chip, core, shard = (lax.axis_index(name) for name in EVERY)
    ranks = chips * cores
    local_rows, model_width = tokens.shape[1:]
    block_len = local_rows // 2
    seq_rows = local_rows * ranks
    weight_rows = w_query.shape[0]
    ff_width = w_gate.shape[1]
    ff_block = ff_width // (ranks * shards)
    rank_width = model_width // ranks
    groups = rank_width // LANES

    steps = cores * shards
    column_width = chips * ff_block
    low_shape = lambda *shape: jax.ShapeDtypeStruct(shape, LOW)
    full_shape = lambda *shape: jax.ShapeDtypeStruct(shape, FULL)

    token_low = tokens[0]
    projections = shuffle(
        pack_heads_kernel, [low_shape(ranks, weight_rows, 3 * rank_width)], w_query, w_key, w_value
    )[0]
    columns = shuffle(
        functools.partial(pack_columns_kernel, chips),
        [low_shape(steps, weight_rows, column_width)] * 2,
        w_gate,
        w_up,
    )

    def exchange(part):
        part = lax.all_to_all(part, ("core", "fsdp"), 0, 0, tiled=True)
        return part.reshape(steps * weight_rows, column_width)

    w_out_rows = lax.all_gather(w_out, "fsdp", axis=0, tiled=True)
    spread = gather_gains(norm1_gain, norm2_gain)
    gains = [row.reshape(-1) for row in jnp.split(spread, 2, axis=1)]
    projections = lax.all_to_all(after(projections, spread), RANKS, 0, 0, tiled=True)
    token_parts = gather_rows(after(token_low, projections), "chip")
    w_down_rows = lax.all_gather(after(w_down, projections), "chip", axis=0, tiled=True)
    gate_cols = exchange(after(columns[0], projections))
    parts = gather_line(projections, "fsdp", gate_cols)
    gate_cols = after(gate_cols, *parts[1:3])
    up_cols = exchange(after(columns[1], gate_cols))
    w_up_cols = lax.all_gather(up_cols, "chip", axis=0, tiled=True)
    near_upstream = gather_each(after(cotangent[0], up_cols), "fsdp")
    gate_blocks = [gate_cols] + [swap_with(gate_cols, "chip", code) for code in range(1, chips)]
    w_gate_cols = place_blocks(chip, gate_blocks)
    parts = [after(part, up_cols, *gate_blocks[1:]) for part in parts]

    w_qkv = spread_shards(shard, parts)
    w_qkv = w_qkv.reshape(model_width, 3 * rank_width)

    starts, cosine, sine = natural_tables(doc_lengths[0], seq_rows)
    order = jnp.arange(2 * ranks, dtype=jnp.int32)
    owner = jnp.where(order < ranks, order, 2 * ranks - 1 - order)
    slot = ((owner // cores) ^ chip) + chips * ((owner % cores) ^ core)
    offsets = slot * local_rows + jnp.where(order < ranks, 0, block_len)

    seq_tokens = join_rows(token_parts)
    normed1, seq_inverse = norm_apply(seq_tokens.astype(FULL), gains[0])
    attn_in = after(normed1.astype(LOW), w_down_rows)
    qkv = matmul(attn_in, w_qkv)
    mixed, query_rows, key_rows, value_rows, lse = attention_forward(
        offsets, qkv, cosine, sine, starts
    )
    mixed = after(mixed, gate_cols)
    half = seq_rows // 2
    far_part = matmul(mixed[half:], w_out_rows)
    near_part = matmul(mixed[:half], w_out_rows)
    token_rows = token_low.astype(FULL)
    hidden1 = token_rows + scatter_rows(near_part, far_part, "chip")
    normed2, inverse2 = norm_apply(hidden1, gains[1])

    far_upstream = swap_with(after(near_upstream, hidden1), "core", 1)
    near_in = gather_each(normed2.astype(LOW), "fsdp")
    far_in = swap_with(near_in, "core", 1)
    mlp_in, activation, gate_low, up_low = expand(
        near_in, far_in, near_upstream, far_upstream, w_gate_cols, w_up_cols, w_down_rows
    )
    half_mlp = mlp_in.shape[0] // 2
    upstream = jnp.concatenate([near_upstream, far_upstream], axis=0)
    back_far = contract(gate_low, up_low, w_gate_cols, w_up_cols, 1, LOW)
    back_near = contract(gate_low, up_low, w_gate_cols, w_up_cols, 0, FULL)
    back_far = swap_with(back_far, "core", 1)
    back_low = (back_near + back_far.astype(FULL)).astype(LOW)
    gate_low, up_low, activation = (
        after(low, back_low) for low in (gate_low, up_low, activation)
    )
    if chips == 4:
        gate31, up23 = pair_products(mlp_in, gate_low, up_low, chip, chips, ((3, 1), (2, 3)))
        gate20, up10 = pair_products(mlp_in, gate_low, up_low, chip, chips, ((2, 0), (1, 0)))
        products = [gate31, up23, gate20, up10]
        gate_in, up_in = swap_with(gate31, "chip", 1), swap_with(up23, "chip", 2)
        arrived = [gate_in, up_in]
    else:
        products = product_rows(mlp_in, [gate_low, up_low], 0, 0, 512)
        arrived = []
    activation = after(activation, *products[:2])
    raw_down = product_rows(activation, [upstream], 0, 0, 256)[0]
    down_far = product_rows(activation[half_mlp:], [w_down_rows], 1, 0, 256)[0]
    down_near = product_rows(activation[:half_mlp], [w_down_rows], 1, 0, 256, FULL)[0]
    down_near = down_near + swap_with(down_far, "core", 1).astype(FULL)
    down_near = down_near.astype(LOW)
    mlp_in_grad = scatter_each(back_low, "fsdp")
    mlp_in_grad = after(mlp_in_grad, raw_down, down_near, *products, *arrived)
    hidden_back, gain2_term = norm_back(hidden1, inverse2, gains[1], mlp_in_grad)
    hidden1_grad = cotangent[0].astype(FULL) + hidden_back

    def exchange_back(part):
        part = part.reshape(steps, weight_rows, column_width)
        return lax.all_to_all(part, ("core", "fsdp"), 0, 0, tiled=True)

    if chips == 4:
        gate_in, up_in = (after(part, hidden1_grad).astype(FULL) for part in arrived)
        rows = gate20.shape[0] // 2
        gate2 = (gate20[:rows].astype(FULL) + gate_in[:rows]).astype(LOW)
        gate0 = gate20[rows:].astype(FULL) + gate_in[rows:]
        up1 = (up10[:rows].astype(FULL) + up_in[rows:]).astype(LOW)
        up0 = up10[rows:].astype(FULL) + up_in[:rows]
        gate_sum = (gate0 + swap_with(gate2, "chip", 2).astype(FULL)).astype(LOW)
        up_sum = (up0 + swap_with(up1, "chip", 1).astype(FULL)).astype(LOW)
    else:
        gate_sum, up_sum = (
            lax.psum_scatter(part, "chip", scatter_dimension=0, tiled=True) for part in products
        )
    gate_packed = exchange_back(gate_sum)
    up_packed = exchange_back(after(up_sum, gate_packed))
    down_parts = lax.psum_scatter(
        after(down_near, hidden1_grad), "fsdp", scatter_dimension=0, tiled=True
    )
    layer_out = hidden1 + down_parts.astype(FULL)
    hidden_low = gather_rows(hidden1_grad.astype(LOW), "chip")
    hidden_low = join_rows(hidden_low)
    down_grad = lax.psum_scatter(
        after(raw_down, down_parts), "chip", scatter_dimension=0, tiled=True
    ).astype(FULL)

    mixed_low = matmul(hidden_low, w_out_rows, 1, 1).astype(LOW)
    mixed_low = after(mixed_low, gate_sum, up_sum)
    out_grad = lax.psum_scatter(
        matmul(mixed, hidden_low, 0, 0).astype(LOW), "fsdp", scatter_dimension=0, tiled=True
    ).astype(FULL)
    qkv_low = attention_backward(
        offsets, mixed_low, query_rows, key_rows, value_rows, lse, cosine, sine, starts
    )
    qkv_low = after(qkv_low, gate_packed)
    raw_grad = matmul(attn_in, qkv_low, 0, 0).astype(LOW)
    qkv_grad = raw_grad.reshape(ranks, shards, weight_rows, 3 * rank_width)
    pieces = [pick_block(qkv_grad, shard ^ code, 1) for code in range(shards)]
    own_grad, early_grads, other_grads = scatter_line(pieces, "fsdp")
    gate_grad, up_grad = (
        shuffle(
            functools.partial(unpack_columns_kernel, chips),
            [full_shape(weight_rows, ff_width)],
            part,
        )[0]
        for part in (gate_packed, up_packed)
    )
    qkv_low = after(qkv_low, raw_grad)
    in_far = matmul(qkv_low[half:], w_qkv, 1, 1)
    in_near = matmul(after(qkv_low[:half], up_packed, *early_grads), w_qkv, 1, 1)
    in_grad = scatter_rows(in_near, in_far, "chip")
    token_back, gain1_term = norm_back(
        token_rows, seq_inverse[:local_rows], gains[0], in_grad
    )
    gain_grads = jnp.stack([gain1_term, gain2_term])
    for axis in RANKS:
        gain_grads = total_over(gain_grads, axis)
    gain_grads = total_over(after(gain_grads, *other_grads), "fsdp")
    gain_grads = lax.dynamic_slice_in_dim(
        gain_grads, ((chip * cores + core) * shards + shard) * weight_rows, weight_rows, 1
    )
    qkv_grad = lax.all_to_all(after(own_grad.astype(LOW), gain_grads), RANKS, 0, 0, tiled=True)
    qkv_grads = shuffle(
        unpack_heads_kernel, [full_shape(weight_rows, model_width)] * 3, qkv_grad
    )

    token_grad = hidden1_grad + token_back
    return (
        layer_out.astype(LOW)[None],
        token_grad[None],
        gain_grads[0],
        *qkv_grads,
        out_grad,
        gain_grads[1],
        gate_grad,
        up_grad,
        down_grad,
    )


def solution(mesh):
    ctx_count, shard_count = mesh.shape["ctx"], mesh.shape["fsdp"]
    grid = Mesh(mesh.devices.reshape(ctx_count // 2, 2, shard_count), EVERY)
    row = P("fsdp", RANKS, None)
    gain = P(EVERY)
    weight = P(EVERY, None)
    return jax.shard_map(
        local,
        mesh=grid,
        in_specs=(row, P("fsdp", None), gain) + (weight,) * 4 + (gain,) + (weight,) * 3 + (row,),
        out_specs=(row, row, gain) + (weight,) * 4 + (gain,) + (weight,) * 3,
        check_vma=False,
    )
```

time: 6070 us -> 703 us (0.12)
  waiting for transfers between devices: 5260 us -> 309 us
  matrix products: 347 us -> 31.3 us
  local copies, waits for them, and re-layouts: 199 us -> 41.8 us
  starting transfers between devices: 1.02 us -> 113 us
  Pallas kernels: 0 us -> 108 us
  other arithmetic: 148 us -> 63 us
  blocking collectives: 85.6 us -> 15 us
    unnamed x18 -> x6, waiting for transfers between devices: 3040 us -> 0.78 us
    reduce_scatter x1 -> x3, waiting for transfers between devices: 1410 us -> 0.01 us  [the longest x1 0.01 us: local(): lax.psum_scatter(after(down_near, hidden1_grad), 'fsdp', scatter_dimensio...]
    all_gather x9 -> x3, waiting for transfers between devices: 810 us -> 0.01 us  [the longest x1 0.01 us: local(): lax.all_gather(after(w_down, projections), 'chip', axis=0, tiled=True)]
    dot_general x77 -> x8, matrix products: 347 us -> 31.3 us  [matmul(): lax.dot_general(left, right, (((left_dim,), (right_dim,)), ((), ())), pre...]
    ppermute x0 -> x46, waiting for transfers between devices: none -> 205 us  [the longest x42 158 us: swap_with(): return lax.ppermute(value, axis, [(i, i ^ code) for i in range(count)])]
    concatenate x4 -> x3, other arithmetic: 132 us -> 8.99 us  [the longest x1 4.77 us: local(): upstream = jnp.concatenate([near_upstream, far_upstream], axis=0)]
    pallas_call x0 -> x19, Pallas kernels: none -> 108 us  [the longest x3 20.7 us: product_rows(): pl.pallas_call(functools.partial(product_kernel, left_dim, right_dim), gr...]
    all_to_all x0 -> x9, waiting for transfers between devices: none -> 103 us  [the longest x2 51.9 us: gather_each(): copies = lax.all_to_all(copies, axis, 0, 0, tiled=True)]
  transfers between devices with their start and end apart: 14 -> 61, of which waited for: 12 -> 28; matrix products, arithmetic and copies ran while one was open for 8% -> 13% of each run, Pallas kernels for 0% -> 11%
where the time goes in v1:
time: 703 us; the launch traced here: 696 us
  waiting for transfers between devices  309 us (44%)
  starting transfers between devices  113 us (16%)
  Pallas kernels  108 us (15%)
  other arithmetic  63 us (9%)
  local copies, waits for them, and re-layouts  41.8 us (6%)
  matrix products  31.3 us (4%)
  blocking collectives  15 us (2%)
  between operations  15 us (2%)
    ppermute x42, waiting for transfers between devices, swap_with(): return lax.ppermute(value, axis, [(i, i ^ code) for i in range(count)])  158 us
    all_to_all x2, waiting for transfers between devices, gather_each(): copies = lax.all_to_all(copies, axis, 0, 0, tiled=True)  51.9 us
    ppermute x4, waiting for transfers between devices, permute(): return lax.ppermute(value, axis, pairs)  46.5 us
    ppermute x42, starting transfers between devices, swap_with(): return lax.ppermute(value, axis, [(i, i ^ code) for i in range(count)])  42.6 us
    all_to_all x2, waiting for transfers between devices, exchange_back(): return lax.all_to_all(part, ('core', 'fsdp'), 0, 0, tiled=True)  38.1 us
    dot_general x8, matrix products, matmul(): lax.dot_general(left, right, (((left_dim,), (right_dim,)), ((), ())), pre...  31.3 us
    unnamed x100, local copies, waits for them, and re-layouts  29.5 us
    ppermute x4, starting transfers between devices, permute(): return lax.ppermute(value, axis, pairs)  25 us
  transfers between devices with their start and end apart: 61, of which 28 were waited for; matrix products, arithmetic and copies ran while one was open for 13% of the time, Pallas kernels for 11%

profile of v1, /device:TPU:0, one launch (start us, length us, event | category | flops | bytes accessed | tf_op | source)
XLA Modules:
  0.0 696.5 jit_solution(5462366549196615441)
XLA Ops:
  8.5 7.3 %all-to-all-start = ((f32[32,1,128]{2,1,0:T(1,128)}), f32[32,1,128]{2,1,0:T(1,128)S(1)}, u32[]{:S(2)}, u32[]{:S(2)}) async-start(f32[32,1,128]{2,1,0:T(1,128)} %broadcast_in_dim.17), calls=%async_computation | async-start | bytes 32768 | tf_op jit(solution)/shard_map/all_to_all | solution.py:280
  19.0 4.0 all-to-all-done
  22.9 15.0 %all_to_all.54.refs_0_ = bf16[8,64,768]{2,1,0:T(8,128)(2,1)S(1)} all-to-all(bf16[8,64,768]{2,1,0:T(8,128)(2,1)S(1)} %shard_map.221), channel_id=1, replica_groups=mesh['chip'=4,'core'=2,'fsdp'=4] {'chip','core'}, dimensions={0} | all-to-all | bytes 1572864 | tf_op jit(solution)/shard_map/all_to_all | solution.py:638
  41.6 3.6 all-to-all-start.2
  49.2 2.4 collective-permute-start.2
  54.1 13.9 %collective-permute-done.refs_1_ = bf16[128,2048]{1,0:T(8,128)(2,1)} collective-permute-done((bf16[128,2048]{1,0:T(8,128)(2,1)S(1)}, bf16[128,2048]{1,0:T(8,128)(2,1)}, u32[]{:S(2)}, u32[]{:S(2)}) %collective-permute-start) | collective-permute-done | bytes 524320 | tf_op jit(solution)/shard_map/ppermute | solution.py:170
  68.5 18.8 %collective-permute-done.2.refs_3_ = bf16[128,2048]{1,0:T(8,128)(2,1)} collective-permute-done((bf16[128,2048]{1,0:T(8,128)(2,1)S(1)}, bf16[128,2048]{1,0:T(8,128)(2,1)}, u32[]{:S(2)}, u32[]{:S(2)}) %collective-permute-start.2) | collective-permute-done | bytes 524320 | tf_op jit(solution)/shard_map/ppermute | solution.py:170
  87.3 7.0 %collective-permute-done.7.refs_1_ = bf16[8,64,768]{2,1,0:T(8,128)(2,1)S(1)} collective-permute-done((bf16[8,64,768]{2,1,0:T(8,128)(2,1)S(1)}, bf16[8,64,768]{2,1,0:T(8,128)(2,1)S(1)}, u32[]{:S(2)}, u32[]{:S(2)}) %collective-permute-start.7) | collective-permute-done | bytes 786464 | tf_op jit(solution)/shard_map/ppermute | solution.py:170
  94.3 3.2 fusion.27
  97.5 3.5 pad_maximum_fusion.1
  101.0 4.6 collective-permute-done.8.refs_2_
  105.6 4.3 all-to-all-start.3
  119.4 3.1 fusion.2
  122.5 41.0 %collective-permute-done.13 = bf16[8,64,768]{2,1,0:T(8,128)(2,1)S(1)} collective-permute-done((bf16[8,64,768]{2,1,0:T(8,128)(2,1)}, bf16[8,64,768]{2,1,0:T(8,128)(2,1)S(1)}, u32[]{:S(2)}, u32[]{:S(2)}) %collective-permute-start.13) | collective-permute-done | bytes 786464 | tf_op jit(solution)/shard_map/ppermute | solution.py:174
  171.9 6.1 fusion.40.qkv
  178.0 9.0 %shard_map.225 = (bf16[1024,256]{1,0:T(8,128)(2,1)S(1)}, bf16[1024,256]{1,0:T(8,128)(2,1)S(1)}, bf16[1024,256]{1,0:T(8,128)(2,1)S(1)}, bf16[1024,256]{1,0:T(8,128)(2,1)S(1)}, f32[2,8,1024]{2,1,0:T(8,128)S(1)}) custom-call(s32[16]{0:T(128)S(1)} %fusion.29.offsets, f32[1024,768]{1,0:T(8,128)S(1)} %fusion.40.qkv, f32[1024,128]{1,0:T(8,128)S(1)} %get-tuple-element.142.cosine, ...), custom_call_target="tpu_custom_call" | custom-call | tf_op jit(solution)/shard_map/pallas_call | solution.py:536
  189.4 3.4 convolution_convert_fusion.1
  194.4 8.4 %all-to-all-start.5 = ((bf16[4,128,2048]{2,1,0:T(8,128)(2,1)}), bf16[4,128,2048]{2,1,0:T(8,128)(2,1)}, u32[]{:S(2)}, u32[]{:S(2)}) async-start(bf16[4,128,2048]{2,1,0:T(8,128)(2,1)} %broadcast_in_dim.19), calls=%async_computation.5 | async-start | bytes 4194304 | tf_op jit(solution)/shard_map/all_to_all | solution.py:266
  202.8 2.7 add_convert_fusion.3
  211.6 12.6 %collective-permute-done.15 = bf16[128,2048]{1,0:T(8,128)(2,1)} collective-permute-done((bf16[128,2048]{1,0:T(8,128)(2,1)}, bf16[128,2048]{1,0:T(8,128)(2,1)}, u32[]{:S(2)}, u32[]{:S(2)}) %collective-permute-start.15) | collective-permute-done | bytes 524320 | tf_op jit(solution)/shard_map/ppermute | solution.py:170
  225.8 19.2 %collective-permute-done.17 = bf16[128,2048]{1,0:T(8,128)(2,1)} collective-permute-done((bf16[128,2048]{1,0:T(8,128)(2,1)}, bf16[128,2048]{1,0:T(8,128)(2,1)}, u32[]{:S(2)}, u32[]{:S(2)}) %collective-permute-start.17) | collective-permute-done | bytes 524320 | tf_op jit(solution)/shard_map/ppermute | solution.py:170
  248.9 3.5 all-to-all-done.5
  252.4 2.6 broadcast_in_dim.18
  255.0 4.6 all-to-all-start.4
  259.7 48.5 %all-to-all-done.4 = bf16[4,128,2048]{2,1,0:T(8,128)(2,1)} async-done(((bf16[4,128,2048]{2,1,0:T(8,128)(2,1)}), bf16[4,128,2048]{2,1,0:T(8,128)(2,1)}, u32[]{:S(2)}, u32[]{:S(2)}) %all-to-all-start.4) | async-done | bytes 2097184 | tf_op jit(solution)/shard_map/all_to_all | solution.py:266
  314.2 20.4 %shard_map.227 = (bf16[1024,2048]{1,0:T(8,128)(2,1)}, bf16[1024,1024]{1,0:T(8,128)(2,1)}, bf16[1024,1024]{1,0:T(8,128)(2,1)}, bf16[1024,1024]{1,0:T(8,128)(2,1)}) custom-call(bf16[512,2048]{1,0:T(8,128)(2,1)} %bitcast.10.near_in, bf16[512,2048]{1,0:T(8,128)(2,1)} %collective-permute-done.18.far_in, bf16[512,2048]{1,0:T(8,128)(2,1)} %bitcast.12.near, ...), custom_call_target="tpu_custom_call" | custom-call | tf_op jit(solution)/shard_map/pallas_call | solution.py:105
  334.5 8.7 %shard_map.229 = bf16[512,2048]{1,0:T(8,128)(2,1)} custom-call(bf16[1024,1024]{1,0:T(8,128)(2,1)} %get-tuple-element.86.left.gate_low, bf16[1024,1024]{1,0:T(8,128)(2,1)} %get-tuple-element.87.right.up_low, bf16[2048,1024]{1,0:T(8,128)(2,1)} %copy-done, bf16[2048,1024]{1,0:T(8,128)(2,1)} %all-gather.8.cloned.1.call-done.up_cols.right_cols), custom_call_target="tpu_custom_call" | custom-call | tf_op jit(solution)/shard_map/pallas_call | solution.py:158
  343.8 9.2 %shard_map.228 = f32[512,2048]{1,0:T(8,128)} custom-call(bf16[1024,1024]{1,0:T(8,128)(2,1)} %get-tuple-element.86.left.gate_low, bf16[1024,1024]{1,0:T(8,128)(2,1)} %get-tuple-element.87.right.up_low, bf16[2048,1024]{1,0:T(8,128)(2,1)} %copy-done, bf16[2048,1024]{1,0:T(8,128)(2,1)} %all-gather.8.cloned.1.call-done.up_cols.right_cols), custom_call_target="tpu_custom_call" | custom-call | tf_op jit(solution)/shard_map/pallas_call | solution.py:158
  353.0 4.2 add_convert_fusion.2
  357.2 4.6 all-to-all-start.6
  362.6 9.5 %shard_map.230 = (bf16[1024,1024]{1,0:T(8,128)(2,1)}, bf16[1024,1024]{1,0:T(8,128)(2,1)}) custom-call(s32[4]{0:T(128)} %get-tuple-element.141.order, bf16[1024,2048]{1,0:T(8,128)(2,1)} %get-tuple-element.85.left.right, bf16[1024,2048]{1,0:T(8,128)(2,1)} %get-tuple-element.85.left.right, bf16[1024,1024]{1,0:T(8,128)(2,1)} %get-tuple-element.86.left.gate_low, ...), custom_call_target="tpu_custom_call" | custom-call | tf_op jit(solution)/shard_map/pallas_call | solution.py:129
  373.5 5.8 shard_map.232
  380.6 4.8 pad_maximum_fusion.refs_0_
  385.4 9.3 %shard_map.234 = (bf16[1024,1024]{1,0:T(8,128)(2,1)}, bf16[1024,1024]{1,0:T(8,128)(2,1)}) custom-call(s32[4]{0:T(128)} %get-tuple-element.140.order, bf16[1024,2048]{1,0:T(8,128)(2,1)} %get-tuple-element.85.left.right, bf16[1024,2048]{1,0:T(8,128)(2,1)} %get-tuple-element.85.left.right, bf16[1024,1024]{1,0:T(8,128)(2,1)} %get-tuple-element.86.left.gate_low, ...), custom_call_target="tpu_custom_call" | custom-call | tf_op jit(solution)/shard_map/pallas_call | solution.py:129
  394.7 8.7 %shard_map.233 = bf16[1024,2048]{1,0:T(8,128)(2,1)} custom-call(bf16[1024,1024]{1,0:T(8,128)(2,1)} %get-tuple-element.90.left, bf16[1024,2048]{1,0:T(8,128)(2,1)} %pad_maximum_fusion.refs_0_), custom_call_target="tpu_custom_call" | custom-call | tf_op jit(solution)/shard_map/pallas_call | solution.py:62
  403.4 6.2 shard_map.231
  409.6 4.9 add_convert_fusion.1
  416.8 11.0 %collective-permute-done.22 = bf16[1024,1024]{1,0:T(8,128)(2,1)} collective-permute-done((bf16[1024,1024]{1,0:T(8,128)(2,1)}, bf16[1024,1024]{1,0:T(8,128)(2,1)}, u32[]{:S(2)}, u32[]{:S(2)}) %collective-permute-start.22) | collective-permute-done | bytes 2097184 | tf_op jit(solution)/shard_map/ppermute | solution.py:170
  438.7 6.6 collective-permute-done.24.refs_1_
  445.3 12.5 %collective-permute-done.25.refs_2_ = bf16[128,2048]{1,0:T(8,128)(2,1)S(1)} collective-permute-done((bf16[128,2048]{1,0:T(8,128)(2,1)S(1)}, bf16[128,2048]{1,0:T(8,128)(2,1)S(1)}, u32[]{:S(2)}, u32[]{:S(2)}) %collective-permute-start.25) | collective-permute-done | bytes 524320 | tf_op jit(solution)/shard_map/ppermute | solution.py:170
  467.9 10.5 %collective-permute-done.31 = bf16[512,1024]{1,0:T(8,128)(2,1)} collective-permute-done((bf16[512,1024]{1,0:T(8,128)(2,1)}, bf16[512,1024]{1,0:T(8,128)(2,1)}, u32[]{:S(2)}, u32[]{:S(2)}) %collective-permute-start.31) | collective-permute-done | bytes 1048608 | tf_op jit(solution)/shard_map/ppermute | solution.py:170
  478.4 3.7 fusion.8
  482.0 5.0 all-to-all-start.7
  488.0 4.2 fusion.5
  493.6 12.9 %shard_map.236 = bf16[1024,768]{1,0:T(8,128)(2,1)S(1)} custom-call(s32[16]{0:T(128)S(1)} %fusion.29.offsets, bf16[1024,256]{1,0:T(8,128)(2,1)S(1)} %convolution_convert_fusion.4.upstream, bf16[1024,256]{1,0:T(8,128)(2,1)S(1)} %get-tuple-element.98.query_in, bf16[1024,256]{1,0:T(8,128)(2,1)S(1)} %copy-done.23, bf16[1024,256]{1,0:T(8,128)(2,1)S(1)} %copy-done.25, ...), custom_call_target="tpu_custom_call" | custom-call | tf_op jit(solution)/shard_map/pallas_call | solution.py:564
  507.6 16.6 %all-to-all-done.7.packed = bf16[8,64,1024]{2,1,0:T(8,128)(2,1)S(1)} async-done(((bf16[8,64,1024]{2,1,0:T(8,128)(2,1)}), bf16[8,64,1024]{2,1,0:T(8,128)(2,1)S(1)}, u32[]{:S(2)}, u32[]{:S(2)}) %all-to-all-start.7) | async-done | bytes 1048608 | tf_op jit(solution)/shard_map/all_to_all | solution.py:712
  524.3 8.1 %convolution_convert_fusion = bf16[2048,768]{1,0:T(8,128)(2,1)} fusion(bf16[1024,2048]{1,0:T(8,128)(2,1)} %fusion.2, bf16[1024,768]{1,0:T(8,128)(2,1)} %copy-done.4), kind=kOutput, calls=%fused_computation.11 | convolution fusion | flops 3222798336 | bytes 8912896 | tf_op jit(solution)/shard_map/dot_general | solution.py:41
  532.3 3.1 convolution_convert_fusion.2
  535.6 3.6 all-to-all-start.8
  539.2 2.8 dynamic-slice_bitcast_fusion
  543.7 21.5 %all-to-all-done.8.packed = bf16[8,64,1024]{2,1,0:T(8,128)(2,1)S(1)} async-done(((bf16[8,64,1024]{2,1,0:T(8,128)(2,1)}), bf16[8,64,1024]{2,1,0:T(8,128)(2,1)S(1)}, u32[]{:S(2)}, u32[]{:S(2)}) %all-to-all-start.8) | async-done | bytes 1048608 | tf_op jit(solution)/shard_map/all_to_all | solution.py:712
  565.2 4.4 add_convert_fusion
  575.6 20.8 %collective-permute-start.41 = (bf16[8,64,768]{2,1,0:T(8,128)(2,1)}, bf16[8,64,768]{2,1,0:T(8,128)(2,1)}, u32[]{:S(2)}, u32[]{:S(2)}) collective-permute-start(bf16[8,64,768]{2,1,0:T(8,128)(2,1)} %get-tuple-element.122), channel_id=1, source_target_pairs={{3,2},{0,1},{7,6},{4,5},{11,10},{8,9},{15,14},{12,13},{19,18},{16,... | collective-permute-start | bytes 2359304 | tf_op jit(solution)/shard_map/ppermute | solution.py:174
  596.4 3.2 collective-permute-done.36
  606.1 5.5 collective-permute-done.41
  611.5 11.3 %collective-permute-start.43 = (bf16[8,64,768]{2,1,0:T(8,128)(2,1)}, bf16[8,64,768]{2,1,0:T(8,128)(2,1)S(1)}, u32[]{:S(2)}, u32[]{:S(2)}) collective-permute-start(bf16[8,64,768]{2,1,0:T(8,128)(2,1)} %get-tuple-element.106), channel_id=1, source_target_pairs={{0,1},{1,0},{2,3},{3,2},{4,5},{5,4},{6,7},{7,6},{8,9},{9,8},{10,11... | collective-permute-start | bytes 2359304 | tf_op jit(solution)/shard_map/ppermute | solution.py:170
  627.9 25.8 %collective-permute-done.43 = bf16[8,64,768]{2,1,0:T(8,128)(2,1)S(1)} collective-permute-done((bf16[8,64,768]{2,1,0:T(8,128)(2,1)}, bf16[8,64,768]{2,1,0:T(8,128)(2,1)S(1)}, u32[]{:S(2)}, u32[]{:S(2)}) %collective-permute-start.43) | collective-permute-done | bytes 786464 | tf_op jit(solution)/shard_map/ppermute | solution.py:170
  653.7 6.6 collective-permute-done.42
  660.4 2.7 fusion.11
  664.5 2.9 collective-permute-start.45
  669.3 3.5 all-to-all-start.9
  672.9 2.8 fusion.16
  676.2 9.2 %all-to-all-done.9.packed = bf16[8,64,768]{2,1,0:T(8,128)(2,1)S(1)} async-done(((bf16[8,64,768]{2,1,0:T(8,128)(2,1)}), bf16[8,64,768]{2,1,0:T(8,128)(2,1)S(1)}, u32[]{:S(2)}, u32[]{:S(2)}) %all-to-all-start.9) | async-done | bytes 786464 | tf_op jit(solution)/shard_map/all_to_all | solution.py:774
  686.6 2.8 convert_element_type.224
  (252 shorter events, 109.7 us)
Async XLA Ops:
  8.5 14.4 %all-to-all-start = ((f32[32,1,128]{2,1,0:T(1,128)}), f32[32,1,128]{2,1,0:T(1,128)S(1)}, u32[]{:S(2)}, u32[]{:S(2)}) async-start(f32[32,1,128]{2,1,0:T(1,128)} %broadcast_in_dim.17), calls=%async_computation | async-start | bytes 32768 | tf_op jit(solution)/shard_map/all_to_all | solution.py:280
  15.9 156.0 %all-gather.4.cloned.1.call-start = ((), (), s32[]{:S(2)}) async-start(), calls=%async_computation.13 | async-start | bytes 5242880 | tf_op jit(solution)/shard_map/all_gather | solution.py:640
  37.9 80.3 %copy-start.6 = (bf16[8,64,768]{2,1,0:T(8,128)(2,1)}, bf16[8,64,768]{2,1,0:T(8,128)(2,1)S(1)}, u32[]{:S(2)}) copy-start(bf16[8,64,768]{2,1,0:T(8,128)(2,1)S(1)} %all_to_all.54.refs_0_) | copy-start | bytes 2359300
  41.6 64.0 %all-to-all-start.2 = ((bf16[8,64,1024]{2,1,0:T(8,128)(2,1)}), bf16[8,64,1024]{2,1,0:T(8,128)(2,1)S(1)}, u32[]{:S(2)}, u32[]{:S(2)}) async-start(bf16[8,64,1024]{2,1,0:T(8,128)(2,1)} %copy-done.19), calls=%async_computation.2 | async-start | bytes 2097152 | tf_op jit(solution)/shard_map/all_to_all | solution.py:632
  45.2 144.2 %all-gather.6.cloned.1.call-start = ((), (), s32[]{:S(2)}) async-start(), calls=%async_computation.14 | async-start | bytes 1310720 | tf_op jit(solution)/shard_map/all_gather | solution.py:635
  46.0 48.4 %collective-permute-start.7 = (bf16[8,64,768]{2,1,0:T(8,128)(2,1)S(1)}, bf16[8,64,768]{2,1,0:T(8,128)(2,1)S(1)}, u32[]{:S(2)}, u32[]{:S(2)}) collective-permute-start(bf16[8,64,768]{2,1,0:T(8,128)(2,1)S(1)} %all_to_all.54.refs_0_), channel_id=1, source_target_pairs={{0,1},{1,0},{2,3},{3,2},{4,5},{5,4},{6,7},{7,6},{8,9},{9,8},{10,11... | collective-permute-start | bytes 2359304 | tf_op jit(solution)/shard_map/ppermute | solution.py:170
  48.1 19.9 %collective-permute-start = (bf16[128,2048]{1,0:T(8,128)(2,1)S(1)}, bf16[128,2048]{1,0:T(8,128)(2,1)}, u32[]{:S(2)}, u32[]{:S(2)}) collective-permute-start(bf16[128,2048]{1,0:T(8,128)(2,1)S(1)} %bitcast.68), channel_id=1, source_target_pairs={{0,8},{8,0},{16,24},{24,16},{1,9},{9,1},{17,25},{25,17},{2,10},{10... | collective-permute-start | bytes 1572872 | tf_op jit(solution)/shard_map/ppermute | solution.py:170
  48.6 19.6 %collective-permute-start.1 = (bf16[128,2048]{1,0:T(8,128)(2,1)S(1)}, bf16[128,2048]{1,0:T(8,128)(2,1)}, u32[]{:S(2)}, u32[]{:S(2)}) collective-permute-start(bf16[128,2048]{1,0:T(8,128)(2,1)S(1)} %bitcast.69), channel_id=1, source_target_pairs={{0,16},{8,24},{16,0},{24,8},{1,17},{9,25},{17,1},{25,9},{2,18},{10... | collective-permute-start | bytes 1572872 | tf_op jit(solution)/shard_map/ppermute | solution.py:170
  49.2 38.1 %collective-permute-start.2 = (bf16[128,2048]{1,0:T(8,128)(2,1)S(1)}, bf16[128,2048]{1,0:T(8,128)(2,1)}, u32[]{:S(2)}, u32[]{:S(2)}) collective-permute-start(bf16[128,2048]{1,0:T(8,128)(2,1)S(1)} %bitcast.70), channel_id=1, source_target_pairs={{0,24},{8,16},{16,8},{24,0},{1,25},{9,17},{17,9},{25,1},{2,26},{10... | collective-permute-start | bytes 1572872 | tf_op jit(solution)/shard_map/ppermute | solution.py:170
  51.6 54.0 %collective-permute-start.8 = (bf16[8,64,768]{2,1,0:T(8,128)(2,1)S(1)}, bf16[8,64,768]{2,1,0:T(8,128)(2,1)}, u32[]{:S(2)}, u32[]{:S(2)}) collective-permute-start(bf16[8,64,768]{2,1,0:T(8,128)(2,1)S(1)} %all_to_all.54.refs_0_), channel_id=1, source_target_pairs={{0,2},{1,3},{2,0},{3,1},{4,6},{5,7},{6,4},{7,5},{8,10},{9,11},{10,... | collective-permute-start | bytes 2359304 | tf_op jit(solution)/shard_map/ppermute | solution.py:170
  68.0 42.0 %collective-permute-start.3 = (bf16[128,2048]{1,0:T(8,128)(2,1)S(1)}, bf16[128,2048]{1,0:T(8,128)(2,1)}, u32[]{:S(2)}, u32[]{:S(2)}) collective-permute-start(bf16[128,2048]{1,0:T(8,128)(2,1)S(1)} %bitcast.71), channel_id=1, source_target_pairs={{0,4},{4,0},{1,5},{5,1},{2,6},{6,2},{3,7},{7,3},{8,12},{12,8},{9,1... | collective-permute-start | bytes 1572872 | tf_op jit(solution)/shard_map/ppermute | solution.py:170
  68.2 41.8 %collective-permute-start.4 = (bf16[128,2048]{1,0:T(8,128)(2,1)}, bf16[128,2048]{1,0:T(8,128)(2,1)}, u32[]{:S(2)}, u32[]{:S(2)}) collective-permute-start(bf16[128,2048]{1,0:T(8,128)(2,1)} %collective-permute-done.refs_1_), channel_id=1, source_target_pairs={{0,4},{4,0},{1,5},{5,1},{2,6},{6,2},{3,7},{7,3},{8,12},{12,8},{9,1... | collective-permute-start | bytes 1572872 | tf_op jit(solution)/shard_map/ppermute | solution.py:170
  87.3 22.7 %collective-permute-start.5 = (bf16[128,2048]{1,0:T(8,128)(2,1)}, bf16[128,2048]{1,0:T(8,128)(2,1)}, u32[]{:S(2)}, u32[]{:S(2)}) collective-permute-start(bf16[128,2048]{1,0:T(8,128)(2,1)} %collective-permute-done.1.refs_2_), channel_id=1, source_target_pairs={{0,4},{4,0},{1,5},{5,1},{2,6},{6,2},{3,7},{7,3},{8,12},{12,8},{9,1... | collective-permute-start | bytes 1572872 | tf_op jit(solution)/shard_map/ppermute | solution.py:170
  94.3 15.7 %collective-permute-start.6 = (bf16[128,2048]{1,0:T(8,128)(2,1)}, bf16[128,2048]{1,0:T(8,128)(2,1)}, u32[]{:S(2)}, u32[]{:S(2)}) collective-permute-start(bf16[128,2048]{1,0:T(8,128)(2,1)} %collective-permute-done.2.refs_3_), channel_id=1, source_target_pairs={{0,4},{4,0},{1,5},{5,1},{2,6},{6,2},{3,7},{7,3},{8,12},{12,8},{9,1... | collective-permute-start | bytes 1572872 | tf_op jit(solution)/shard_map/ppermute | solution.py:170
  105.6 61.0 %all-to-all-start.3 = ((bf16[8,64,1024]{2,1,0:T(8,128)(2,1)}), bf16[8,64,1024]{2,1,0:T(8,128)(2,1)}, u32[]{:S(2)}, u32[]{:S(2)}) async-start(bf16[8,64,1024]{2,1,0:T(8,128)(2,1)} %copy-done.18), calls=%async_computation.3 | async-start | bytes 2097152 | tf_op jit(solution)/shard_map/all_to_all | solution.py:632
  113.3 50.2 %collective-permute-start.13 = (bf16[8,64,768]{2,1,0:T(8,128)(2,1)}, bf16[8,64,768]{2,1,0:T(8,128)(2,1)S(1)}, u32[]{:S(2)}, u32[]{:S(2)}) collective-permute-start(bf16[8,64,768]{2,1,0:T(8,128)(2,1)} %collective-permute-done.8.refs_2_), channel_id=1, source_target_pairs={{2,3},{1,0},{6,7},{5,4},{10,11},{9,8},{14,15},{13,12},{18,19},{17,... | collective-permute-start | bytes 2359304 | tf_op jit(solution)/shard_map/ppermute | solution.py:174
  114.6 49.0 %collective-permute-start.10 = (bf16[512,1024]{1,0:T(8,128)(2,1)S(1)}, bf16[512,1024]{1,0:T(8,128)(2,1)S(1)}, u32[]{:S(2)}, u32[]{:S(2)}) collective-permute-start(bf16[512,1024]{1,0:T(8,128)(2,1)S(1)} %bitcast.73), channel_id=1, source_target_pairs={{0,16},{8,24},{16,0},{24,8},{1,17},{9,25},{17,1},{25,9},{2,18},{10... | collective-permute-start | bytes 3145736 | tf_op jit(solution)/shard_map/ppermute | solution.py:170
  115.2 49.4 %collective-permute-start.11 = (bf16[512,1024]{1,0:T(8,128)(2,1)S(1)}, bf16[512,1024]{1,0:T(8,128)(2,1)S(1)}, u32[]{:S(2)}, u32[]{:S(2)}) collective-permute-start(bf16[512,1024]{1,0:T(8,128)(2,1)S(1)} %bitcast.74), channel_id=1, source_target_pairs={{0,24},{8,16},{16,8},{24,0},{1,25},{9,17},{17,9},{25,1},{2,26},{10... | collective-permute-start | bytes 3145736 | tf_op jit(solution)/shard_map/ppermute | solution.py:170
  116.6 48.9 %collective-permute-start.9 = (bf16[512,1024]{1,0:T(8,128)(2,1)S(1)}, bf16[512,1024]{1,0:T(8,128)(2,1)S(1)}, u32[]{:S(2)}, u32[]{:S(2)}) collective-permute-start(bf16[512,1024]{1,0:T(8,128)(2,1)S(1)} %bitcast.75), channel_id=1, source_target_pairs={{0,8},{8,0},{16,24},{24,16},{1,9},{9,1},{17,25},{25,17},{2,10},{10... | collective-permute-start | bytes 3145736 | tf_op jit(solution)/shard_map/ppermute | solution.py:170
  118.2 4.3 collective-permute-start.12
  192.8 10.0 %collective-permute-start.14 = (bf16[512,2048]{1,0:T(8,128)(2,1)}, bf16[512,2048]{1,0:T(8,128)(2,1)}, u32[]{:S(2)}, u32[]{:S(2)}) collective-permute-start(bf16[512,2048]{1,0:T(8,128)(2,1)} %convolution_convert_fusion.1), channel_id=1, source_target_pairs={{0,4},{4,0},{1,5},{5,1},{2,6},{6,2},{3,7},{7,3},{8,12},{12,8},{9,1... | collective-permute-start | bytes 6291464 | tf_op jit(solution)/shard_map/ppermute | solution.py:170
  194.4 57.9 %all-to-all-start.5 = ((bf16[4,128,2048]{2,1,0:T(8,128)(2,1)}), bf16[4,128,2048]{2,1,0:T(8,128)(2,1)}, u32[]{:S(2)}, u32[]{:S(2)}) async-start(bf16[4,128,2048]{2,1,0:T(8,128)(2,1)} %broadcast_in_dim.19), calls=%async_computation.5 | async-start | bytes 4194304 | tf_op jit(solution)/shard_map/all_to_all | solution.py:266
  202.8 111.3 %all-gather.8.cloned.1.call-start = ((), (), s32[]{:S(2)}) async-start(), calls=%async_computation.15 | async-start | bytes 5242880 | tf_op jit(solution)/shard_map/all_gather | solution.py:645
  208.1 16.1 %collective-permute-start.15 = (bf16[128,2048]{1,0:T(8,128)(2,1)}, bf16[128,2048]{1,0:T(8,128)(2,1)}, u32[]{:S(2)}, u32[]{:S(2)}) collective-permute-start(bf16[128,2048]{1,0:T(8,128)(2,1)} %get-tuple-element.128), channel_id=1, source_target_pairs={{0,8},{8,0},{16,24},{24,16},{1,9},{9,1},{17,25},{25,17},{2,10},{10... | collective-permute-start | bytes 1572872 | tf_op jit(solution)/shard_map/ppermute | solution.py:170
  208.7 17.1 %collective-permute-start.16 = (bf16[128,2048]{1,0:T(8,128)(2,1)}, bf16[128,2048]{1,0:T(8,128)(2,1)}, u32[]{:S(2)}, u32[]{:S(2)}) collective-permute-start(bf16[128,2048]{1,0:T(8,128)(2,1)} %get-tuple-element.130), channel_id=1, source_target_pairs={{0,16},{8,24},{16,0},{24,8},{1,17},{9,25},{17,1},{25,9},{2,18},{10... | collective-permute-start | bytes 1572872 | tf_op jit(solution)/shard_map/ppermute | solution.py:170
  209.2 35.8 %collective-permute-start.17 = (bf16[128,2048]{1,0:T(8,128)(2,1)}, bf16[128,2048]{1,0:T(8,128)(2,1)}, u32[]{:S(2)}, u32[]{:S(2)}) collective-permute-start(bf16[128,2048]{1,0:T(8,128)(2,1)} %get-tuple-element.129), channel_id=1, source_target_pairs={{0,24},{8,16},{16,8},{24,0},{1,25},{9,17},{17,9},{25,1},{2,26},{10... | collective-permute-start | bytes 1572872 | tf_op jit(solution)/shard_map/ppermute | solution.py:170
  255.0 53.2 %all-to-all-start.4 = ((bf16[4,128,2048]{2,1,0:T(8,128)(2,1)}), bf16[4,128,2048]{2,1,0:T(8,128)(2,1)}, u32[]{:S(2)}, u32[]{:S(2)}) async-start(bf16[4,128,2048]{2,1,0:T(8,128)(2,1)} %broadcast_in_dim.18), calls=%async_computation.4 | async-start | bytes 4194304 | tf_op jit(solution)/shard_map/all_to_all | solution.py:266
  259.6 54.5 %collective-permute-start.19 = (bf16[512,2048]{1,0:T(8,128)(2,1)}, bf16[512,2048]{1,0:T(8,128)(2,1)}, u32[]{:S(2)}, u32[]{:S(2)}) collective-permute-start(bf16[512,2048]{1,0:T(8,128)(2,1)} %bitcast.12.near), channel_id=1, source_target_pairs={{0,4},{4,0},{1,5},{5,1},{2,6},{6,2},{3,7},{7,3},{8,12},{12,8},{9,1... | collective-permute-start | bytes 6291464 | tf_op jit(solution)/shard_map/ppermute | solution.py:170
  308.2 6.0 collective-permute-start.18
  343.3 9.7 %collective-permute-start.20 = (bf16[512,2048]{1,0:T(8,128)(2,1)}, bf16[512,2048]{1,0:T(8,128)(2,1)S(1)}, u32[]{:S(2)}, u32[]{:S(2)}) collective-permute-start(bf16[512,2048]{1,0:T(8,128)(2,1)} %shard_map.229), channel_id=1, source_target_pairs={{0,4},{4,0},{1,5},{5,1},{2,6},{6,2},{3,7},{7,3},{8,12},{12,8},{9,1... | collective-permute-start | bytes 6291464 | tf_op jit(solution)/shard_map/ppermute | solution.py:170
  357.2 57.3 %all-to-all-start.6 = ((bf16[4,128,2048]{2,1,0:T(8,128)(2,1)}), bf16[4,128,2048]{2,1,0:T(8,128)(2,1)}, u32[]{:S(2)}, u32[]{:S(2)}) async-start(bf16[4,128,2048]{2,1,0:T(8,128)(2,1)} %bitcast.82), calls=%async_computation.6 | async-start | bytes 4194304 | tf_op jit(solution)/shard_map/all_to_all | solution.py:272
  361.8 162.4 %reduce-scatter.4.cloned.1.call-start = ((), (), s32[]{:S(2)}) async-start(), calls=%async_computation.16 | async-start | bytes 2621440 | tf_op jit(solution)/shard_map/reduce_scatter | solution.py:729
  379.4 30.2 %collective-permute-start.21 = (bf16[512,2048]{1,0:T(8,128)(2,1)}, bf16[512,2048]{1,0:T(8,128)(2,1)}, u32[]{:S(2)}, u32[]{:S(2)}) collective-permute-start(bf16[512,2048]{1,0:T(8,128)(2,1)} %shard_map.232), channel_id=1, source_target_pairs={{0,4},{4,0},{1,5},{5,1},{2,6},{6,2},{3,7},{7,3},{8,12},{12,8},{9,1... | collective-permute-start | bytes 6291464 | tf_op jit(solution)/shard_map/ppermute | solution.py:170
  379.4 48.3 %collective-permute-start.22 = (bf16[1024,1024]{1,0:T(8,128)(2,1)}, bf16[1024,1024]{1,0:T(8,128)(2,1)}, u32[]{:S(2)}, u32[]{:S(2)}) collective-permute-start(bf16[1024,1024]{1,0:T(8,128)(2,1)} %get-tuple-element.88), channel_id=1, source_target_pairs={{0,8},{8,0},{16,24},{24,16},{1,9},{9,1},{17,25},{25,17},{2,10},{10... | collective-permute-start | bytes 6291464 | tf_op jit(solution)/shard_map/ppermute | solution.py:170
  380.2 48.1 %collective-permute-start.23 = (bf16[1024,1024]{1,0:T(8,128)(2,1)}, bf16[1024,1024]{1,0:T(8,128)(2,1)}, u32[]{:S(2)}, u32[]{:S(2)}) collective-permute-start(bf16[1024,1024]{1,0:T(8,128)(2,1)} %get-tuple-element.89), channel_id=1, source_target_pairs={{0,16},{8,24},{16,0},{24,8},{1,17},{9,25},{17,1},{25,9},{2,18},{10... | collective-permute-start | bytes 6291464 | tf_op jit(solution)/shard_map/ppermute | solution.py:170
  430.0 174.1 %reduce-scatter.6.cloned.1.call-start = ((), (), s32[]{:S(2)}) async-start(), calls=%async_computation.17 | async-start | bytes 1310720 | tf_op jit(solution)/shard_map/reduce_scatter | solution.py:741
  430.3 14.9 %collective-permute-start.24 = (bf16[128,2048]{1,0:T(8,128)(2,1)S(1)}, bf16[128,2048]{1,0:T(8,128)(2,1)S(1)}, u32[]{:S(2)}, u32[]{:S(2)}) collective-permute-start(bf16[128,2048]{1,0:T(8,128)(2,1)S(1)} %get-tuple-element.117.refs_0_), channel_id=1, source_target_pairs={{0,8},{8,0},{16,24},{24,16},{1,9},{9,1},{17,25},{25,17},{2,10},{10... | collective-permute-start | bytes 1572872 | tf_op jit(solution)/shard_map/ppermute | solution.py:170
  431.6 26.1 %collective-permute-start.25 = (bf16[128,2048]{1,0:T(8,128)(2,1)S(1)}, bf16[128,2048]{1,0:T(8,128)(2,1)S(1)}, u32[]{:S(2)}, u32[]{:S(2)}) collective-permute-start(bf16[128,2048]{1,0:T(8,128)(2,1)S(1)} %get-tuple-element.117.refs_0_), channel_id=1, source_target_pairs={{0,16},{8,24},{16,0},{24,8},{1,17},{9,25},{17,1},{25,9},{2,18},{10... | collective-permute-start | bytes 1572872 | tf_op jit(solution)/shard_map/ppermute | solution.py:170
  432.4 25.3 %collective-permute-start.26 = (bf16[128,2048]{1,0:T(8,128)(2,1)S(1)}, bf16[128,2048]{1,0:T(8,128)(2,1)S(1)}, u32[]{:S(2)}, u32[]{:S(2)}) collective-permute-start(bf16[128,2048]{1,0:T(8,128)(2,1)S(1)} %get-tuple-element.117.refs_0_), channel_id=1, source_target_pairs={{0,24},{8,16},{16,8},{24,0},{1,25},{9,17},{17,9},{25,1},{2,26},{10... | collective-permute-start | bytes 1572872 | tf_op jit(solution)/shard_map/ppermute | solution.py:170
  438.3 40.1 %collective-permute-start.31 = (bf16[512,1024]{1,0:T(8,128)(2,1)}, bf16[512,1024]{1,0:T(8,128)(2,1)}, u32[]{:S(2)}, u32[]{:S(2)}) collective-permute-start(bf16[512,1024]{1,0:T(8,128)(2,1)} %fusion.6), channel_id=1, source_target_pairs={{0,16},{8,24},{16,0},{24,8},{1,17},{9,25},{17,1},{25,9},{2,18},{10... | collective-permute-start | bytes 3145736 | tf_op jit(solution)/shard_map/ppermute | solution.py:170
  438.7 23.9 %collective-permute-start.27 = (bf16[128,2048]{1,0:T(8,128)(2,1)S(1)}, bf16[128,2048]{1,0:T(8,128)(2,1)S(1)}, u32[]{:S(2)}, u32[]{:S(2)}) collective-permute-start(bf16[128,2048]{1,0:T(8,128)(2,1)S(1)} %get-tuple-element.117.refs_0_), channel_id=1, source_target_pairs={{0,4},{4,0},{1,5},{5,1},{2,6},{6,2},{3,7},{7,3},{8,12},{12,8},{9,1... | collective-permute-start | bytes 1572872 | tf_op jit(solution)/shard_map/ppermute | solution.py:170
  445.3 18.2 %collective-permute-start.28 = (bf16[128,2048]{1,0:T(8,128)(2,1)S(1)}, bf16[128,2048]{1,0:T(8,128)(2,1)S(1)}, u32[]{:S(2)}, u32[]{:S(2)}) collective-permute-start(bf16[128,2048]{1,0:T(8,128)(2,1)S(1)} %collective-permute-done.24.refs_1_), channel_id=1, source_target_pairs={{0,4},{4,0},{1,5},{5,1},{2,6},{6,2},{3,7},{7,3},{8,12},{12,8},{9,1... | collective-permute-start | bytes 1572872 | tf_op jit(solution)/shard_map/ppermute | solution.py:170
  457.7 5.7 collective-permute-start.29
  457.7 5.7 collective-permute-start.30
  462.6 25.4 %collective-permute-start.32 = (bf16[512,1024]{1,0:T(8,128)(2,1)}, bf16[512,1024]{1,0:T(8,128)(2,1)}, u32[]{:S(2)}, u32[]{:S(2)}) collective-permute-start(bf16[512,1024]{1,0:T(8,128)(2,1)} %fusion.3), channel_id=1, source_target_pairs={{0,8},{8,0},{16,24},{24,16},{1,9},{9,1},{17,25},{25,17},{2,10},{10... | collective-permute-start | bytes 3145736 | tf_op jit(solution)/shard_map/ppermute | solution.py:170
  482.0 42.2 %all-to-all-start.7 = ((bf16[8,64,1024]{2,1,0:T(8,128)(2,1)}), bf16[8,64,1024]{2,1,0:T(8,128)(2,1)S(1)}, u32[]{:S(2)}, u32[]{:S(2)}) async-start(bf16[8,64,1024]{2,1,0:T(8,128)(2,1)} %bitcast.84), calls=%async_computation.8 | async-start | bytes 2097152 | tf_op jit(solution)/shard_map/all_to_all | solution.py:712
  487.1 199.6 %reduce-scatter.8.cloned.1.call-start = ((), (), s32[]{:S(2)}) async-start(), calls=%async_computation.18 | async-start | bytes 5242880 | tf_op jit(solution)/shard_map/reduce_scatter | solution.py:735
  535.5 29.7 %collective-permute-start.34 = (bf16[512,2048]{1,0:T(8,128)(2,1)}, bf16[512,2048]{1,0:T(8,128)(2,1)}, u32[]{:S(2)}, u32[]{:S(2)}) collective-permute-start(bf16[512,2048]{1,0:T(8,128)(2,1)} %convolution_convert_fusion.2), channel_id=1, source_target_pairs={{0,4},{4,0},{1,5},{5,1},{2,6},{6,2},{3,7},{7,3},{8,12},{12,8},{9,1... | collective-permute-start | bytes 6291464 | tf_op jit(solution)/shard_map/ppermute | solution.py:170
  535.6 29.6 %all-to-all-start.8 = ((bf16[8,64,1024]{2,1,0:T(8,128)(2,1)}), bf16[8,64,1024]{2,1,0:T(8,128)(2,1)S(1)}, u32[]{:S(2)}, u32[]{:S(2)}) async-start(bf16[8,64,1024]{2,1,0:T(8,128)(2,1)} %bitcast.83), calls=%async_computation.9 | async-start | bytes 2097152 | tf_op jit(solution)/shard_map/all_to_all | solution.py:712
  539.2 26.0 %slice-start = ((bf16[1024,768]{1,0:T(8,128)(2,1)}), bf16[512,768]{1,0:T(8,128)(2,1)S(1)}, s32[]{:S(2)}) async-start(bf16[1024,768]{1,0:T(8,128)(2,1)} %copy-done.4), calls=%async_computation.19 | async-start | bytes 1572864 | tf_op jit(solution)/shard_map/slice | solution.py:762
  542.0 1.7 collective-permute-start.33
  572.1 24.3 %collective-permute-start.35 = (bf16[128,2048]{1,0:T(8,128)(2,1)}, bf16[128,2048]{1,0:T(8,128)(2,1)S(1)}, u32[]{:S(2)}, u32[]{:S(2)}) collective-permute-start(bf16[128,2048]{1,0:T(8,128)(2,1)} %get-tuple-element.123), channel_id=1, source_target_pairs={{0,8},{8,0},{16,24},{24,16},{1,9},{9,1},{17,25},{25,17},{2,10},{10... | collective-permute-start | bytes 1572872 | tf_op jit(solution)/shard_map/ppermute | solution.py:170
  573.5 26.0 %collective-permute-start.36 = (bf16[128,2048]{1,0:T(8,128)(2,1)}, bf16[128,2048]{1,0:T(8,128)(2,1)}, u32[]{:S(2)}, u32[]{:S(2)}) collective-permute-start(bf16[128,2048]{1,0:T(8,128)(2,1)} %get-tuple-element.125), channel_id=1, source_target_pairs={{0,16},{8,24},{16,0},{24,8},{1,17},{9,25},{17,1},{25,9},{2,18},{10... | collective-permute-start | bytes 1572872 | tf_op jit(solution)/shard_map/ppermute | solution.py:170
  575.0 24.6 %collective-permute-start.37 = (bf16[128,2048]{1,0:T(8,128)(2,1)}, bf16[128,2048]{1,0:T(8,128)(2,1)}, u32[]{:S(2)}, u32[]{:S(2)}) collective-permute-start(bf16[128,2048]{1,0:T(8,128)(2,1)} %get-tuple-element.124), channel_id=1, source_target_pairs={{0,24},{8,16},{16,8},{24,0},{1,25},{9,17},{17,9},{25,1},{2,26},{10... | collective-permute-start | bytes 1572872 | tf_op jit(solution)/shard_map/ppermute | solution.py:170
  575.6 36.0 %collective-permute-start.41 = (bf16[8,64,768]{2,1,0:T(8,128)(2,1)}, bf16[8,64,768]{2,1,0:T(8,128)(2,1)}, u32[]{:S(2)}, u32[]{:S(2)}) collective-permute-start(bf16[8,64,768]{2,1,0:T(8,128)(2,1)} %get-tuple-element.122), channel_id=1, source_target_pairs={{3,2},{0,1},{7,6},{4,5},{11,10},{8,9},{15,14},{12,13},{19,18},{16,... | collective-permute-start | bytes 2359304 | tf_op jit(solution)/shard_map/ppermute | solution.py:174
  601.6 21.3 %collective-permute-start.38 = (f32[2,2048]{1,0:T(2,128)S(1)}, f32[2,2048]{1,0:T(2,128)S(1)}, u32[]{:S(2)}, u32[]{:S(2)}) collective-permute-start(f32[2,2048]{1,0:T(2,128)S(1)} %pad_maximum_fusion.3), channel_id=1, source_target_pairs={{0,8},{8,0},{16,24},{24,16},{1,9},{9,1},{17,25},{25,17},{2,10},{10... | collective-permute-start | bytes 49160 | tf_op jit(solution)/shard_map/ppermute | solution.py:170
  604.2 22.6 %copy-start.46 = (bf16[128,2048]{1,0:T(8,128)(2,1)S(1)}, bf16[128,2048]{1,0:T(8,128)(2,1)}, u32[]{:S(2)}) copy-start(bf16[128,2048]{1,0:T(8,128)(2,1)} %reduce-scatter.4.cloned.1.call-done) | copy-start | bytes 1572868
  611.5 42.2 %collective-permute-start.43 = (bf16[8,64,768]{2,1,0:T(8,128)(2,1)}, bf16[8,64,768]{2,1,0:T(8,128)(2,1)S(1)}, u32[]{:S(2)}, u32[]{:S(2)}) collective-permute-start(bf16[8,64,768]{2,1,0:T(8,128)(2,1)} %get-tuple-element.106), channel_id=1, source_target_pairs={{0,1},{1,0},{2,3},{3,2},{4,5},{5,4},{6,7},{7,6},{8,9},{9,8},{10,11... | collective-permute-start | bytes 2359304 | tf_op jit(solution)/shard_map/ppermute | solution.py:170
  622.8 3.8 collective-permute-start.39
  625.4 35.0 %collective-permute-start.42 = (bf16[8,64,768]{2,1,0:T(8,128)(2,1)S(1)}, bf16[8,64,768]{2,1,0:T(8,128)(2,1)S(1)}, u32[]{:S(2)}, u32[]{:S(2)}) collective-permute-start(bf16[8,64,768]{2,1,0:T(8,128)(2,1)S(1)} %fusion.12), channel_id=1, source_target_pairs={{0,2},{1,3},{2,0},{3,1},{4,6},{5,7},{6,4},{7,5},{8,10},{9,11},{10,... | collective-permute-start | bytes 2359304 | tf_op jit(solution)/shard_map/ppermute | solution.py:170
  626.7 1.2 collective-permute-start.40
  660.4 4.2 collective-permute-start.44
  664.5 4.7 collective-permute-start.45
  669.3 16.1 %all-to-all-start.9 = ((bf16[8,64,768]{2,1,0:T(8,128)(2,1)}), bf16[8,64,768]{2,1,0:T(8,128)(2,1)S(1)}, u32[]{:S(2)}, u32[]{:S(2)}) async-start(bf16[8,64,768]{2,1,0:T(8,128)(2,1)} %fusion.11), calls=%async_computation.10 | async-start | bytes 1572864 | tf_op jit(solution)/shard_map/all_to_all | solution.py:774
  (48 other events, 231.9 us)
Sparse Core Ops, SparseCore 0:
  38.0 64.4 all-gather.3
  104.1 47.8 all-gather.5
  211.7 64.0 all-gather.7
  430.1 44.2 reduce-scatter.3
  476.7 38.4 reduce-scatter.5
  524.4 51.9 reduce-scatter.7

commit v2 on v1

--- a/solution.py
+++ b/solution.py
@@ -68,6 +68,26 @@
         out_shape=[jax.ShapeDtypeStruct((extent, width), dtype) for width in widths],
         compiler_params=pltpu.CompilerParams(vmem_limit_bytes=VMEM_BYTES),
     )(left, *rights)
+
+
+def halves_kernel(left, near, far, out):
+    half = near.shape[0]
+    total = matmul(left[:half, :], near[...], 0, 0) + matmul(left[half:, :], far[...], 0, 0)
+    out[...] = total.astype(LOW)
+
+
+def product_halves(left, near, far):
+    count, hidden = left.shape
+    tile = min(TILE, hidden)
+    whole = pl.BlockSpec(near.shape, lambda i: (0, 0))
+    return pl.pallas_call(
+        halves_kernel,
+        grid=(hidden // tile,),
+        in_specs=[pl.BlockSpec((count, tile), lambda i: (0, i)), whole, whole],
+        out_specs=pl.BlockSpec((tile, near.shape[1]), lambda i: (i, 0)),
+        out_shape=jax.ShapeDtypeStruct((hidden, near.shape[1]), LOW),
+        compiler_params=pltpu.CompilerParams(vmem_limit_bytes=VMEM_BYTES),
+    )(left, near, far)
 
 
 def expand_kernel(
@@ -94,23 +114,24 @@
         up_low[here, :] = (act_grad * silu).astype(LOW)
 
 
-def expand(near_in, far_in, near, far, gate_cols, up_cols, down_rows):
+def expand(near_in, far_in, near, far, cols, down_rows):
     half, width = near.shape
     total = 2 * half
-    hidden = gate_cols.shape[1]
+    hidden = cols.shape[1] // 2
     tile = min(TILE, hidden)
     once = pl.BlockSpec((half, width), lambda i: (0, 0), pipeline_mode=pl.Buffered(1))
     column = pl.BlockSpec((width, tile), lambda i: (0, i))
+    other = pl.BlockSpec((width, tile), lambda i: (0, hidden // tile + i))
     out = pl.BlockSpec((total, tile), lambda i: (0, i))
     return pl.pallas_call(
         expand_kernel,
         grid=(hidden // tile,),
-        in_specs=[once] * 4 + [column, column, pl.BlockSpec((tile, width), lambda i: (i, 0))],
+        in_specs=[once] * 4 + [column, other, pl.BlockSpec((tile, width), lambda i: (i, 0))],
         out_specs=[pl.BlockSpec((total, width), lambda i: (0, 0))] + [out] * 3,
         out_shape=[jax.ShapeDtypeStruct((total, width), LOW)]
         + [jax.ShapeDtypeStruct((total, hidden), LOW)] * 3,
         compiler_params=pltpu.CompilerParams(vmem_limit_bytes=VMEM_BYTES),
-    )(near_in, far_in, near, far, gate_cols, up_cols, down_rows)
+    )(near_in, far_in, near, far, cols, cols, down_rows)
 
 
 def pair_kernel(order, left, right, gate_low, up_low, gate_out, up_out):
@@ -144,25 +165,34 @@
     )(order, rows, rows, gate_low, up_low)
 
 
-def contract_kernel(left, right, left_cols, right_cols, out):
-    total = matmul(left[...], left_cols[...], 1, 1) + matmul(right[...], right_cols[...], 1, 1)
+def contract_kernel(left, right, cols, out):
+    hidden = left.shape[1]
+    total = matmul(left[...], cols[:, :hidden], 1, 1) + matmul(right[...], cols[:, hidden:], 1, 1)
     out[...] = total.astype(out.dtype)
 
 
-def contract(left, right, left_cols, right_cols, part, dtype):
+def contract(left, right, cols, part, dtype):
     count, hidden = left.shape
-    width = left_cols.shape[0]
+    width = cols.shape[0]
     tile = min(512, width)
     rows = pl.BlockSpec((count // 2, hidden), lambda i: (part, 0))
-    cols = pl.BlockSpec((tile, hidden), lambda i: (i, 0))
     return pl.pallas_call(
         contract_kernel,
         grid=(width // tile,),
-        in_specs=[rows, rows, cols, cols],
+        in_specs=[rows, rows, pl.BlockSpec((tile, 2 * hidden), lambda i: (i, 0))],
         out_specs=pl.BlockSpec((count // 2, tile), lambda i: (0, i)),
         out_shape=jax.ShapeDtypeStruct((count // 2, width), dtype),
         compiler_params=pltpu.CompilerParams(vmem_limit_bytes=VMEM_BYTES),
-    )(left, right, left_cols, right_cols)
+    )(left, right, cols)
+
+
+def region(flag, body, *operands):
+    shapes = jax.eval_shape(body, *operands)
+
+    def other(*operands):
+        return jax.tree.map(lambda leaf: jnp.zeros(leaf.shape, leaf.dtype), shapes)
+
+    return lax.cond(flag, body, other, *operands)
 
 
 def swap_with(value, axis, code):
@@ -186,22 +216,6 @@
     return [value, near, far, jnp.where((place == 1) | (place == 2), middle, ends)]
 
 
-def scatter_line(pieces, axis):
-    count = lax.axis_size(axis)
-    if count != 4:
-        early, late = [], [swap_with(pieces[code], axis, code) for code in range(1, count)]
-    else:
-        ends = permute(pieces[3], axis, [(3, 2), (0, 1)])
-        middle = permute(pieces[3], axis, [(1, 2), (2, 1)])
-        passed = (pieces[2].astype(FULL) + ends.astype(FULL)).astype(LOW)
-        early = [middle]
-        late = [swap_with(passed, axis, 2), swap_with(after(pieces[1], ends), axis, 1)]
-    total = pieces[0].astype(FULL)
-    for part in early + late:
-        total = total + part.astype(FULL)
-    return total, early, late
-
-
 def gather_rows(rows, axis, *earlier):
     near = [swap_with(rows, axis, code) for code in range(1, lax.axis_size(axis))]
     near = [rows] + [after(part, *earlier) if earlier else part for part in near]
@@ -300,25 +314,26 @@
                 out[:, target : target + LANES] = packed[rank, :, start : start + LANES].astype(FULL)
 
 
-def pack_columns_kernel(chips, gate, up, gate_out, up_out):
-    steps, _, width = gate_out.shape
-    block = width // chips
-    for weight, out in ((gate, gate_out), (up, up_out)):
+def pack_columns_kernel(chips, gate, up, out):
+    steps, _, width = out.shape
+    block = width // (2 * chips)
+    for side, weight in enumerate((gate, up)):
         for step in range(steps):
             for chip in range(chips):
                 start = (chip * steps + step) * block
-                here = slice(chip * block, (chip + 1) * block)
-                out[step, :, here] = weight[:, start : start + block]
-
-
-def unpack_columns_kernel(chips, packed, out):
+                place = (side * chips + chip) * block
+                out[step, :, place : place + block] = weight[:, start : start + block]
+
+
+def unpack_columns_kernel(chips, packed, gate, up):
     steps, _, width = packed.shape
-    block = width // chips
-    for step in range(steps):
-        for chip in range(chips):
-            start = (chip * steps + step) * block
-            here = slice(chip * block, (chip + 1) * block)
-            out[:, start : start + block] = packed[step, :, here].astype(FULL)
+    block = width // (2 * chips)
+    for side, out in enumerate((gate, up)):
+        for step in range(steps):
+            for chip in range(chips):
+                start = (chip * steps + step) * block
+                place = (side * chips + chip) * block
+                out[:, start : start + block] = packed[step, :, place : place + block].astype(FULL)
 
 
 def join_kernel(*refs):
@@ -610,110 +625,97 @@
     ff_width = w_gate.shape[1]
     ff_block = ff_width // (ranks * shards)
     rank_width = model_width // ranks
-    groups = rank_width // LANES
+    half = seq_rows // 2
 
     steps = cores * shards
     column_width = chips * ff_block
     low_shape = lambda *shape: jax.ShapeDtypeStruct(shape, LOW)
     full_shape = lambda *shape: jax.ShapeDtypeStruct(shape, FULL)
+    flag = doc_lengths[0, 0] > 0
 
     token_low = tokens[0]
-    projections = shuffle(
+    token_rows = token_low.astype(FULL)
+    packed_heads = shuffle(
         pack_heads_kernel, [low_shape(ranks, weight_rows, 3 * rank_width)], w_query, w_key, w_value
     )[0]
     columns = shuffle(
         functools.partial(pack_columns_kernel, chips),
-        [low_shape(steps, weight_rows, column_width)] * 2,
+        [low_shape(steps, weight_rows, 2 * column_width)],
         w_gate,
         w_up,
-    )
-
-    def exchange(part):
-        part = lax.all_to_all(part, ("core", "fsdp"), 0, 0, tiled=True)
-        return part.reshape(steps * weight_rows, column_width)
-
-    w_out_rows = lax.all_gather(w_out, "fsdp", axis=0, tiled=True)
-    spread = gather_gains(norm1_gain, norm2_gain)
-    gains = [row.reshape(-1) for row in jnp.split(spread, 2, axis=1)]
-    projections = lax.all_to_all(after(projections, spread), RANKS, 0, 0, tiled=True)
-    token_parts = gather_rows(after(token_low, projections), "chip")
-    w_down_rows = lax.all_gather(after(w_down, projections), "chip", axis=0, tiled=True)
-    gate_cols = exchange(after(columns[0], projections))
-    parts = gather_line(projections, "fsdp", gate_cols)
-    gate_cols = after(gate_cols, *parts[1:3])
-    up_cols = exchange(after(columns[1], gate_cols))
-    w_up_cols = lax.all_gather(up_cols, "chip", axis=0, tiled=True)
-    near_upstream = gather_each(after(cotangent[0], up_cols), "fsdp")
-    gate_blocks = [gate_cols] + [swap_with(gate_cols, "chip", code) for code in range(1, chips)]
-    w_gate_cols = place_blocks(chip, gate_blocks)
-    parts = [after(part, up_cols, *gate_blocks[1:]) for part in parts]
-
-    w_qkv = spread_shards(shard, parts)
-    w_qkv = w_qkv.reshape(model_width, 3 * rank_width)
-
+    )[0]
     starts, cosine, sine = natural_tables(doc_lengths[0], seq_rows)
     order = jnp.arange(2 * ranks, dtype=jnp.int32)
     owner = jnp.where(order < ranks, order, 2 * ranks - 1 - order)
     slot = ((owner // cores) ^ chip) + chips * ((owner % cores) ^ core)
     offsets = slot * local_rows + jnp.where(order < ranks, 0, block_len)
 
-    seq_tokens = join_rows(token_parts)
-    normed1, seq_inverse = norm_apply(seq_tokens.astype(FULL), gains[0])
-    attn_in = after(normed1.astype(LOW), w_down_rows)
-    qkv = matmul(attn_in, w_qkv)
-    mixed, query_rows, key_rows, value_rows, lse = attention_forward(
-        offsets, qkv, cosine, sine, starts
-    )
-    mixed = after(mixed, gate_cols)
-    half = seq_rows // 2
-    far_part = matmul(mixed[half:], w_out_rows)
-    near_part = matmul(mixed[:half], w_out_rows)
-    token_rows = token_low.astype(FULL)
-    hidden1 = token_rows + scatter_rows(near_part, far_part, "chip")
-    normed2, inverse2 = norm_apply(hidden1, gains[1])
-
-    far_upstream = swap_with(after(near_upstream, hidden1), "core", 1)
-    near_in = gather_each(normed2.astype(LOW), "fsdp")
-    far_in = swap_with(near_in, "core", 1)
+    w_out_rows = lax.all_gather(w_out, "fsdp", axis=0, tiled=True)
+    spread = gather_gains(norm1_gain, norm2_gain)
+    gains = [row.reshape(-1) for row in jnp.split(spread, 2, axis=1)]
+    projections = lax.all_to_all(after(packed_heads, spread), RANKS, 0, 0, tiled=True)
+
+    projections = after(projections, w_out_rows)
+    w_down_rows = lax.all_gather(after(w_down, projections), "chip", axis=0, tiled=True)
+
+    def gather_region(projections, token_low, gain):
+        token_parts = gather_rows(token_low, "chip")
+        parts = gather_line(projections, "fsdp")
+        w_qkv = spread_shards(shard, parts).reshape(model_width, 3 * rank_width)
+        seq_tokens = join_rows(token_parts)
+        normed1, seq_inverse = norm_apply(seq_tokens.astype(FULL), gain)
+        return w_qkv, normed1.astype(LOW), seq_inverse[:local_rows]
+
+    w_qkv, attn_in, inverse1 = region(flag, gather_region, projections, token_low, gains[0])
+    w_qkv = after(w_qkv, w_down_rows)
+    columns = lax.all_to_all(after(columns, w_qkv), ("core", "fsdp"), 0, 0, tiled=True)
+    columns = columns.reshape(steps * weight_rows, 2 * column_width)
+
+    def forward_region(w_qkv, attn_in, w_out_rows, token_rows, gain):
+        qkv = matmul(attn_in, w_qkv)
+        mixed, *saved = attention_forward(offsets, qkv, cosine, sine, starts)
+        far_part = matmul(mixed[half:], w_out_rows)
+        near_part = matmul(mixed[:half], w_out_rows)
+        hidden1 = token_rows + scatter_rows(near_part, far_part, "chip")
+        normed2, inverse2 = norm_apply(hidden1, gain)
+        return mixed, saved, hidden1, normed2.astype(LOW), inverse2
+
+    mixed, saved, hidden1, normed2, inverse2 = region(
+        flag, forward_region, w_qkv, attn_in, w_out_rows, token_rows, gains[1]
+    )
+    normed2 = after(normed2, columns)
+    near_upstream = lax.all_gather(
+        after(cotangent[0], normed2), "fsdp", axis=0, tiled=True
+    )
+    w_cols = gather_each(after(columns, normed2), "chip")
+
+    def widen_region(normed2):
+        parts = [normed2] + [swap_with(normed2, "fsdp", code) for code in range(1, shards)]
+        near_in = place_blocks(shard, parts)
+        return near_in, swap_with(near_in, "core", 1)
+
+    near_in, far_in = region(flag, widen_region, normed2)
+    near_upstream = after(near_upstream, near_in)
+    far_upstream = swap_with(near_upstream, "core", 1)
     mlp_in, activation, gate_low, up_low = expand(
-        near_in, far_in, near_upstream, far_upstream, w_gate_cols, w_up_cols, w_down_rows
+        near_in, far_in, near_upstream, far_upstream, w_cols, w_down_rows
     )
     half_mlp = mlp_in.shape[0] // 2
-    upstream = jnp.concatenate([near_upstream, far_upstream], axis=0)
-    back_far = contract(gate_low, up_low, w_gate_cols, w_up_cols, 1, LOW)
-    back_near = contract(gate_low, up_low, w_gate_cols, w_up_cols, 0, FULL)
+    if chips == 4:
+        gate31, up23 = pair_products(mlp_in, gate_low, up_low, chip, chips, ((3, 1), (2, 3)))
+        gate_in, up_in = swap_with(gate31, "chip", 1), swap_with(up23, "chip", 2)
+        gate_low, up_low = after(gate_low, gate31), after(up_low, up23)
+    back_far = contract(gate_low, up_low, w_cols, 1, LOW)
+    back_near = contract(gate_low, up_low, w_cols, 0, FULL)
     back_far = swap_with(back_far, "core", 1)
     back_low = (back_near + back_far.astype(FULL)).astype(LOW)
     gate_low, up_low, activation = (
         after(low, back_low) for low in (gate_low, up_low, activation)
     )
     if chips == 4:
-        gate31, up23 = pair_products(mlp_in, gate_low, up_low, chip, chips, ((3, 1), (2, 3)))
         gate20, up10 = pair_products(mlp_in, gate_low, up_low, chip, chips, ((2, 0), (1, 0)))
-        products = [gate31, up23, gate20, up10]
-        gate_in, up_in = swap_with(gate31, "chip", 1), swap_with(up23, "chip", 2)
-        arrived = [gate_in, up_in]
-    else:
-        products = product_rows(mlp_in, [gate_low, up_low], 0, 0, 512)
-        arrived = []
-    activation = after(activation, *products[:2])
-    raw_down = product_rows(activation, [upstream], 0, 0, 256)[0]
-    down_far = product_rows(activation[half_mlp:], [w_down_rows], 1, 0, 256)[0]
-    down_near = product_rows(activation[:half_mlp], [w_down_rows], 1, 0, 256, FULL)[0]
-    down_near = down_near + swap_with(down_far, "core", 1).astype(FULL)
-    down_near = down_near.astype(LOW)
-    mlp_in_grad = scatter_each(back_low, "fsdp")
-    mlp_in_grad = after(mlp_in_grad, raw_down, down_near, *products, *arrived)
-    hidden_back, gain2_term = norm_back(hidden1, inverse2, gains[1], mlp_in_grad)
-    hidden1_grad = cotangent[0].astype(FULL) + hidden_back
-
-    def exchange_back(part):
-        part = part.reshape(steps, weight_rows, column_width)
-        return lax.all_to_all(part, ("core", "fsdp"), 0, 0, tiled=True)
-
-    if chips == 4:
-        gate_in, up_in = (after(part, hidden1_grad).astype(FULL) for part in arrived)
         rows = gate20.shape[0] // 2
+        gate_in, up_in = gate_in.astype(FULL), up_in.astype(FULL)
         gate2 = (gate20[:rows].astype(FULL) + gate_in[:rows]).astype(LOW)
         gate0 = gate20[rows:].astype(FULL) + gate_in[rows:]
         up1 = (up10[:rows].astype(FULL) + up_in[rows:]).astype(LOW)
@@ -722,71 +724,95 @@
         up_sum = (up0 + swap_with(up1, "chip", 1).astype(FULL)).astype(LOW)
     else:
         gate_sum, up_sum = (
-            lax.psum_scatter(part, "chip", scatter_dimension=0, tiled=True) for part in products
+            lax.psum_scatter(part, "chip", scatter_dimension=0, tiled=True)
+            for part in product_rows(mlp_in, [gate_low, up_low], 0, 0, 512)
         )
-    gate_packed = exchange_back(gate_sum)
-    up_packed = exchange_back(after(up_sum, gate_packed))
+    column_sum = jnp.concatenate([gate_sum, up_sum], axis=1)
+    down_far = product_rows(activation[half_mlp:], [w_down_rows], 1, 0, 256)[0]
+    down_near = product_rows(activation[:half_mlp], [w_down_rows], 1, 0, 256, FULL)[0]
+    down_near = down_near + swap_with(down_far, "core", 1).astype(FULL)
+    down_near = down_near.astype(LOW)
+    mlp_in_grad = scatter_each(back_low, "fsdp")
+    mlp_in_grad = after(mlp_in_grad, down_near, column_sum)
+    hidden_back, gain2_term = norm_back(hidden1, inverse2, gains[1], mlp_in_grad)
+    hidden1_grad = cotangent[0].astype(FULL) + hidden_back
+
+    column_sum = after(column_sum, hidden1_grad).reshape(steps, weight_rows, 2 * column_width)
+    column_sum = lax.all_to_all(column_sum, ("core", "fsdp"), 0, 0, tiled=True)
     down_parts = lax.psum_scatter(
         after(down_near, hidden1_grad), "fsdp", scatter_dimension=0, tiled=True
     )
-    layer_out = hidden1 + down_parts.astype(FULL)
-    hidden_low = gather_rows(hidden1_grad.astype(LOW), "chip")
-    hidden_low = join_rows(hidden_low)
-    down_grad = lax.psum_scatter(
-        after(raw_down, down_parts), "chip", scatter_dimension=0, tiled=True
-    ).astype(FULL)
-
-    mixed_low = matmul(hidden_low, w_out_rows, 1, 1).astype(LOW)
-    mixed_low = after(mixed_low, gate_sum, up_sum)
-    out_grad = lax.psum_scatter(
-        matmul(mixed, hidden_low, 0, 0).astype(LOW), "fsdp", scatter_dimension=0, tiled=True
-    ).astype(FULL)
-    qkv_low = attention_backward(
-        offsets, mixed_low, query_rows, key_rows, value_rows, lse, cosine, sine, starts
-    )
-    qkv_low = after(qkv_low, gate_packed)
+
+    def backward_region(low_rows, w_out_rows, saved, mixed, activation, near, far):
+        raw_down = product_halves(activation, near, far)
+        hidden_low = join_rows(gather_rows(low_rows, "chip"))
+        mixed_low = matmul(hidden_low, w_out_rows, 1, 1).astype(LOW)
+        query_rows, key_rows, value_rows, lse = saved
+        qkv_low = attention_backward(
+            offsets, mixed_low, query_rows, key_rows, value_rows, lse, cosine, sine, starts
+        )
+        raw_out = matmul(mixed, hidden_low, 0, 0).astype(LOW)
+        return raw_down, raw_out, qkv_low
+
+    raw_down, raw_out, qkv_low = region(
+        flag,
+        backward_region,
+        hidden1_grad.astype(LOW),
+        w_out_rows,
+        saved,
+        mixed,
+        activation,
+        near_upstream,
+        far_upstream,
+    )
     raw_grad = matmul(attn_in, qkv_low, 0, 0).astype(LOW)
-    qkv_grad = raw_grad.reshape(ranks, shards, weight_rows, 3 * rank_width)
-    pieces = [pick_block(qkv_grad, shard ^ code, 1) for code in range(shards)]
-    own_grad, early_grads, other_grads = scatter_line(pieces, "fsdp")
-    gate_grad, up_grad = (
-        shuffle(
-            functools.partial(unpack_columns_kernel, chips),
-            [full_shape(weight_rows, ff_width)],
-            part,
-        )[0]
-        for part in (gate_packed, up_packed)
-    )
-    qkv_low = after(qkv_low, raw_grad)
-    in_far = matmul(qkv_low[half:], w_qkv, 1, 1)
-    in_near = matmul(after(qkv_low[:half], up_packed, *early_grads), w_qkv, 1, 1)
-    in_grad = scatter_rows(in_near, in_far, "chip")
-    token_back, gain1_term = norm_back(
-        token_rows, seq_inverse[:local_rows], gains[0], in_grad
-    )
-    gain_grads = jnp.stack([gain1_term, gain2_term])
-    for axis in RANKS:
-        gain_grads = total_over(gain_grads, axis)
-    gain_grads = total_over(after(gain_grads, *other_grads), "fsdp")
+    qkv_low = after(qkv_low, raw_grad, column_sum, down_parts)
+    qkv_grad = raw_grad.reshape(ranks, shards, weight_rows, 3 * rank_width).transpose(1, 0, 2, 3)
+    qkv_grad = lax.all_to_all(after(qkv_grad, column_sum), "fsdp", 0, 0, tiled=True)
+    raw_down = after(raw_down, qkv_low)
+    down_grad = lax.psum_scatter(raw_down, "chip", scatter_dimension=0, tiled=True)
+
+    def finish_region(qkv_low, w_qkv, token_rows, inverse1, gain, gain2_term):
+        in_far = matmul(qkv_low[half:], w_qkv, 1, 1)
+        in_near = matmul(qkv_low[:half], w_qkv, 1, 1)
+        in_grad = scatter_rows(in_near, in_far, "chip")
+        token_back, gain1_term = norm_back(token_rows, inverse1, gain, in_grad)
+        gain_grads = jnp.stack([gain1_term, gain2_term])
+        for axis in EVERY:
+            gain_grads = total_over(gain_grads, axis)
+        return token_back, gain_grads
+
+    token_back, gain_grads = region(
+        flag, finish_region, qkv_low, w_qkv, token_rows, inverse1, gains[0], gain2_term
+    )
+    raw_out = after(raw_out, down_grad, gain_grads)
+    out_grad = lax.psum_scatter(raw_out, "fsdp", scatter_dimension=0, tiled=True)
     gain_grads = lax.dynamic_slice_in_dim(
         gain_grads, ((chip * cores + core) * shards + shard) * weight_rows, weight_rows, 1
     )
-    qkv_grad = lax.all_to_all(after(own_grad.astype(LOW), gain_grads), RANKS, 0, 0, tiled=True)
+    own_grad = jnp.sum(qkv_grad.astype(FULL).reshape(shards, ranks, weight_rows, -1), axis=0)
+    own_grad = after(own_grad.astype(LOW), gain_grads)
+    qkv_grad = lax.all_to_all(own_grad, RANKS, 0, 0, tiled=True)
     qkv_grads = shuffle(
         unpack_heads_kernel, [full_shape(weight_rows, model_width)] * 3, qkv_grad
     )
-
+    gate_grad, up_grad = shuffle(
+        functools.partial(unpack_columns_kernel, chips),
+        [full_shape(weight_rows, ff_width)] * 2,
+        column_sum,
+    )
+    layer_out = hidden1 + down_parts.astype(FULL)
     token_grad = hidden1_grad + token_back
     return (
         layer_out.astype(LOW)[None],
         token_grad[None],
         gain_grads[0],
         *qkv_grads,
-        out_grad,
+        out_grad.astype(FULL),
         gain_grads[1],
         gate_grad,
         up_grad,
-        down_grad,
+        down_grad.astype(FULL),
     )
 
 

time: 703 us -> 636 us (0.905)
  starting transfers between devices: 113 us -> 73.1 us
  waiting for transfers between devices: 309 us -> 289 us
  local copies, waits for them, and re-layouts: 41.8 us -> 28.4 us
  Pallas kernels: 108 us -> 117 us
    ppermute x42 -> x40, waiting for transfers between devices: 158 us -> 221 us  [swap_with(): return lax.ppermute(value, axis, [(i, i ^ code) for i in range(count)])]
    all_to_all x2 -> x1, waiting for transfers between devices: 51.9 us -> 3.46 us  [gather_each(): copies = lax.all_to_all(copies, axis, 0, 0, tiled=True)]
    ppermute x4 -> x2, waiting for transfers between devices: 46.5 us -> 11 us  [permute(): return lax.ppermute(value, axis, pairs)]
    unnamed x100 -> x50, local copies, waits for them, and re-layouts: 29.5 us -> 5.85 us
    ppermute x4 -> x2, starting transfers between devices: 25 us -> 1.99 us  [permute(): return lax.ppermute(value, axis, pairs)]
    all_to_all x5 -> x4, waiting for transfers between devices: 47.3 us -> 25.5 us  [the longest x1 15.8 us: local(): column_sum = lax.all_to_all(column_sum, ('core', 'fsdp'), 0, 0, tiled=True)]
    all_gather x1, waiting for transfers between devices: 0.01 us -> 17 us  [local(): lax.all_gather(after(cotangent[0], normed2), 'fsdp', axis=0, tiled=True)]
    ppermute x42 -> x40, starting transfers between devices: 42.6 us -> 31.1 us  [swap_with(): return lax.ppermute(value, axis, [(i, i ^ code) for i in range(count)])]
  transfers between devices with their start and end apart: 61 -> 55, of which waited for: 28 -> 35; matrix products, arithmetic and copies ran while one was open for 13% -> 15% of each run, Pallas kernels for 11% -> 12%
where the time goes in v2:
time: 636 us; the launch traced here: 630 us
  waiting for transfers between devices  289 us (45%)
  Pallas kernels  117 us (18%)
  starting transfers between devices  73.1 us (11%)
  other arithmetic  60.3 us (9%)
  matrix products  30.3 us (5%)
  local copies, waits for them, and re-layouts  28.4 us (4%)
  blocking collectives  15.6 us (2%)
  between operations  14.9 us (2%)
    ppermute x40, waiting for transfers between devices, swap_with(): return lax.ppermute(value, axis, [(i, i ^ code) for i in range(count)])  221 us
    ppermute x40, starting transfers between devices, swap_with(): return lax.ppermute(value, axis, [(i, i ^ code) for i in range(count)])  31.1 us
    dot_general x8, matrix products, matmul(): lax.dot_general(left, right, (((left_dim,), (right_dim,)), ((), ())), pre...  30.3 us
    pallas_call x1, Pallas kernels, expand(): pl.pallas_call(expand_kernel, grid=(hidden // tile,), in_specs=[once] * 4...  20.4 us
    pallas_call x2, Pallas kernels, pair_products(): pl.pallas_call(pair_kernel, grid_spec=pltpu.PrefetchScalarGridSpec(num_sc...  18.7 us
    pallas_call x2, Pallas kernels, contract(): pl.pallas_call(contract_kernel, grid=(width // tile,), in_specs=[rows, ro...  18 us
    all_gather x1, waiting for transfers between devices, local(): lax.all_gather(after(cotangent[0], normed2), 'fsdp', axis=0, tiled=True)  17 us
    all_to_all x1, waiting for transfers between devices, local(): column_sum = lax.all_to_all(column_sum, ('core', 'fsdp'), 0, 0, tiled=True)  15.8 us
  transfers between devices with their start and end apart: 55, of which 35 were waited for; matrix products, arithmetic and copies ran while one was open for 15% of the time, Pallas kernels for 12%

profile of v2, /device:TPU:0, one launch (start us, length us, event | category | flops | bytes accessed | tf_op | source)
XLA Modules:
  0.0 629.8 jit_solution(14939337633018607718)
XLA Ops:
  9.3 7.3 %all-to-all-start = ((f32[32,1,128]{2,1,0:T(1,128)}), f32[32,1,128]{2,1,0:T(1,128)S(1)}, u32[]{:S(2)}, u32[]{:S(2)}) async-start(f32[32,1,128]{2,1,0:T(1,128)} %broadcast_in_dim.15), calls=%async_computation | async-start | bytes 32768 | tf_op jit(solution)/shard_map/all_to_all | solution.py:294
  19.8 3.9 all-to-all-done
  23.7 15.6 %all_to_all.44 = bf16[8,64,768]{2,1,0:T(8,128)(2,1)} all-to-all(bf16[8,64,768]{2,1,0:T(8,128)(2,1)S(1)} %shard_map.221), channel_id=1, replica_groups=mesh['chip'=4,'core'=2,'fsdp'=4] {'chip','core'}, dimensions={0} | all-to-all | bytes 1572864 | tf_op jit(solution)/shard_map/all_to_all | solution.py:656
  42.0 63.2 %conditional.5 = (bf16[2048,768]{1,0:T(8,128)(2,1)}, bf16[1024,2048]{1,0:T(8,128)(2,1)}, f32[128,1]{0,1:T(1,128)S(1)}) conditional(s32[]{:T(128)} %bitcast.10, () %tuple.73, (s32[]{:T(128)}, bf16[8,64,768]{2,1,0:T(8,128)(2,1)}, bf16[128,2048]{1,0:T(8,128)(2,1)}, f32[32,64]{1,0:T(8,128)S(1)}) %tuple.76), branch_computations={%region_0.0_spmd, %region_1.3_spmd} | conditional | flops 15074309 | bytes 42247672 | solution.py:195
  47.9 17.1 %collective-permute-done.8.refs_1_ = bf16[128,2048]{1,0:T(8,128)(2,1)S(1)} collective-permute-done((bf16[128,2048]{1,0:T(8,128)(2,1)}, bf16[128,2048]{1,0:T(8,128)(2,1)S(1)}, u32[]{:S(2)}, u32[]{:S(2)}) %collective-permute-start.8) | collective-permute-done | bytes 524320 | tf_op jit(solution)/shard_map/cond/branch_1_fun/ppermute | solution.py:200
  65.0 4.5 collective-permute-done.9.refs_2_
  69.5 10.7 %collective-permute-done.10.refs_3_ = bf16[128,2048]{1,0:T(8,128)(2,1)S(1)} collective-permute-done((bf16[128,2048]{1,0:T(8,128)(2,1)}, bf16[128,2048]{1,0:T(8,128)(2,1)S(1)}, u32[]{:S(2)}, u32[]{:S(2)}) %collective-permute-start.10) | collective-permute-done | bytes 524320 | tf_op jit(solution)/shard_map/cond/branch_1_fun/ppermute | solution.py:200
  88.0 3.1 fusion.2
  91.1 11.0 %collective-permute-done.7 = bf16[8,64,768]{2,1,0:T(8,128)(2,1)S(1)} collective-permute-done((bf16[8,64,768]{2,1,0:T(8,128)(2,1)S(1)}, bf16[8,64,768]{2,1,0:T(8,128)(2,1)S(1)}, u32[]{:S(2)}, u32[]{:S(2)}) %collective-permute-start.7) | collective-permute-done | bytes 786464 | tf_op jit(solution)/shard_map/cond/branch_1_fun/ppermute | solution.py:204
  102.2 3.0 branch_1_fun.7
  105.2 4.5 all-gather.6.cloned.1.call-done.down_rows.refs_0_
  109.7 4.6 all-to-all-start.2
  118.4 59.3 %conditional.6 = (bf16[1024,256]{1,0:T(8,128)(2,1)}, bf16[1024,256]{1,0:T(8,128)(2,1)}, bf16[1024,256]{1,0:T(8,128)(2,1)}, bf16[1024,256]{1,0:T(8,128)(2,1)}, f3...) conditional(s32[]{:T(128)} %bitcast.10, () %tuple.72, ...), branch_computations={%region_5.6_spmd, %region_6.8_spmd} | conditional | flops 4302569984 | bytes 57700128 | solution.py:195
  120.1 6.1 fusion.36.qkv
  126.3 9.4 %branch_1_fun.9 = (bf16[1024,256]{1,0:T(8,128)(2,1)}, bf16[1024,256]{1,0:T(8,128)(2,1)}, bf16[1024,256]{1,0:T(8,128)(2,1)}, bf16[1024,256]{1,0:T(8,128)(2,1)}, f32[2,8,1024]{2,1,0:T(8,128)S(1)}) custom-call(s32[16]{0:T(128)S(1)} %get-tuple-element.84.offsets, f32[1024,768]{1,0:T(8,128)S(1)} %fusion.36.qkv, f32[1024,128]{1,0:T(8,128)S(1)} %copy.30.cosine, ...), custom_call_target="tpu_custom_call" | custom-call | tf_op jit(solution)/shard_map/cond/branch_1_fun/pallas_call | solution.py:551
  138.0 3.8 collective-permute-done.15
  149.5 12.3 %collective-permute-done.18 = bf16[128,2048]{1,0:T(8,128)(2,1)S(1)} collective-permute-done((bf16[128,2048]{1,0:T(8,128)(2,1)}, bf16[128,2048]{1,0:T(8,128)(2,1)S(1)}, u32[]{:S(2)}, u32[]{:S(2)}) %collective-permute-start.18) | collective-permute-done | bytes 524320 | tf_op jit(solution)/shard_map/cond/branch_1_fun/ppermute | solution.py:200
  161.8 10.6 %collective-permute-done.17 = bf16[128,2048]{1,0:T(8,128)(2,1)S(1)} collective-permute-done((bf16[128,2048]{1,0:T(8,128)(2,1)}, bf16[128,2048]{1,0:T(8,128)(2,1)S(1)}, u32[]{:S(2)}, u32[]{:S(2)}) %collective-permute-start.17) | collective-permute-done | bytes 524320 | tf_op jit(solution)/shard_map/cond/branch_1_fun/ppermute | solution.py:200
  172.6 2.9 multiply_reduce_fusion
  177.8 4.4 broadcast_in_dim.18
  182.1 5.7 all-to-all-start.3
  188.6 67.1 %conditional.7 = (bf16[512,2048]{1,0:T(8,128)(2,1)}, bf16[512,2048]{1,0:T(8,128)(2,1)}) conditional(s32[]{:T(128)} %bitcast.10, () %tuple.80, (s32[]{:T(128)}, bf16[128,2048]{1,0:T(8,128)(2,1)}) %tuple.83), branch_computations={%region_8.9_spmd, %region_9.10_spmd} | conditional | bytes 14680240 | solution.py:195
  193.1 34.4 %collective-permute-done.refs_1_ = bf16[128,2048]{1,0:T(8,128)(2,1)S(1)} collective-permute-done((bf16[128,2048]{1,0:T(8,128)(2,1)}, bf16[128,2048]{1,0:T(8,128)(2,1)S(1)}, u32[]{:S(2)}, u32[]{:S(2)}) %collective-permute-start) | collective-permute-done | bytes 524320 | tf_op jit(solution)/shard_map/cond/branch_1_fun/ppermute | solution.py:200
  228.2 20.1 %collective-permute-done.2.refs_3_ = bf16[128,2048]{1,0:T(8,128)(2,1)S(1)} collective-permute-done((bf16[128,2048]{1,0:T(8,128)(2,1)}, bf16[128,2048]{1,0:T(8,128)(2,1)S(1)}, u32[]{:S(2)}, u32[]{:S(2)}) %collective-permute-start.2) | collective-permute-done | bytes 524320 | tf_op jit(solution)/shard_map/cond/branch_1_fun/ppermute | solution.py:200
  250.8 4.5 collective-permute-done.3
  255.8 17.0 %all-gather.8.cloned.1.call-done.near = bf16[512,2048]{1,0:T(8,128)(2,1)} async-done(((bf16[128,2048]{1,0:T(8,128)(2,1)}), bf16[512,2048]{1,0:T(8,128)(2,1)}) %all-gather.8.cloned.1.call-update) | async-done | bytes 2097168 | tf_op jit(solution)/shard_map/all_gather | solution.py:687
  273.4 3.7 collective-permute-done.35.far
  277.2 3.5 all-to-all-done.3
  280.6 20.4 %shard_map.223 = (bf16[1024,2048]{1,0:T(8,128)(2,1)}, bf16[1024,1024]{1,0:T(8,128)(2,1)}, bf16[1024,1024]{1,0:T(8,128)(2,1)}, bf16[1024,1024]{1,0:T(8,128)(2,1)}) custom-call(bf16[512,2048]{1,0:T(8,128)(2,1)} %get-tuple-element.196.near_in, bf16[512,2048]{1,0:T(8,128)(2,1)} %get-tuple-element.197.far_in, ...), custom_call_target="tpu_custom_call" | custom-call | tf_op jit(solution)/shard_map/pallas_call | solution.py:126
  301.0 9.3 %shard_map.224 = (bf16[1024,1024]{1,0:T(8,128)(2,1)}, bf16[1024,1024]{1,0:T(8,128)(2,1)}) custom-call(s32[4]{0:T(128)} %get-tuple-element.287.order, bf16[1024,2048]{1,0:T(8,128)(2,1)} %get-tuple-element.203.left.right, bf16[1024,2048]{1,0:T(8,128)(2,1)} %get-tuple-element.203.left.right, bf16[1024,1024]{1,0:T(8,128)(2,1)} %get-tuple-element.211.gate_low.left, ...), custom_call_target="tpu_custom_call" | custom-call | tf_op jit(solution)/shard_map/pallas_call | solution.py:150
  310.3 8.8 %shard_map.226 = bf16[512,2048]{1,0:T(8,128)(2,1)} custom-call(bf16[1024,1024]{1,0:T(8,128)(2,1)} %get-tuple-element.211.gate_low.left, bf16[1024,1024]{1,0:T(8,128)(2,1)} %get-tuple-element.212.up_low.right, bf16[2048,2048]{1,0:T(8,128)(2,1)} %bitcast.19.gate_cols.up_cols.cols), custom_call_target="tpu_custom_call" | custom-call | tf_op jit(solution)/shard_map/pallas_call | solution.py:179
  321.1 9.3 %shard_map.225 = f32[512,2048]{1,0:T(8,128)} custom-call(bf16[1024,1024]{1,0:T(8,128)(2,1)} %get-tuple-element.211.gate_low.left, bf16[1024,1024]{1,0:T(8,128)(2,1)} %get-tuple-element.212.up_low.right, bf16[2048,2048]{1,0:T(8,128)(2,1)} %bitcast.19.gate_cols.up_cols.cols), custom_call_target="tpu_custom_call" | custom-call | tf_op jit(solution)/shard_map/pallas_call | solution.py:179
  330.4 4.3 add_convert_fusion.3
  334.6 7.3 %all-to-all-start.4 = ((bf16[4,128,2048]{2,1,0:T(8,128)(2,1)}), bf16[4,128,2048]{2,1,0:T(8,128)(2,1)}, u32[]{:S(2)}, u32[]{:S(2)}) async-start(bf16[4,128,2048]{2,1,0:T(8,128)(2,1)} %bitcast.63), calls=%async_computation.4 | async-start | bytes 4194304 | tf_op jit(solution)/shard_map/all_to_all | solution.py:286
  343.7 5.8 shard_map.228
  349.5 9.3 %shard_map.229 = (bf16[1024,1024]{1,0:T(8,128)(2,1)}, bf16[1024,1024]{1,0:T(8,128)(2,1)}) custom-call(s32[4]{0:T(128)} %get-tuple-element.286.order, bf16[1024,2048]{1,0:T(8,128)(2,1)} %get-tuple-element.203.left.right, bf16[1024,2048]{1,0:T(8,128)(2,1)} %get-tuple-element.203.left.right, bf16[1024,1024]{1,0:T(8,128)(2,1)} %get-tuple-element.211.gate_low.left, ...), custom_call_target="tpu_custom_call" | custom-call | tf_op jit(solution)/shard_map/pallas_call | solution.py:150
  358.9 8.6 %collective-permute-done.40 = bf16[1024,1024]{1,0:T(8,128)(2,1)} collective-permute-done((bf16[1024,1024]{1,0:T(8,128)(2,1)}, bf16[1024,1024]{1,0:T(8,128)(2,1)}, u32[]{:S(2)}, u32[]{:S(2)}) %collective-permute-start.40) | collective-permute-done | bytes 2097184 | tf_op jit(solution)/shard_map/ppermute | solution.py:200
  378.3 6.3 %shard_map.227 = f32[512,2048]{1,0:T(8,128)} custom-call(bf16[512,1024]{1,0:T(8,128)(2,1)} %get-tuple-element.278.left, bf16[1024,2048]{1,0:T(8,128)(2,1)} %all-gather.6.cloned.1.call-done.down_rows.refs_0_), custom_call_target="tpu_custom_call" | custom-call | tf_op jit(solution)/shard_map/pallas_call | solution.py:62
  384.6 12.2 %collective-permute-done.41 = bf16[512,1024]{1,0:T(8,128)(2,1)S(1)} collective-permute-done((bf16[512,1024]{1,0:T(8,128)(2,1)}, bf16[512,1024]{1,0:T(8,128)(2,1)S(1)}, u32[]{:S(2)}, u32[]{:S(2)}) %collective-permute-start.41) | collective-permute-done | bytes 1048608 | tf_op jit(solution)/shard_map/ppermute | solution.py:200
  398.6 3.8 collective-permute-done.39
  407.1 3.7 add_convert_fusion.2
  414.9 2.8 fusion.31
  417.7 6.1 all-to-all-start.5
  423.9 58.6 %conditional.8 = (bf16[1024,2048]{1,0:T(8,128)(2,1)}, bf16[256,2048]{0,1:T(8,128)(2,1)}, bf16[1024,768]{1,0:T(8,128)(2,1)}) conditional(s32[]{:T(128)} %bitcast.10, () %tuple.95, (bf16[1024,1024]{1,0:T(8,128)(2,1)}, bf16[512,2048]{1,0:T(8,128)(2,1)}, bf16[512,2048]{1,0:T(8,128)(2,1)}, bf16[128,2048]{1,0:T(8,128)(2,1)}, ...), branch_computations={%region_13.14_spmd, %region_14.15_spmd} | conditional | flops 2148270080 | bytes 32506188 | solution.py:195
  427.7 11.5 %collective-permute-done.19.refs_1_ = bf16[128,2048]{1,0:T(8,128)(2,1)} collective-permute-done((bf16[128,2048]{1,0:T(8,128)(2,1)}, bf16[128,2048]{1,0:T(8,128)(2,1)}, u32[]{:S(2)}, u32[]{:S(2)}) %collective-permute-start.19) | collective-permute-done | bytes 524320 | tf_op jit(solution)/shard_map/cond/branch_1_fun/ppermute | solution.py:200
  439.3 10.2 %collective-permute-done.20.refs_2_ = bf16[128,2048]{1,0:T(8,128)(2,1)} collective-permute-done((bf16[128,2048]{1,0:T(8,128)(2,1)}, bf16[128,2048]{1,0:T(8,128)(2,1)}, u32[]{:S(2)}, u32[]{:S(2)}) %collective-permute-start.20) | collective-permute-done | bytes 524320 | tf_op jit(solution)/shard_map/cond/branch_1_fun/ppermute | solution.py:200
  452.4 8.7 %branch_1_fun.11 = bf16[1024,2048]{1,0:T(8,128)(2,1)} custom-call(bf16[1024,1024]{1,0:T(8,128)(2,1)} %get-tuple-element.100.left, bf16[512,2048]{1,0:T(8,128)(2,1)} %get-tuple-element.101.near, bf16[512,2048]{1,0:T(8,128)(2,1)} %get-tuple-element.102.far), custom_call_target="tpu_custom_call" | custom-call | tf_op jit(solution)/shard_map/cond/branch_1_fun/pallas_call | solution.py:83
  463.6 3.5 fusion.9
  468.4 13.9 %branch_1_fun.13 = bf16[1024,768]{1,0:T(8,128)(2,1)} custom-call(s32[16]{0:T(128)S(1)} %get-tuple-element.105.offsets, bf16[1024,256]{1,0:T(8,128)(2,1)S(1)} %convolution_convert_fusion.2.upstream, bf16[1024,256]{1,0:T(8,128)(2,1)} %get-tuple-element.107.query_in, bf16[1024,256]{1,0:T(8,128)(2,1)} %get-tuple-element.108.key_in, ...), custom_call_target="tpu_custom_call" | custom-call | tf_op jit(solution)/shard_map/cond/branch_1_fun/pallas_call | solution.py:579
  482.6 7.9 %convolution_convert_fusion.4 = bf16[2048,768]{1,0:T(8,128)(2,1)} fusion(bf16[1024,2048]{1,0:T(8,128)(2,1)} %get-tuple-element.188, bf16[1024,768]{1,0:T(8,128)(2,1)} %get-tuple-element.225), kind=kOutput, calls=%fused_computation.39 | convolution fusion | flops 3222798336 | bytes 8912896 | tf_op jit(solution)/shard_map/dot_general | solution.py:41
  490.5 15.8 %all-to-all-done.5.packed = bf16[8,64,2048]{2,1,0:T(8,128)(2,1)S(1)} async-done(((bf16[8,64,2048]{2,1,0:T(8,128)(2,1)}), bf16[8,64,2048]{2,1,0:T(8,128)(2,1)S(1)}, u32[]{:S(2)}, u32[]{:S(2)}) %all-to-all-start.5) | async-done | bytes 2097184 | tf_op jit(solution)/shard_map/all_to_all | solution.py:741
  506.3 3.9 copy.37
  510.2 5.0 all-to-all-start.6
  516.4 75.1 %conditional.9 = (f32[128,2048]{1,0:T(8,128)}, f32[2,2048]{1,0:T(2,128)S(1)}) conditional(s32[]{:T(128)} %bitcast.10, () %tuple.94, (f32[128,1]{0,1:T(1,128)S(1)}, bf16[1024,768]{1,0:T(8,128)(2,1)}, bf16[2048,768]{1,0:T(8,128)(2,1)}, f32[32,64]{1,0:T(8,128)S(1)}, f32[128,2048]{1,0:T(8,128)}, /*index=5*/f32[128,2048]{1,0:T(8,128)S(1)}, ...), branch_computations={%region_15.16_spmd, %region_16.20_spmd} | conditional | flops 3232792832 | bytes 59921328 | solution.py:195
  516.4 4.0 convolution_convert_fusion.3
  520.5 4.1 collective-permute-done.26
  524.6 4.1 add_convert_fusion.1
  536.7 13.4 %collective-permute-done.29 = bf16[128,2048]{1,0:T(8,128)(2,1)} collective-permute-done((bf16[128,2048]{1,0:T(8,128)(2,1)}, bf16[128,2048]{1,0:T(8,128)(2,1)}, u32[]{:S(2)}, u32[]{:S(2)}) %collective-permute-start.29) | collective-permute-done | bytes 524320 | tf_op jit(solution)/shard_map/cond/branch_1_fun/ppermute | solution.py:200
  550.1 10.0 %collective-permute-done.28 = bf16[128,2048]{1,0:T(8,128)(2,1)} collective-permute-done((bf16[128,2048]{1,0:T(8,128)(2,1)}, bf16[128,2048]{1,0:T(8,128)(2,1)}, u32[]{:S(2)}, u32[]{:S(2)}) %collective-permute-start.28) | collective-permute-done | bytes 524320 | tf_op jit(solution)/shard_map/cond/branch_1_fun/ppermute | solution.py:200
  573.4 13.3 %collective-permute-done.33 = f32[2,2048]{1,0:T(2,128)S(1)} collective-permute-done((f32[2,2048]{1,0:T(2,128)S(1)}, f32[2,2048]{1,0:T(2,128)S(1)}, u32[]{:S(2)}, u32[]{:S(2)}) %collective-permute-start.33) | collective-permute-done | bytes 16416 | tf_op jit(solution)/shard_map/cond/branch_1_fun/ppermute | solution.py:200
  586.9 3.1 multiply_subtract_fusion
  598.2 3.6 reduce_sum.88
  601.8 3.5 all-to-all-start.7
  608.2 9.7 %all-to-all-done.7.packed = bf16[8,64,768]{2,1,0:T(8,128)(2,1)S(1)} async-done(((bf16[8,64,768]{2,1,0:T(8,128)(2,1)}), bf16[8,64,768]{2,1,0:T(8,128)(2,1)S(1)}, u32[]{:S(2)}, u32[]{:S(2)}) %all-to-all-start.7) | async-done | bytes 786464 | tf_op jit(solution)/shard_map/all_to_all | solution.py:795
  (214 shorter events, 121.9 us)
Async XLA Ops:
  7.2 33.1 %all-gather.4.cloned.1.call-start = ((), (), s32[]{:S(2)}) async-start(), calls=%async_computation.11 | async-start | bytes 1310720 | tf_op jit(solution)/shard_map/all_gather | solution.py:653
  9.3 14.4 %all-to-all-start = ((f32[32,1,128]{2,1,0:T(1,128)}), f32[32,1,128]{2,1,0:T(1,128)S(1)}, u32[]{:S(2)}, u32[]{:S(2)}) async-start(f32[32,1,128]{2,1,0:T(1,128)} %broadcast_in_dim.15), calls=%async_computation | async-start | bytes 32768 | tf_op jit(solution)/shard_map/all_to_all | solution.py:294
  16.6 23.7 %copy-start = (bf16[64,8192]{1,0:T(8,128)(2,1)S(1)}, bf16[64,8192]{1,0:T(8,128)(2,1)}, u32[]{:S(2)}) copy-start(bf16[64,8192]{1,0:T(8,128)(2,1)} %gate.1) | copy-start | bytes 3145732
  16.6 23.7 %copy-start.1 = (bf16[64,8192]{1,0:T(8,128)(2,1)S(1)}, bf16[64,8192]{1,0:T(8,128)(2,1)}, u32[]{:S(2)}) copy-start(bf16[64,8192]{1,0:T(8,128)(2,1)} %up.1) | copy-start | bytes 3145732
  16.6 93.1 %all-gather.6.cloned.1.call-start = ((), (), s32[]{:S(2)}) async-start(), calls=%async_computation.12 | async-start | bytes 5242880 | tf_op jit(solution)/shard_map/all_gather | solution.py:659
  19.7 20.6 %copy-start.29 = (s32[1,4]{1,0:T(1,128)S(1)}, s32[1,4]{1,0:T(1,128)}, u32[]{:S(2)}) copy-start(s32[1,4]{1,0:T(1,128)} %param.25) | copy-start | bytes 52
  42.0 38.3 %collective-permute-start.4 = (bf16[8,64,768]{2,1,0:T(8,128)(2,1)}, bf16[8,64,768]{2,1,0:T(8,128)(2,1)S(1)}, u32[]{:S(2)}, u32[]{:S(2)}) collective-permute-start(bf16[8,64,768]{2,1,0:T(8,128)(2,1)} %get-tuple-element.81.refs_0_), channel_id=1, source_target_pairs={{0,1},{1,0},{2,3},{3,2},{4,5},{5,4},{6,7},{7,6},{8,9},{9,8},{10,11... | collective-permute-start | bytes 2359304 | tf_op jit(solution)/shard_map/cond/branch_1_fun/ppermute | solution.py:200
  43.4 21.6 %collective-permute-start.8 = (bf16[128,2048]{1,0:T(8,128)(2,1)}, bf16[128,2048]{1,0:T(8,128)(2,1)S(1)}, u32[]{:S(2)}, u32[]{:S(2)}) collective-permute-start(bf16[128,2048]{1,0:T(8,128)(2,1)} %get-tuple-element.82.refs_0_), channel_id=1, source_target_pairs={{0,8},{8,0},{16,24},{24,16},{1,9},{9,1},{17,25},{25,17},{2,10},{10... | collective-permute-start | bytes 1572872 | tf_op jit(solution)/shard_map/cond/branch_1_fun/ppermute | solution.py:200
  44.9 24.7 %collective-permute-start.9 = (bf16[128,2048]{1,0:T(8,128)(2,1)}, bf16[128,2048]{1,0:T(8,128)(2,1)S(1)}, u32[]{:S(2)}, u32[]{:S(2)}) collective-permute-start(bf16[128,2048]{1,0:T(8,128)(2,1)} %get-tuple-element.82.refs_0_), channel_id=1, source_target_pairs={{0,16},{8,24},{16,0},{24,8},{1,17},{9,25},{17,1},{25,9},{2,18},{10... | collective-permute-start | bytes 1572872 | tf_op jit(solution)/shard_map/cond/branch_1_fun/ppermute | solution.py:200
  46.3 33.9 %collective-permute-start.10 = (bf16[128,2048]{1,0:T(8,128)(2,1)}, bf16[128,2048]{1,0:T(8,128)(2,1)S(1)}, u32[]{:S(2)}, u32[]{:S(2)}) collective-permute-start(bf16[128,2048]{1,0:T(8,128)(2,1)} %get-tuple-element.82.refs_0_), channel_id=1, source_target_pairs={{0,24},{8,16},{16,8},{24,0},{1,25},{9,17},{17,9},{25,1},{2,26},{10... | collective-permute-start | bytes 1572872 | tf_op jit(solution)/shard_map/cond/branch_1_fun/ppermute | solution.py:200
  46.9 35.9 %collective-permute-start.5 = (bf16[8,64,768]{2,1,0:T(8,128)(2,1)}, bf16[8,64,768]{2,1,0:T(8,128)(2,1)S(1)}, u32[]{:S(2)}, u32[]{:S(2)}) collective-permute-start(bf16[8,64,768]{2,1,0:T(8,128)(2,1)} %get-tuple-element.81.refs_0_), channel_id=1, source_target_pairs={{0,2},{1,3},{2,0},{3,1},{4,6},{5,7},{6,4},{7,5},{8,10},{9,11},{10,... | collective-permute-start | bytes 2359304 | tf_op jit(solution)/shard_map/cond/branch_1_fun/ppermute | solution.py:200
  65.0 19.2 %collective-permute-start.11 = (bf16[128,2048]{1,0:T(8,128)(2,1)}, bf16[128,2048]{1,0:T(8,128)(2,1)}, u32[]{:S(2)}, u32[]{:S(2)}) collective-permute-start(bf16[128,2048]{1,0:T(8,128)(2,1)} %get-tuple-element.82.refs_0_), channel_id=1, source_target_pairs={{0,4},{4,0},{1,5},{5,1},{2,6},{6,2},{3,7},{7,3},{8,12},{12,8},{9,1... | collective-permute-start | bytes 1572872 | tf_op jit(solution)/shard_map/cond/branch_1_fun/ppermute | solution.py:200
  69.5 15.3 %collective-permute-start.12 = (bf16[128,2048]{1,0:T(8,128)(2,1)S(1)}, bf16[128,2048]{1,0:T(8,128)(2,1)}, u32[]{:S(2)}, u32[]{:S(2)}) collective-permute-start(bf16[128,2048]{1,0:T(8,128)(2,1)S(1)} %collective-permute-done.8.refs_1_), channel_id=1, source_target_pairs={{0,4},{4,0},{1,5},{5,1},{2,6},{6,2},{3,7},{7,3},{8,12},{12,8},{9,1... | collective-permute-start | bytes 1572872 | tf_op jit(solution)/shard_map/cond/branch_1_fun/ppermute | solution.py:200
  80.2 4.7 collective-permute-start.13
  80.2 4.7 collective-permute-start.14
  82.8 19.3 %collective-permute-start.7 = (bf16[8,64,768]{2,1,0:T(8,128)(2,1)S(1)}, bf16[8,64,768]{2,1,0:T(8,128)(2,1)S(1)}, u32[]{:S(2)}, u32[]{:S(2)}) collective-permute-start(bf16[8,64,768]{2,1,0:T(8,128)(2,1)S(1)} %collective-permute-done.5.refs_2_), channel_id=1, source_target_pairs={{2,3},{1,0},{6,7},{5,4},{10,11},{9,8},{14,15},{13,12},{18,19},{17,... | collective-permute-start | bytes 2359304 | tf_op jit(solution)/shard_map/cond/branch_1_fun/ppermute | solution.py:204
  84.1 7.0 %collective-permute-start.6 = (bf16[8,64,768]{2,1,0:T(8,128)(2,1)}, bf16[8,64,768]{2,1,0:T(8,128)(2,1)S(1)}, u32[]{:S(2)}, u32[]{:S(2)}) collective-permute-start(bf16[8,64,768]{2,1,0:T(8,128)(2,1)} %get-tuple-element.81.refs_0_), channel_id=1, source_target_pairs={{1,2},{2,1},{5,6},{6,5},{9,10},{10,9},{13,14},{14,13},{17,18},{18,... | collective-permute-start | bytes 2359304 | tf_op jit(solution)/shard_map/cond/branch_1_fun/ppermute | solution.py:204
  109.7 68.0 %all-to-all-start.2 = ((bf16[8,64,2048]{2,1,0:T(8,128)(2,1)}), bf16[8,64,2048]{2,1,0:T(8,128)(2,1)S(1)}, u32[]{:S(2)}, u32[]{:S(2)}) async-start(bf16[8,64,2048]{2,1,0:T(8,128)(2,1)} %shard_map.222), calls=%async_computation.2 | async-start | bytes 4194304 | tf_op jit(solution)/shard_map/all_to_all | solution.py:671
  137.4 4.4 collective-permute-start.15
  145.9 15.9 %collective-permute-start.18 = (bf16[128,2048]{1,0:T(8,128)(2,1)}, bf16[128,2048]{1,0:T(8,128)(2,1)S(1)}, u32[]{:S(2)}, u32[]{:S(2)}) collective-permute-start(bf16[128,2048]{1,0:T(8,128)(2,1)} %get-tuple-element.275), channel_id=1, source_target_pairs={{0,24},{8,16},{16,8},{24,0},{1,25},{9,17},{17,9},{25,1},{2,26},{10... | collective-permute-start | bytes 1572872 | tf_op jit(solution)/shard_map/cond/branch_1_fun/ppermute | solution.py:200
  147.4 25.1 %collective-permute-start.17 = (bf16[128,2048]{1,0:T(8,128)(2,1)}, bf16[128,2048]{1,0:T(8,128)(2,1)S(1)}, u32[]{:S(2)}, u32[]{:S(2)}) collective-permute-start(bf16[128,2048]{1,0:T(8,128)(2,1)} %get-tuple-element.276), channel_id=1, source_target_pairs={{0,16},{8,24},{16,0},{24,8},{1,17},{9,25},{17,1},{25,9},{2,18},{10... | collective-permute-start | bytes 1572872 | tf_op jit(solution)/shard_map/cond/branch_1_fun/ppermute | solution.py:200
  148.9 23.8 %collective-permute-start.16 = (bf16[128,2048]{1,0:T(8,128)(2,1)}, bf16[128,2048]{1,0:T(8,128)(2,1)}, u32[]{:S(2)}, u32[]{:S(2)}) collective-permute-start(bf16[128,2048]{1,0:T(8,128)(2,1)} %get-tuple-element.274), channel_id=1, source_target_pairs={{0,8},{8,0},{16,24},{24,16},{1,9},{9,1},{17,25},{25,17},{2,10},{10... | collective-permute-start | bytes 1572872 | tf_op jit(solution)/shard_map/cond/branch_1_fun/ppermute | solution.py:200
  182.1 98.5 %all-to-all-start.3 = ((bf16[4,512,2048]{2,1,0:T(8,128)(2,1)}), bf16[4,512,2048]{2,1,0:T(8,128)(2,1)}, u32[]{:S(2)}, u32[]{:S(2)}) async-start(bf16[4,512,2048]{2,1,0:T(8,128)(2,1)} %broadcast_in_dim.18), calls=%async_computation.3 | async-start | bytes 16777216 | tf_op jit(solution)/shard_map/all_to_all | solution.py:280
  187.9 84.9 %all-gather.8.cloned.1.call-start = ((), (), s32[]{:S(2)}) async-start(), calls=%async_computation.13 | async-start | bytes 2621440 | tf_op jit(solution)/shard_map/all_gather | solution.py:687
  188.6 84.3 %copy-start.27 = (s32[4]{0:T(128)S(1)}, s32[4]{0:T(128)}, u32[]{:S(2)}) copy-start(s32[4]{0:T(128)} %constant.126.clone) | copy-start | bytes 52
  188.6 84.2 %copy-start.28 = (s32[4]{0:T(128)S(1)}, s32[4]{0:T(128)}, u32[]{:S(2)}) copy-start(s32[4]{0:T(128)} %constant.125.clone) | copy-start | bytes 52
  188.7 38.9 %collective-permute-start = (bf16[128,2048]{1,0:T(8,128)(2,1)}, bf16[128,2048]{1,0:T(8,128)(2,1)S(1)}, u32[]{:S(2)}, u32[]{:S(2)}) collective-permute-start(bf16[128,2048]{1,0:T(8,128)(2,1)} %get-tuple-element.99.refs_0_), channel_id=1, source_target_pairs={{0,1},{1,0},{2,3},{3,2},{4,5},{5,4},{6,7},{7,6},{8,9},{9,8},{10,11... | collective-permute-start | bytes 1572872 | tf_op jit(solution)/shard_map/cond/branch_1_fun/ppermute | solution.py:200
  190.4 37.8 %collective-permute-start.1 = (bf16[128,2048]{1,0:T(8,128)(2,1)}, bf16[128,2048]{1,0:T(8,128)(2,1)S(1)}, u32[]{:S(2)}, u32[]{:S(2)}) collective-permute-start(bf16[128,2048]{1,0:T(8,128)(2,1)} %get-tuple-element.99.refs_0_), channel_id=1, source_target_pairs={{0,2},{1,3},{2,0},{3,1},{4,6},{5,7},{6,4},{7,5},{8,10},{9,11},{10,... | collective-permute-start | bytes 1572872 | tf_op jit(solution)/shard_map/cond/branch_1_fun/ppermute | solution.py:200
  192.7 55.5 %collective-permute-start.2 = (bf16[128,2048]{1,0:T(8,128)(2,1)}, bf16[128,2048]{1,0:T(8,128)(2,1)S(1)}, u32[]{:S(2)}, u32[]{:S(2)}) collective-permute-start(bf16[128,2048]{1,0:T(8,128)(2,1)} %get-tuple-element.99.refs_0_), channel_id=1, source_target_pairs={{0,3},{1,2},{2,1},{3,0},{4,7},{5,6},{6,5},{7,4},{8,11},{9,10},{10,... | collective-permute-start | bytes 1572872 | tf_op jit(solution)/shard_map/cond/branch_1_fun/ppermute | solution.py:200
  250.8 4.5 collective-permute-start.3
  272.8 4.4 collective-permute-start.35
  277.2 23.8 %copy-start.12 = (bf16[512,2048]{1,0:T(8,128)(2,1)}, bf16[512,2048]{1,0:T(8,128)(2,1)S(1)}, u32[]{:S(2)}) copy-start(bf16[512,2048]{1,0:T(8,128)(2,1)S(1)} %collective-permute-done.35.far) | copy-start | bytes 6291460
  319.1 11.3 %collective-permute-start.36 = (bf16[512,2048]{1,0:T(8,128)(2,1)}, bf16[512,2048]{1,0:T(8,128)(2,1)S(1)}, u32[]{:S(2)}, u32[]{:S(2)}) collective-permute-start(bf16[512,2048]{1,0:T(8,128)(2,1)} %shard_map.226), channel_id=1, source_target_pairs={{0,4},{4,0},{1,5},{5,1},{2,6},{6,2},{3,7},{7,3},{8,12},{12,8},{9,1... | collective-permute-start | bytes 6291464 | tf_op jit(solution)/shard_map/ppermute | solution.py:200
  319.1 48.4 %collective-permute-start.40 = (bf16[1024,1024]{1,0:T(8,128)(2,1)}, bf16[1024,1024]{1,0:T(8,128)(2,1)}, u32[]{:S(2)}, u32[]{:S(2)}) collective-permute-start(bf16[1024,1024]{1,0:T(8,128)(2,1)} %get-tuple-element.207), channel_id=1, source_target_pairs={{0,16},{8,24},{16,0},{24,8},{1,17},{9,25},{17,1},{25,9},{2,18},{10... | collective-permute-start | bytes 6291464 | tf_op jit(solution)/shard_map/ppermute | solution.py:200
  320.6 52.7 %collective-permute-start.38 = (bf16[1024,1024]{1,0:T(8,128)(2,1)}, bf16[1024,1024]{1,0:T(8,128)(2,1)}, u32[]{:S(2)}, u32[]{:S(2)}) collective-permute-start(bf16[1024,1024]{1,0:T(8,128)(2,1)} %get-tuple-element.205), channel_id=1, source_target_pairs={{0,8},{8,0},{16,24},{24,16},{1,9},{9,1},{17,25},{25,17},{2,10},{10... | collective-permute-start | bytes 6291464 | tf_op jit(solution)/shard_map/ppermute | solution.py:200
  334.6 76.2 %all-to-all-start.4 = ((bf16[4,128,2048]{2,1,0:T(8,128)(2,1)}), bf16[4,128,2048]{2,1,0:T(8,128)(2,1)}, u32[]{:S(2)}, u32[]{:S(2)}) async-start(bf16[4,128,2048]{2,1,0:T(8,128)(2,1)} %bitcast.63), calls=%async_computation.4 | async-start | bytes 4194304 | tf_op jit(solution)/shard_map/all_to_all | solution.py:286
  342.0 164.4 %reduce-scatter.4.cloned.1.call-start = ((), (), s32[]{:S(2)}) async-start(), calls=%async_computation.14 | async-start | bytes 2621440 | tf_op jit(solution)/shard_map/reduce_scatter | solution.py:742
  349.5 56.1 %collective-permute-start.37 = (bf16[512,2048]{1,0:T(8,128)(2,1)}, bf16[512,2048]{1,0:T(8,128)(2,1)}, u32[]{:S(2)}, u32[]{:S(2)}) collective-permute-start(bf16[512,2048]{1,0:T(8,128)(2,1)} %shard_map.228), channel_id=1, source_target_pairs={{0,4},{4,0},{1,5},{5,1},{2,6},{6,2},{3,7},{7,3},{8,12},{12,8},{9,1... | collective-permute-start | bytes 6291464 | tf_op jit(solution)/shard_map/ppermute | solution.py:200
  371.8 25.0 %collective-permute-start.41 = (bf16[512,1024]{1,0:T(8,128)(2,1)}, bf16[512,1024]{1,0:T(8,128)(2,1)S(1)}, u32[]{:S(2)}, u32[]{:S(2)}) collective-permute-start(bf16[512,1024]{1,0:T(8,128)(2,1)} %fusion.17), channel_id=1, source_target_pairs={{0,8},{8,0},{16,24},{24,16},{1,9},{9,1},{17,25},{25,17},{2,10},{10... | collective-permute-start | bytes 3145736 | tf_op jit(solution)/shard_map/ppermute | solution.py:200
  377.6 24.8 %collective-permute-start.39 = (bf16[512,1024]{1,0:T(8,128)(2,1)}, bf16[512,1024]{1,0:T(8,128)(2,1)}, u32[]{:S(2)}, u32[]{:S(2)}) collective-permute-start(bf16[512,1024]{1,0:T(8,128)(2,1)} %fusion.20), channel_id=1, source_target_pairs={{0,16},{8,24},{16,0},{24,8},{1,17},{9,25},{17,1},{25,9},{2,18},{10... | collective-permute-start | bytes 3145736 | tf_op jit(solution)/shard_map/ppermute | solution.py:200
  378.3 18.5 %copy-start.8 = (f32[1024,1024]{1,0:T(8,128)S(1)}, f32[1024,1024]{1,0:T(8,128)}, u32[]{:S(2)}) copy-start(f32[1024,1024]{1,0:T(8,128)} %copy-done.7) | copy-start | bytes 12582916
  384.6 17.8 %copy-start.10 = (f32[1024,1024]{1,0:T(8,128)S(1)}, f32[1024,1024]{1,0:T(8,128)}, u32[]{:S(2)}) copy-start(f32[1024,1024]{1,0:T(8,128)} %copy-done.9) | copy-start | bytes 12582916
  417.7 88.6 %all-to-all-start.5 = ((bf16[8,64,2048]{2,1,0:T(8,128)(2,1)}), bf16[8,64,2048]{2,1,0:T(8,128)(2,1)S(1)}, u32[]{:S(2)}, u32[]{:S(2)}) async-start(bf16[8,64,2048]{2,1,0:T(8,128)(2,1)} %bitcast.62), calls=%async_computation.6 | async-start | bytes 4194304 | tf_op jit(solution)/shard_map/all_to_all | solution.py:741
  423.9 167.6 %reduce-scatter.6.cloned.1.call-start = ((), (), s32[]{:S(2)}) async-start(), calls=%async_computation.15 | async-start | bytes 5242880 | tf_op jit(solution)/shard_map/reduce_scatter | solution.py:773
  424.1 15.1 %collective-permute-start.19 = (bf16[128,2048]{1,0:T(8,128)(2,1)}, bf16[128,2048]{1,0:T(8,128)(2,1)}, u32[]{:S(2)}, u32[]{:S(2)}) collective-permute-start(bf16[128,2048]{1,0:T(8,128)(2,1)} %get-tuple-element.103.refs_0_), channel_id=1, source_target_pairs={{0,8},{8,0},{16,24},{24,16},{1,9},{9,1},{17,25},{25,17},{2,10},{10... | collective-permute-start | bytes 1572872 | tf_op jit(solution)/shard_map/cond/branch_1_fun/ppermute | solution.py:200
  424.9 24.6 %collective-permute-start.20 = (bf16[128,2048]{1,0:T(8,128)(2,1)}, bf16[128,2048]{1,0:T(8,128)(2,1)}, u32[]{:S(2)}, u32[]{:S(2)}) collective-permute-start(bf16[128,2048]{1,0:T(8,128)(2,1)} %get-tuple-element.103.refs_0_), channel_id=1, source_target_pairs={{0,16},{8,24},{16,0},{24,8},{1,17},{9,25},{17,1},{25,9},{2,18},{10... | collective-permute-start | bytes 1572872 | tf_op jit(solution)/shard_map/cond/branch_1_fun/ppermute | solution.py:200
  426.4 24.6 %collective-permute-start.21 = (bf16[128,2048]{1,0:T(8,128)(2,1)}, bf16[128,2048]{1,0:T(8,128)(2,1)}, u32[]{:S(2)}, u32[]{:S(2)}) collective-permute-start(bf16[128,2048]{1,0:T(8,128)(2,1)} %get-tuple-element.103.refs_0_), channel_id=1, source_target_pairs={{0,24},{8,16},{16,8},{24,0},{1,25},{9,17},{17,9},{25,1},{2,26},{10... | collective-permute-start | bytes 1572872 | tf_op jit(solution)/shard_map/cond/branch_1_fun/ppermute | solution.py:200
  427.7 33.4 %collective-permute-start.22 = (bf16[128,2048]{1,0:T(8,128)(2,1)}, bf16[128,2048]{1,0:T(8,128)(2,1)}, u32[]{:S(2)}, u32[]{:S(2)}) collective-permute-start(bf16[128,2048]{1,0:T(8,128)(2,1)} %get-tuple-element.103.refs_0_), channel_id=1, source_target_pairs={{0,4},{4,0},{1,5},{5,1},{2,6},{6,2},{3,7},{7,3},{8,12},{12,8},{9,1... | collective-permute-start | bytes 1572872 | tf_op jit(solution)/shard_map/cond/branch_1_fun/ppermute | solution.py:200
  439.3 21.9 %collective-permute-start.23 = (bf16[128,2048]{1,0:T(8,128)(2,1)}, bf16[128,2048]{1,0:T(8,128)(2,1)}, u32[]{:S(2)}, u32[]{:S(2)}) collective-permute-start(bf16[128,2048]{1,0:T(8,128)(2,1)} %collective-permute-done.19.refs_1_), channel_id=1, source_target_pairs={{0,4},{4,0},{1,5},{5,1},{2,6},{6,2},{3,7},{7,3},{8,12},{12,8},{9,1... | collective-permute-start | bytes 1572872 | tf_op jit(solution)/shard_map/cond/branch_1_fun/ppermute | solution.py:200
  449.5 11.7 %collective-permute-start.24 = (bf16[128,2048]{1,0:T(8,128)(2,1)}, bf16[128,2048]{1,0:T(8,128)(2,1)}, u32[]{:S(2)}, u32[]{:S(2)}) collective-permute-start(bf16[128,2048]{1,0:T(8,128)(2,1)} %collective-permute-done.20.refs_2_), channel_id=1, source_target_pairs={{0,4},{4,0},{1,5},{5,1},{2,6},{6,2},{3,7},{7,3},{8,12},{12,8},{9,1... | collective-permute-start | bytes 1572872 | tf_op jit(solution)/shard_map/cond/branch_1_fun/ppermute | solution.py:200
  451.0 10.2 %collective-permute-start.25 = (bf16[128,2048]{1,0:T(8,128)(2,1)}, bf16[128,2048]{1,0:T(8,128)(2,1)}, u32[]{:S(2)}, u32[]{:S(2)}) collective-permute-start(bf16[128,2048]{1,0:T(8,128)(2,1)} %collective-permute-done.21.refs_3_), channel_id=1, source_target_pairs={{0,4},{4,0},{1,5},{5,1},{2,6},{6,2},{3,7},{7,3},{8,12},{12,8},{9,1... | collective-permute-start | bytes 1572872 | tf_op jit(solution)/shard_map/cond/branch_1_fun/ppermute | solution.py:200
  510.2 88.0 %all-to-all-start.6 = ((bf16[4,8,64,768]{3,2,1,0:T(8,128)(2,1)}), bf16[4,8,64,768]{3,2,1,0:T(8,128)(2,1)}, u32[]{:S(2)}, u32[]{:S(2)}) async-start(bf16[4,8,64,768]{3,2,1,0:T(8,128)(2,1)} %bitcast.60), calls=%async_computation.7 | async-start | bytes 6291456 | tf_op jit(solution)/shard_map/all_to_all | solution.py:771
  515.2 105.4 %reduce-scatter.8.cloned.1.call-start = ((), (), s32[]{:S(2)}) async-start(), calls=%async_computation.16 | async-start | bytes 1310720 | tf_op jit(solution)/shard_map/reduce_scatter | solution.py:789
  520.4 4.2 collective-permute-start.26
  531.2 18.8 %collective-permute-start.29 = (bf16[128,2048]{1,0:T(8,128)(2,1)}, bf16[128,2048]{1,0:T(8,128)(2,1)}, u32[]{:S(2)}, u32[]{:S(2)}) collective-permute-start(bf16[128,2048]{1,0:T(8,128)(2,1)} %get-tuple-element.272), channel_id=1, source_target_pairs={{0,24},{8,16},{16,8},{24,0},{1,25},{9,17},{17,9},{25,1},{2,26},{10... | collective-permute-start | bytes 1572872 | tf_op jit(solution)/shard_map/cond/branch_1_fun/ppermute | solution.py:200
  532.5 27.5 %collective-permute-start.28 = (bf16[128,2048]{1,0:T(8,128)(2,1)}, bf16[128,2048]{1,0:T(8,128)(2,1)}, u32[]{:S(2)}, u32[]{:S(2)}) collective-permute-start(bf16[128,2048]{1,0:T(8,128)(2,1)} %get-tuple-element.273), channel_id=1, source_target_pairs={{0,16},{8,24},{16,0},{24,8},{1,17},{9,25},{17,1},{25,9},{2,18},{10... | collective-permute-start | bytes 1572872 | tf_op jit(solution)/shard_map/cond/branch_1_fun/ppermute | solution.py:200
  533.0 27.1 %collective-permute-start.27 = (bf16[128,2048]{1,0:T(8,128)(2,1)}, bf16[128,2048]{1,0:T(8,128)(2,1)}, u32[]{:S(2)}, u32[]{:S(2)}) collective-permute-start(bf16[128,2048]{1,0:T(8,128)(2,1)} %get-tuple-element.271), channel_id=1, source_target_pairs={{0,8},{8,0},{16,24},{24,16},{1,9},{9,1},{17,25},{25,17},{2,10},{10... | collective-permute-start | bytes 1572872 | tf_op jit(solution)/shard_map/cond/branch_1_fun/ppermute | solution.py:200
  534.8 25.3 %copy-start.21 = (bf16[512,2048]{1,0:T(8,128)(2,1)S(1)}, bf16[512,2048]{1,0:T(8,128)(2,1)}, u32[]{:S(2)}) copy-start(bf16[512,2048]{1,0:T(8,128)(2,1)} %copy-done.20) | copy-start | bytes 6291460 | tf_op jit(solution)/shard_map/cond
  562.3 4.1 collective-permute-start.30
  566.5 4.1 collective-permute-start.31
  570.6 1.2 collective-permute-start.32
  571.9 14.9 %collective-permute-start.33 = (f32[2,2048]{1,0:T(2,128)S(1)}, f32[2,2048]{1,0:T(2,128)S(1)}, u32[]{:S(2)}, u32[]{:S(2)}) collective-permute-start(f32[2,2048]{1,0:T(2,128)S(1)} %add.109), channel_id=1, source_target_pairs={{0,1},{1,0},{2,3},{3,2},{4,5},{5,4},{6,7},{7,6},{8,9},{9,8},{10,11... | collective-permute-start | bytes 49160 | tf_op jit(solution)/shard_map/cond/branch_1_fun/ppermute | solution.py:200
  586.8 4.7 collective-permute-start.34
  601.8 16.1 %all-to-all-start.7 = ((bf16[8,64,768]{2,1,0:T(8,128)(2,1)}), bf16[8,64,768]{2,1,0:T(8,128)(2,1)S(1)}, u32[]{:S(2)}, u32[]{:S(2)}) async-start(bf16[8,64,768]{2,1,0:T(8,128)(2,1)} %reduce_sum.88), calls=%async_computation.8 | async-start | bytes 1572864 | tf_op jit(solution)/shard_map/all_to_all | solution.py:795
  (21 other events, 94.9 us)
Sparse Core Ops, SparseCore 0:
  9.6 30.6 all-gather.3
  42.1 67.5 all-gather.5
  190.3 82.4 all-gather.7
  417.8 85.1 reduce-scatter.3
  506.5 66.7 reduce-scatter.5
  593.9 25.2 reduce-scatter.7

commit v3 on v2

--- a/solution.py
+++ b/solution.py
@@ -664,9 +664,11 @@
         w_qkv = spread_shards(shard, parts).reshape(model_width, 3 * rank_width)
         seq_tokens = join_rows(token_parts)
         normed1, seq_inverse = norm_apply(seq_tokens.astype(FULL), gain)
-        return w_qkv, normed1.astype(LOW), seq_inverse[:local_rows]
-
-    w_qkv, attn_in, inverse1 = region(flag, gather_region, projections, token_low, gains[0])
+        return w_qkv, normed1.astype(LOW), seq_tokens[:half], seq_inverse[:half]
+
+    w_qkv, attn_in, near_tokens, near_inverse = region(
+        flag, gather_region, projections, token_low, gains[0]
+    )
     w_qkv = after(w_qkv, w_down_rows)
     columns = lax.all_to_all(after(columns, w_qkv), ("core", "fsdp"), 0, 0, tiled=True)
     columns = columns.reshape(steps * weight_rows, 2 * column_width)
@@ -706,9 +708,9 @@
         gate_in, up_in = swap_with(gate31, "chip", 1), swap_with(up23, "chip", 2)
         gate_low, up_low = after(gate_low, gate31), after(up_low, up23)
     back_far = contract(gate_low, up_low, w_cols, 1, LOW)
-    back_near = contract(gate_low, up_low, w_cols, 0, FULL)
+    back_near = contract(gate_low, up_low, w_cols, 0, LOW)
     back_far = swap_with(back_far, "core", 1)
-    back_low = (back_near + back_far.astype(FULL)).astype(LOW)
+    back_low = (back_near.astype(FULL) + back_far.astype(FULL)).astype(LOW)
     gate_low, up_low, activation = (
         after(low, back_low) for low in (gate_low, up_low, activation)
     )
@@ -729,8 +731,8 @@
         )
     column_sum = jnp.concatenate([gate_sum, up_sum], axis=1)
     down_far = product_rows(activation[half_mlp:], [w_down_rows], 1, 0, 256)[0]
-    down_near = product_rows(activation[:half_mlp], [w_down_rows], 1, 0, 256, FULL)[0]
-    down_near = down_near + swap_with(down_far, "core", 1).astype(FULL)
+    down_near = product_rows(activation[:half_mlp], [w_down_rows], 1, 0, 256)[0]
+    down_near = down_near.astype(FULL) + swap_with(down_far, "core", 1).astype(FULL)
     down_near = down_near.astype(LOW)
     mlp_in_grad = scatter_each(back_low, "fsdp")
     mlp_in_grad = after(mlp_in_grad, down_near, column_sum)
@@ -772,27 +774,41 @@
     raw_down = after(raw_down, qkv_low)
     down_grad = lax.psum_scatter(raw_down, "chip", scatter_dimension=0, tiled=True)
 
-    def finish_region(qkv_low, w_qkv, token_rows, inverse1, gain, gain2_term):
-        in_far = matmul(qkv_low[half:], w_qkv, 1, 1)
+    def finish_region(qkv_low, w_qkv, token_rows, near_tokens, near_inverse, gain, gain2_term):
+        in_far = matmul(qkv_low[half:], w_qkv, 1, 1).astype(LOW)
         in_near = matmul(qkv_low[:half], w_qkv, 1, 1)
-        in_grad = scatter_rows(in_near, in_far, "chip")
-        token_back, gain1_term = norm_back(token_rows, inverse1, gain, in_grad)
+        in_near = in_near + swap_with(in_far, "core", 1).astype(FULL)
+        gain1_term = jnp.sum(in_near * near_tokens.astype(FULL) * near_inverse, axis=0)
+        in_grad = sum_rows(in_near.astype(LOW), "chip")
         gain_grads = jnp.stack([gain1_term, gain2_term])
-        for axis in EVERY:
+        for axis in RANKS:
             gain_grads = total_over(gain_grads, axis)
+        token_back, _ = norm_back(token_rows, near_inverse[:local_rows], gain, in_grad)
         return token_back, gain_grads
 
     token_back, gain_grads = region(
-        flag, finish_region, qkv_low, w_qkv, token_rows, inverse1, gains[0], gain2_term
+        flag,
+        finish_region,
+        qkv_low,
+        w_qkv,
+        token_rows,
+        near_tokens,
+        near_inverse,
+        gains[0],
+        gain2_term,
     )
     raw_out = after(raw_out, down_grad, gain_grads)
     out_grad = lax.psum_scatter(raw_out, "fsdp", scatter_dimension=0, tiled=True)
-    gain_grads = lax.dynamic_slice_in_dim(
-        gain_grads, ((chip * cores + core) * shards + shard) * weight_rows, weight_rows, 1
-    )
     own_grad = jnp.sum(qkv_grad.astype(FULL).reshape(shards, ranks, weight_rows, -1), axis=0)
     own_grad = after(own_grad.astype(LOW), gain_grads)
     qkv_grad = lax.all_to_all(own_grad, RANKS, 0, 0, tiled=True)
+    gain_grads = region(
+        flag, lambda part: total_over(part, "fsdp"), after(gain_grads, own_grad)
+    )
+    qkv_grad = after(qkv_grad, gain_grads)
+    gain_grads = lax.dynamic_slice_in_dim(
+        gain_grads, ((chip * cores + core) * shards + shard) * weight_rows, weight_rows, 1
+    )
     qkv_grads = shuffle(
         unpack_heads_kernel, [full_shape(weight_rows, model_width)] * 3, qkv_grad
     )

time: 636 us -> 623 us (0.980)
  waiting for transfers between devices: 289 us -> 281 us
    all_to_all x1, waiting for transfers between devices: 9.68 us -> 0.12 us  [local(): qkv_grad = lax.all_to_all(own_grad, RANKS, 0, 0, tiled=True)]
  transfers between devices with their start and end apart: 55 -> 55, of which waited for: 35 -> 34; matrix products, arithmetic and copies ran while one was open for 15% -> 16% of each run, Pallas kernels for 12% -> 13%
where the time goes in v3:
time: 623 us; the launch traced here: 616 us
  waiting for transfers between devices  281 us (45%)
  Pallas kernels  116 us (19%)
  starting transfers between devices  71.1 us (11%)
  other arithmetic  57.7 us (9%)
  matrix products  31.1 us (5%)
  local copies, waits for them, and re-layouts  26.9 us (4%)
  blocking collectives  15.7 us (3%)
  between operations  14.7 us (2%)
    ppermute x40, waiting for transfers between devices, swap_with(): return lax.ppermute(value, axis, [(i, i ^ code) for i in range(count)])  222 us
    dot_general x8, matrix products, matmul(): lax.dot_general(left, right, (((left_dim,), (right_dim,)), ((), ())), pre...  31.1 us
    ppermute x40, starting transfers between devices, swap_with(): return lax.ppermute(value, axis, [(i, i ^ code) for i in range(count)])  28.5 us
    pallas_call x1, Pallas kernels, expand(): pl.pallas_call(expand_kernel, grid=(hidden // tile,), in_specs=[once] * 4...  20.4 us
    pallas_call x2, Pallas kernels, pair_products(): pl.pallas_call(pair_kernel, grid_spec=pltpu.PrefetchScalarGridSpec(num_sc...  18.8 us
    pallas_call x2, Pallas kernels, contract(): pl.pallas_call(contract_kernel, grid=(width // tile,), in_specs=[rows, ro...  17.6 us
    all_gather x1, waiting for transfers between devices, local(): lax.all_gather(after(cotangent[0], normed2), 'fsdp', axis=0, tiled=True)  17.3 us
    all_to_all x1, blocking collectives, local(): lax.all_to_all(after(packed_heads, spread), RANKS, 0, 0, tiled=True)  15.7 us
  transfers between devices with their start and end apart: 55, of which 34 were waited for; matrix products, arithmetic and copies ran while one was open for 16% of the time, Pallas kernels for 13%

profile of v3, /device:TPU:0, one launch (start us, length us, event | category | flops | bytes accessed | tf_op | source)
XLA Modules:
  0.0 615.6 jit_solution(12774026267771015657)
XLA Ops:
  9.3 7.3 %all-to-all-start = ((f32[32,1,128]{2,1,0:T(1,128)}), f32[32,1,128]{2,1,0:T(1,128)S(1)}, u32[]{:S(2)}, u32[]{:S(2)}) async-start(f32[32,1,128]{2,1,0:T(1,128)} %broadcast_in_dim.15), calls=%async_computation | async-start | bytes 32768 | tf_op jit(solution)/shard_map/all_to_all | solution.py:294
  19.8 3.9 all-to-all-done
  23.7 15.7 %all_to_all.44 = bf16[8,64,768]{2,1,0:T(8,128)(2,1)} all-to-all(bf16[8,64,768]{2,1,0:T(8,128)(2,1)S(1)} %shard_map.221), channel_id=1, replica_groups=mesh['chip'=4,'core'=2,'fsdp'=4] {'chip','core'}, dimensions={0} | all-to-all | bytes 1572864 | tf_op jit(solution)/shard_map/all_to_all | solution.py:656
  42.0 63.2 %conditional.6 = (bf16[2048,768]{1,0:T(8,128)(2,1)}, bf16[1024,2048]{1,0:T(8,128)(2,1)}, bf16[512,2048]{1,0:T(8,128)(2,1)}, f32[512,1]{0,1:T(1,128)S(1)}) conditional(s32[]{:T(128)} %bitcast.11, () %tuple.81, (s32[]{:T(128)}, bf16[8,64,768]{2,1,0:T(8,128)(2,1)}, bf16[128,2048]{1,0:T(8,128)(2,1)}, f32[32,64]{1,0:T(8,128)S(1)}) %tuple.84), branch_computations={%region_0.0_spmd, %region_1.3_spmd} | conditional | flops 15074309 | bytes 46445056 | solution.py:195
  47.9 17.1 %collective-permute-done.10.refs_1_ = bf16[128,2048]{1,0:T(8,128)(2,1)S(1)} collective-permute-done((bf16[128,2048]{1,0:T(8,128)(2,1)}, bf16[128,2048]{1,0:T(8,128)(2,1)S(1)}, u32[]{:S(2)}, u32[]{:S(2)}) %collective-permute-start.10) | collective-permute-done | bytes 524320 | tf_op jit(solution)/shard_map/cond/branch_1_fun/ppermute | solution.py:200
  65.0 4.5 collective-permute-done.11.refs_2_
  69.5 10.7 %collective-permute-done.12.refs_3_ = bf16[128,2048]{1,0:T(8,128)(2,1)S(1)} collective-permute-done((bf16[128,2048]{1,0:T(8,128)(2,1)}, bf16[128,2048]{1,0:T(8,128)(2,1)S(1)}, u32[]{:S(2)}, u32[]{:S(2)}) %collective-permute-start.12) | collective-permute-done | bytes 524320 | tf_op jit(solution)/shard_map/cond/branch_1_fun/ppermute | solution.py:200
  89.6 3.1 fusion.2
  92.7 9.5 %collective-permute-done.9 = bf16[8,64,768]{2,1,0:T(8,128)(2,1)S(1)} collective-permute-done((bf16[8,64,768]{2,1,0:T(8,128)(2,1)S(1)}, bf16[8,64,768]{2,1,0:T(8,128)(2,1)S(1)}, u32[]{:S(2)}, u32[]{:S(2)}) %collective-permute-start.9) | collective-permute-done | bytes 786464 | tf_op jit(solution)/shard_map/cond/branch_1_fun/ppermute | solution.py:204
  102.2 3.0 branch_1_fun.7
  105.2 4.5 all-gather.6.cloned.1.call-done.down_rows.refs_0_
  109.7 4.6 all-to-all-start.2
  118.4 59.3 %conditional.7 = (bf16[1024,256]{1,0:T(8,128)(2,1)}, bf16[1024,256]{1,0:T(8,128)(2,1)}, bf16[1024,256]{1,0:T(8,128)(2,1)}, bf16[1024,256]{1,0:T(8,128)(2,1)}, f3...) conditional(s32[]{:T(128)} %bitcast.11, () %tuple.80, ...), branch_computations={%region_5.6_spmd, %region_6.8_spmd} | conditional | flops 4302569984 | bytes 57700128 | solution.py:195
  120.0 6.1 fusion.35.qkv
  126.2 9.4 %branch_1_fun.9 = (bf16[1024,256]{1,0:T(8,128)(2,1)}, bf16[1024,256]{1,0:T(8,128)(2,1)}, bf16[1024,256]{1,0:T(8,128)(2,1)}, bf16[1024,256]{1,0:T(8,128)(2,1)}, f32[2,8,1024]{2,1,0:T(8,128)S(1)}) custom-call(s32[16]{0:T(128)S(1)} %get-tuple-element.90.offsets, f32[1024,768]{1,0:T(8,128)S(1)} %fusion.35.qkv, f32[1024,128]{1,0:T(8,128)S(1)} %copy.32.cosine, ...), custom_call_target="tpu_custom_call" | custom-call | tf_op jit(solution)/shard_map/cond/branch_1_fun/pallas_call | solution.py:551
  137.9 3.8 collective-permute-done.17
  149.4 11.4 %collective-permute-done.18 = bf16[128,2048]{1,0:T(8,128)(2,1)S(1)} collective-permute-done((bf16[128,2048]{1,0:T(8,128)(2,1)}, bf16[128,2048]{1,0:T(8,128)(2,1)S(1)}, u32[]{:S(2)}, u32[]{:S(2)}) %collective-permute-start.18) | collective-permute-done | bytes 524320 | tf_op jit(solution)/shard_map/cond/branch_1_fun/ppermute | solution.py:200
  160.8 11.9 %collective-permute-done.19 = bf16[128,2048]{1,0:T(8,128)(2,1)S(1)} collective-permute-done((bf16[128,2048]{1,0:T(8,128)(2,1)}, bf16[128,2048]{1,0:T(8,128)(2,1)S(1)}, u32[]{:S(2)}, u32[]{:S(2)}) %collective-permute-start.19) | collective-permute-done | bytes 524320 | tf_op jit(solution)/shard_map/cond/branch_1_fun/ppermute | solution.py:200
  172.7 2.9 multiply_reduce_fusion
  177.7 4.4 broadcast_in_dim.18
  182.1 5.7 all-to-all-start.3
  188.6 66.0 %conditional.8 = (bf16[512,2048]{1,0:T(8,128)(2,1)}, bf16[512,2048]{1,0:T(8,128)(2,1)}) conditional(s32[]{:T(128)} %bitcast.11, () %tuple.88, (s32[]{:T(128)}, bf16[128,2048]{1,0:T(8,128)(2,1)}) %tuple.91), branch_computations={%region_8.9_spmd, %region_9.10_spmd} | conditional | bytes 14680240 | solution.py:195
  193.1 35.9 %collective-permute-done.refs_1_ = bf16[128,2048]{1,0:T(8,128)(2,1)S(1)} collective-permute-done((bf16[128,2048]{1,0:T(8,128)(2,1)}, bf16[128,2048]{1,0:T(8,128)(2,1)S(1)}, u32[]{:S(2)}, u32[]{:S(2)}) %collective-permute-start) | collective-permute-done | bytes 524320 | tf_op jit(solution)/shard_map/cond/branch_1_fun/ppermute | solution.py:200
  230.0 17.4 %collective-permute-done.2.refs_3_ = bf16[128,2048]{1,0:T(8,128)(2,1)S(1)} collective-permute-done((bf16[128,2048]{1,0:T(8,128)(2,1)}, bf16[128,2048]{1,0:T(8,128)(2,1)S(1)}, u32[]{:S(2)}, u32[]{:S(2)}) %collective-permute-start.2) | collective-permute-done | bytes 524320 | tf_op jit(solution)/shard_map/cond/branch_1_fun/ppermute | solution.py:200
  250.0 4.5 collective-permute-done.3
  254.6 17.3 %all-gather.8.cloned.1.call-done.near = bf16[512,2048]{1,0:T(8,128)(2,1)} async-done(((bf16[128,2048]{1,0:T(8,128)(2,1)}), bf16[512,2048]{1,0:T(8,128)(2,1)}) %all-gather.8.cloned.1.call-update) | async-done | bytes 2097168 | tf_op jit(solution)/shard_map/all_gather | solution.py:689
  272.6 3.7 collective-permute-done.35.far
  276.4 3.7 all-to-all-done.3
  280.0 20.4 %shard_map.223 = (bf16[1024,2048]{1,0:T(8,128)(2,1)}, bf16[1024,1024]{1,0:T(8,128)(2,1)}, bf16[1024,1024]{1,0:T(8,128)(2,1)}, bf16[1024,1024]{1,0:T(8,128)(2,1)}) custom-call(bf16[512,2048]{1,0:T(8,128)(2,1)} %get-tuple-element.206.near_in, bf16[512,2048]{1,0:T(8,128)(2,1)} %get-tuple-element.207.far_in, ...), custom_call_target="tpu_custom_call" | custom-call | tf_op jit(solution)/shard_map/pallas_call | solution.py:126
  300.4 9.4 %shard_map.224 = (bf16[1024,1024]{1,0:T(8,128)(2,1)}, bf16[1024,1024]{1,0:T(8,128)(2,1)}) custom-call(s32[4]{0:T(128)} %get-tuple-element.311.order, bf16[1024,2048]{1,0:T(8,128)(2,1)} %get-tuple-element.213.left.right, bf16[1024,2048]{1,0:T(8,128)(2,1)} %get-tuple-element.213.left.right, bf16[1024,1024]{1,0:T(8,128)(2,1)} %get-tuple-element.221.gate_low.left, ...), custom_call_target="tpu_custom_call" | custom-call | tf_op jit(solution)/shard_map/pallas_call | solution.py:150
  309.8 8.8 %shard_map.226 = bf16[512,2048]{1,0:T(8,128)(2,1)} custom-call(bf16[1024,1024]{1,0:T(8,128)(2,1)} %get-tuple-element.221.gate_low.left, bf16[1024,1024]{1,0:T(8,128)(2,1)} %get-tuple-element.222.up_low.right, bf16[2048,2048]{1,0:T(8,128)(2,1)} %bitcast.20.gate_cols.up_cols.cols), custom_call_target="tpu_custom_call" | custom-call | tf_op jit(solution)/shard_map/pallas_call | solution.py:179
  320.6 8.9 %shard_map.225 = bf16[512,2048]{1,0:T(8,128)(2,1)} custom-call(bf16[1024,1024]{1,0:T(8,128)(2,1)} %get-tuple-element.221.gate_low.left, bf16[1024,1024]{1,0:T(8,128)(2,1)} %get-tuple-element.222.up_low.right, bf16[2048,2048]{1,0:T(8,128)(2,1)} %bitcast.20.gate_cols.up_cols.cols), custom_call_target="tpu_custom_call" | custom-call | tf_op jit(solution)/shard_map/pallas_call | solution.py:179
  329.4 3.9 add_convert_fusion.2
  333.3 7.5 %all-to-all-start.4 = ((bf16[4,128,2048]{2,1,0:T(8,128)(2,1)}), bf16[4,128,2048]{2,1,0:T(8,128)(2,1)}, u32[]{:S(2)}, u32[]{:S(2)}) async-start(bf16[4,128,2048]{2,1,0:T(8,128)(2,1)} %bitcast.63), calls=%async_computation.4 | async-start | bytes 4194304 | tf_op jit(solution)/shard_map/all_to_all | solution.py:286
  342.7 5.8 shard_map.228
  348.5 9.3 %shard_map.229 = (bf16[1024,1024]{1,0:T(8,128)(2,1)}, bf16[1024,1024]{1,0:T(8,128)(2,1)}) custom-call(s32[4]{0:T(128)} %get-tuple-element.310.order, bf16[1024,2048]{1,0:T(8,128)(2,1)} %get-tuple-element.213.left.right, bf16[1024,2048]{1,0:T(8,128)(2,1)} %get-tuple-element.213.left.right, bf16[1024,1024]{1,0:T(8,128)(2,1)} %get-tuple-element.221.gate_low.left, ...), custom_call_target="tpu_custom_call" | custom-call | tf_op jit(solution)/shard_map/pallas_call | solution.py:150
  357.9 9.1 %collective-permute-done.38 = bf16[1024,1024]{1,0:T(8,128)(2,1)} collective-permute-done((bf16[1024,1024]{1,0:T(8,128)(2,1)}, bf16[1024,1024]{1,0:T(8,128)(2,1)}, u32[]{:S(2)}, u32[]{:S(2)}) %collective-permute-start.38) | collective-permute-done | bytes 2097184 | tf_op jit(solution)/shard_map/ppermute | solution.py:200
  377.7 6.0 shard_map.227
  383.8 12.5 %collective-permute-done.39 = bf16[512,1024]{1,0:T(8,128)(2,1)S(1)} collective-permute-done((bf16[512,1024]{1,0:T(8,128)(2,1)}, bf16[512,1024]{1,0:T(8,128)(2,1)S(1)}, u32[]{:S(2)}, u32[]{:S(2)}) %collective-permute-start.39) | collective-permute-done | bytes 1048608 | tf_op jit(solution)/shard_map/ppermute | solution.py:200
  398.0 3.9 collective-permute-done.41
  412.5 2.8 fusion.30
  415.4 6.2 %all-to-all-start.5 = ((bf16[8,64,2048]{2,1,0:T(8,128)(2,1)}), bf16[8,64,2048]{2,1,0:T(8,128)(2,1)S(1)}, u32[]{:S(2)}, u32[]{:S(2)}) async-start(bf16[8,64,2048]{2,1,0:T(8,128)(2,1)} %bitcast.64), calls=%async_computation.6 | async-start | bytes 4194304 | tf_op jit(solution)/shard_map/all_to_all | solution.py:743
  421.6 59.3 %conditional.9 = (bf16[1024,2048]{1,0:T(8,128)(2,1)}, bf16[256,2048]{0,1:T(8,128)(2,1)}, bf16[1024,768]{1,0:T(8,128)(2,1)}) conditional(s32[]{:T(128)} %bitcast.11, () %tuple.103, (bf16[1024,1024]{1,0:T(8,128)(2,1)}, bf16[512,2048]{1,0:T(8,128)(2,1)}, bf16[512,2048]{1,0:T(8,128)(2,1)}, bf16[128,2048]{1,0:T(8,128)(2,1)}, ...), branch_computations={%region_13.14_spmd, %region_14.15_spmd} | conditional | flops 2148270080 | bytes 32506188 | solution.py:195
  425.4 11.5 %collective-permute-done.21.refs_1_ = bf16[128,2048]{1,0:T(8,128)(2,1)} collective-permute-done((bf16[128,2048]{1,0:T(8,128)(2,1)}, bf16[128,2048]{1,0:T(8,128)(2,1)}, u32[]{:S(2)}, u32[]{:S(2)}) %collective-permute-start.21) | collective-permute-done | bytes 524320 | tf_op jit(solution)/shard_map/cond/branch_1_fun/ppermute | solution.py:200
  436.9 12.0 %collective-permute-done.22.refs_2_ = bf16[128,2048]{1,0:T(8,128)(2,1)} collective-permute-done((bf16[128,2048]{1,0:T(8,128)(2,1)}, bf16[128,2048]{1,0:T(8,128)(2,1)}, u32[]{:S(2)}, u32[]{:S(2)}) %collective-permute-start.22) | collective-permute-done | bytes 524320 | tf_op jit(solution)/shard_map/cond/branch_1_fun/ppermute | solution.py:200
  450.9 8.8 %branch_1_fun.11 = bf16[1024,2048]{1,0:T(8,128)(2,1)} custom-call(bf16[1024,1024]{1,0:T(8,128)(2,1)} %get-tuple-element.106.left, bf16[512,2048]{1,0:T(8,128)(2,1)} %get-tuple-element.107.near, bf16[512,2048]{1,0:T(8,128)(2,1)} %get-tuple-element.108.far), custom_call_target="tpu_custom_call" | custom-call | tf_op jit(solution)/shard_map/cond/branch_1_fun/pallas_call | solution.py:83
  463.5 3.4 fusion.9
  466.8 13.9 %branch_1_fun.13 = bf16[1024,768]{1,0:T(8,128)(2,1)} custom-call(s32[16]{0:T(128)S(1)} %get-tuple-element.111.offsets, bf16[1024,256]{1,0:T(8,128)(2,1)S(1)} %convolution_convert_fusion.2.upstream, bf16[1024,256]{1,0:T(8,128)(2,1)} %get-tuple-element.113.query_in, bf16[1024,256]{1,0:T(8,128)(2,1)} %get-tuple-element.114.key_in, ...), custom_call_target="tpu_custom_call" | custom-call | tf_op jit(solution)/shard_map/cond/branch_1_fun/pallas_call | solution.py:579
  481.0 7.9 %convolution_convert_fusion.4 = bf16[2048,768]{1,0:T(8,128)(2,1)} fusion(bf16[1024,2048]{1,0:T(8,128)(2,1)} %get-tuple-element.198, bf16[1024,768]{1,0:T(8,128)(2,1)} %get-tuple-element.235), kind=kOutput, calls=%fused_computation.40 | convolution fusion | flops 3222798336 | bytes 8912896 | tf_op jit(solution)/shard_map/dot_general | solution.py:41
  488.9 15.2 %all-to-all-done.5.packed = bf16[8,64,2048]{2,1,0:T(8,128)(2,1)S(1)} async-done(((bf16[8,64,2048]{2,1,0:T(8,128)(2,1)}), bf16[8,64,2048]{2,1,0:T(8,128)(2,1)S(1)}, u32[]{:S(2)}, u32[]{:S(2)}) %all-to-all-start.5) | async-done | bytes 2097184 | tf_op jit(solution)/shard_map/all_to_all | solution.py:743
  504.0 3.9 copy.39
  508.0 5.0 all-to-all-start.6
  513.2 62.0 %conditional.10 = (f32[128,2048]{1,0:T(8,128)}, f32[2,2048]{1,0:T(2,128)S(1)}) conditional(s32[]{:T(128)} %bitcast.11, () %tuple.102, (f32[512,1]{0,1:T(1,128)S(1)}, bf16[1024,768]{1,0:T(8,128)(2,1)}, bf16[2048,768]{1,0:T(8,128)(2,1)}, f32[32,64]{1,0:T(8,128)S(1)}, f32[128,2048]{1,0:T(8,128)}, /*index=5*/bf16[512,2048]{1,0:T(8,128)(2,1)}, ...), branch_computations={%region_15.16_spmd, %region_16.20_spmd} | conditional | flops 3236192512 | bytes 53402436 | solution.py:195
  513.2 4.0 convolution_convert_fusion.3
  521.4 5.1 multiply_reduce_fusion.1
  536.8 13.2 %collective-permute-done.29 = bf16[128,2048]{1,0:T(8,128)(2,1)S(1)} collective-permute-done((bf16[128,2048]{1,0:T(8,128)(2,1)}, bf16[128,2048]{1,0:T(8,128)(2,1)S(1)}, u32[]{:S(2)}, u32[]{:S(2)}) %collective-permute-start.29) | collective-permute-done | bytes 524320 | tf_op jit(solution)/shard_map/cond/branch_1_fun/ppermute | solution.py:200
  550.0 3.3 collective-permute-done.30
  553.4 16.9 %collective-permute-done.31 = bf16[128,2048]{1,0:T(8,128)(2,1)} collective-permute-done((bf16[128,2048]{1,0:T(8,128)(2,1)}, bf16[128,2048]{1,0:T(8,128)(2,1)}, u32[]{:S(2)}, u32[]{:S(2)}) %collective-permute-start.31) | collective-permute-done | bytes 524320 | tf_op jit(solution)/shard_map/cond/branch_1_fun/ppermute | solution.py:200
  572.2 3.0 multiply_subtract_fusion
  584.3 3.5 reduce_sum.88
  587.8 3.7 all-to-all-start.7
  593.6 9.7 %conditional.11 = (f32[2,2048]{1,0:T(2,128)S(1)}) conditional(s32[]{:T(128)} %bitcast.11, () %tuple.108, f32[2,2048]{1,0:T(2,128)S(1)} %get-tuple-element.241), branch_computations={%region_21.22_spmd, %region_22.23_spmd} | conditional | flops 8192 | bytes 229464 | solution.py:195
  593.6 4.5 collective-permute-done.4
  598.2 5.0 collective-permute-done.5
  (214 shorter events, 119.7 us)
Async XLA Ops:
  7.2 33.1 %all-gather.4.cloned.1.call-start = ((), (), s32[]{:S(2)}) async-start(), calls=%async_computation.11 | async-start | bytes 1310720 | tf_op jit(solution)/shard_map/all_gather | solution.py:653
  9.3 14.4 %all-to-all-start = ((f32[32,1,128]{2,1,0:T(1,128)}), f32[32,1,128]{2,1,0:T(1,128)S(1)}, u32[]{:S(2)}, u32[]{:S(2)}) async-start(f32[32,1,128]{2,1,0:T(1,128)} %broadcast_in_dim.15), calls=%async_computation | async-start | bytes 32768 | tf_op jit(solution)/shard_map/all_to_all | solution.py:294
  16.6 23.7 %copy-start = (bf16[64,8192]{1,0:T(8,128)(2,1)S(1)}, bf16[64,8192]{1,0:T(8,128)(2,1)}, u32[]{:S(2)}) copy-start(bf16[64,8192]{1,0:T(8,128)(2,1)} %gate.1) | copy-start | bytes 3145732
  16.6 23.7 %copy-start.1 = (bf16[64,8192]{1,0:T(8,128)(2,1)S(1)}, bf16[64,8192]{1,0:T(8,128)(2,1)}, u32[]{:S(2)}) copy-start(bf16[64,8192]{1,0:T(8,128)(2,1)} %up.1) | copy-start | bytes 3145732
  16.6 93.1 %all-gather.6.cloned.1.call-start = ((), (), s32[]{:S(2)}) async-start(), calls=%async_computation.12 | async-start | bytes 5242880 | tf_op jit(solution)/shard_map/all_gather | solution.py:659
  19.7 20.6 %copy-start.28 = (s32[1,4]{1,0:T(1,128)S(1)}, s32[1,4]{1,0:T(1,128)}, u32[]{:S(2)}) copy-start(s32[1,4]{1,0:T(1,128)} %param.27) | copy-start | bytes 52
  42.0 38.3 %collective-permute-start.6 = (bf16[8,64,768]{2,1,0:T(8,128)(2,1)}, bf16[8,64,768]{2,1,0:T(8,128)(2,1)S(1)}, u32[]{:S(2)}, u32[]{:S(2)}) collective-permute-start(bf16[8,64,768]{2,1,0:T(8,128)(2,1)} %get-tuple-element.87.refs_0_), channel_id=1, source_target_pairs={{0,1},{1,0},{2,3},{3,2},{4,5},{5,4},{6,7},{7,6},{8,9},{9,8},{10,11... | collective-permute-start | bytes 2359304 | tf_op jit(solution)/shard_map/cond/branch_1_fun/ppermute | solution.py:200
  43.4 21.6 %collective-permute-start.10 = (bf16[128,2048]{1,0:T(8,128)(2,1)}, bf16[128,2048]{1,0:T(8,128)(2,1)S(1)}, u32[]{:S(2)}, u32[]{:S(2)}) collective-permute-start(bf16[128,2048]{1,0:T(8,128)(2,1)} %get-tuple-element.88.refs_0_), channel_id=1, source_target_pairs={{0,8},{8,0},{16,24},{24,16},{1,9},{9,1},{17,25},{25,17},{2,10},{10... | collective-permute-start | bytes 1572872 | tf_op jit(solution)/shard_map/cond/branch_1_fun/ppermute | solution.py:200
  44.9 24.7 %collective-permute-start.11 = (bf16[128,2048]{1,0:T(8,128)(2,1)}, bf16[128,2048]{1,0:T(8,128)(2,1)S(1)}, u32[]{:S(2)}, u32[]{:S(2)}) collective-permute-start(bf16[128,2048]{1,0:T(8,128)(2,1)} %get-tuple-element.88.refs_0_), channel_id=1, source_target_pairs={{0,16},{8,24},{16,0},{24,8},{1,17},{9,25},{17,1},{25,9},{2,18},{10... | collective-permute-start | bytes 1572872 | tf_op jit(solution)/shard_map/cond/branch_1_fun/ppermute | solution.py:200
  46.3 33.9 %collective-permute-start.12 = (bf16[128,2048]{1,0:T(8,128)(2,1)}, bf16[128,2048]{1,0:T(8,128)(2,1)S(1)}, u32[]{:S(2)}, u32[]{:S(2)}) collective-permute-start(bf16[128,2048]{1,0:T(8,128)(2,1)} %get-tuple-element.88.refs_0_), channel_id=1, source_target_pairs={{0,24},{8,16},{16,8},{24,0},{1,25},{9,17},{17,9},{25,1},{2,26},{10... | collective-permute-start | bytes 1572872 | tf_op jit(solution)/shard_map/cond/branch_1_fun/ppermute | solution.py:200
  46.9 35.9 %collective-permute-start.7 = (bf16[8,64,768]{2,1,0:T(8,128)(2,1)}, bf16[8,64,768]{2,1,0:T(8,128)(2,1)S(1)}, u32[]{:S(2)}, u32[]{:S(2)}) collective-permute-start(bf16[8,64,768]{2,1,0:T(8,128)(2,1)} %get-tuple-element.87.refs_0_), channel_id=1, source_target_pairs={{0,2},{1,3},{2,0},{3,1},{4,6},{5,7},{6,4},{7,5},{8,10},{9,11},{10,... | collective-permute-start | bytes 2359304 | tf_op jit(solution)/shard_map/cond/branch_1_fun/ppermute | solution.py:200
  65.0 19.2 %collective-permute-start.13 = (bf16[128,2048]{1,0:T(8,128)(2,1)}, bf16[128,2048]{1,0:T(8,128)(2,1)}, u32[]{:S(2)}, u32[]{:S(2)}) collective-permute-start(bf16[128,2048]{1,0:T(8,128)(2,1)} %get-tuple-element.88.refs_0_), channel_id=1, source_target_pairs={{0,4},{4,0},{1,5},{5,1},{2,6},{6,2},{3,7},{7,3},{8,12},{12,8},{9,1... | collective-permute-start | bytes 1572872 | tf_op jit(solution)/shard_map/cond/branch_1_fun/ppermute | solution.py:200
  69.5 15.3 %collective-permute-start.14 = (bf16[128,2048]{1,0:T(8,128)(2,1)S(1)}, bf16[128,2048]{1,0:T(8,128)(2,1)}, u32[]{:S(2)}, u32[]{:S(2)}) collective-permute-start(bf16[128,2048]{1,0:T(8,128)(2,1)S(1)} %collective-permute-done.10.refs_1_), channel_id=1, source_target_pairs={{0,4},{4,0},{1,5},{5,1},{2,6},{6,2},{3,7},{7,3},{8,12},{12,8},{9,1... | collective-permute-start | bytes 1572872 | tf_op jit(solution)/shard_map/cond/branch_1_fun/ppermute | solution.py:200
  80.2 4.7 collective-permute-start.15
  80.2 4.7 collective-permute-start.16
  82.8 19.3 %collective-permute-start.9 = (bf16[8,64,768]{2,1,0:T(8,128)(2,1)S(1)}, bf16[8,64,768]{2,1,0:T(8,128)(2,1)S(1)}, u32[]{:S(2)}, u32[]{:S(2)}) collective-permute-start(bf16[8,64,768]{2,1,0:T(8,128)(2,1)S(1)} %collective-permute-done.7.refs_2_), channel_id=1, source_target_pairs={{2,3},{1,0},{6,7},{5,4},{10,11},{9,8},{14,15},{13,12},{18,19},{17,... | collective-permute-start | bytes 2359304 | tf_op jit(solution)/shard_map/cond/branch_1_fun/ppermute | solution.py:204
  84.1 8.5 %collective-permute-start.8 = (bf16[8,64,768]{2,1,0:T(8,128)(2,1)}, bf16[8,64,768]{2,1,0:T(8,128)(2,1)S(1)}, u32[]{:S(2)}, u32[]{:S(2)}) collective-permute-start(bf16[8,64,768]{2,1,0:T(8,128)(2,1)} %get-tuple-element.87.refs_0_), channel_id=1, source_target_pairs={{1,2},{2,1},{5,6},{6,5},{9,10},{10,9},{13,14},{14,13},{17,18},{18,... | collective-permute-start | bytes 2359304 | tf_op jit(solution)/shard_map/cond/branch_1_fun/ppermute | solution.py:204
  109.7 68.0 %all-to-all-start.2 = ((bf16[8,64,2048]{2,1,0:T(8,128)(2,1)}), bf16[8,64,2048]{2,1,0:T(8,128)(2,1)S(1)}, u32[]{:S(2)}, u32[]{:S(2)}) async-start(bf16[8,64,2048]{2,1,0:T(8,128)(2,1)} %shard_map.222), calls=%async_computation.2 | async-start | bytes 4194304 | tf_op jit(solution)/shard_map/all_to_all | solution.py:673
  137.3 4.4 collective-permute-start.17
  145.8 15.0 %collective-permute-start.18 = (bf16[128,2048]{1,0:T(8,128)(2,1)}, bf16[128,2048]{1,0:T(8,128)(2,1)S(1)}, u32[]{:S(2)}, u32[]{:S(2)}) collective-permute-start(bf16[128,2048]{1,0:T(8,128)(2,1)} %get-tuple-element.298), channel_id=1, source_target_pairs={{0,8},{8,0},{16,24},{24,16},{1,9},{9,1},{17,25},{25,17},{2,10},{10... | collective-permute-start | bytes 1572872 | tf_op jit(solution)/shard_map/cond/branch_1_fun/ppermute | solution.py:200
  147.3 25.4 %collective-permute-start.19 = (bf16[128,2048]{1,0:T(8,128)(2,1)}, bf16[128,2048]{1,0:T(8,128)(2,1)S(1)}, u32[]{:S(2)}, u32[]{:S(2)}) collective-permute-start(bf16[128,2048]{1,0:T(8,128)(2,1)} %get-tuple-element.300), channel_id=1, source_target_pairs={{0,16},{8,24},{16,0},{24,8},{1,17},{9,25},{17,1},{25,9},{2,18},{10... | collective-permute-start | bytes 1572872 | tf_op jit(solution)/shard_map/cond/branch_1_fun/ppermute | solution.py:200
  147.9 24.8 %collective-permute-start.20 = (bf16[128,2048]{1,0:T(8,128)(2,1)}, bf16[128,2048]{1,0:T(8,128)(2,1)}, u32[]{:S(2)}, u32[]{:S(2)}) collective-permute-start(bf16[128,2048]{1,0:T(8,128)(2,1)} %get-tuple-element.299), channel_id=1, source_target_pairs={{0,24},{8,16},{16,8},{24,0},{1,25},{9,17},{17,9},{25,1},{2,26},{10... | collective-permute-start | bytes 1572872 | tf_op jit(solution)/shard_map/cond/branch_1_fun/ppermute | solution.py:200
  182.1 97.9 %all-to-all-start.3 = ((bf16[4,512,2048]{2,1,0:T(8,128)(2,1)}), bf16[4,512,2048]{2,1,0:T(8,128)(2,1)}, u32[]{:S(2)}, u32[]{:S(2)}) async-start(bf16[4,512,2048]{2,1,0:T(8,128)(2,1)} %broadcast_in_dim.18), calls=%async_computation.3 | async-start | bytes 16777216 | tf_op jit(solution)/shard_map/all_to_all | solution.py:280
  187.8 84.1 %all-gather.8.cloned.1.call-start = ((), (), s32[]{:S(2)}) async-start(), calls=%async_computation.13 | async-start | bytes 2621440 | tf_op jit(solution)/shard_map/all_gather | solution.py:689
  188.6 83.5 %copy-start.26 = (s32[4]{0:T(128)S(1)}, s32[4]{0:T(128)}, u32[]{:S(2)}) copy-start(s32[4]{0:T(128)} %constant.128.clone) | copy-start | bytes 52
  188.6 83.5 %copy-start.27 = (s32[4]{0:T(128)S(1)}, s32[4]{0:T(128)}, u32[]{:S(2)}) copy-start(s32[4]{0:T(128)} %constant.129.clone) | copy-start | bytes 52
  188.6 40.3 %collective-permute-start = (bf16[128,2048]{1,0:T(8,128)(2,1)}, bf16[128,2048]{1,0:T(8,128)(2,1)S(1)}, u32[]{:S(2)}, u32[]{:S(2)}) collective-permute-start(bf16[128,2048]{1,0:T(8,128)(2,1)} %get-tuple-element.105.refs_0_), channel_id=1, source_target_pairs={{0,1},{1,0},{2,3},{3,2},{4,5},{5,4},{6,7},{7,6},{8,9},{9,8},{10,11... | collective-permute-start | bytes 1572872 | tf_op jit(solution)/shard_map/cond/branch_1_fun/ppermute | solution.py:200
  190.4 39.6 %collective-permute-start.1 = (bf16[128,2048]{1,0:T(8,128)(2,1)}, bf16[128,2048]{1,0:T(8,128)(2,1)S(1)}, u32[]{:S(2)}, u32[]{:S(2)}) collective-permute-start(bf16[128,2048]{1,0:T(8,128)(2,1)} %get-tuple-element.105.refs_0_), channel_id=1, source_target_pairs={{0,2},{1,3},{2,0},{3,1},{4,6},{5,7},{6,4},{7,5},{8,10},{9,11},{10,... | collective-permute-start | bytes 1572872 | tf_op jit(solution)/shard_map/cond/branch_1_fun/ppermute | solution.py:200
  192.7 54.7 %collective-permute-start.2 = (bf16[128,2048]{1,0:T(8,128)(2,1)}, bf16[128,2048]{1,0:T(8,128)(2,1)S(1)}, u32[]{:S(2)}, u32[]{:S(2)}) collective-permute-start(bf16[128,2048]{1,0:T(8,128)(2,1)} %get-tuple-element.105.refs_0_), channel_id=1, source_target_pairs={{0,3},{1,2},{2,1},{3,0},{4,7},{5,6},{6,5},{7,4},{8,11},{9,10},{10,... | collective-permute-start | bytes 1572872 | tf_op jit(solution)/shard_map/cond/branch_1_fun/ppermute | solution.py:200
  250.0 4.5 collective-permute-start.3
  272.0 4.4 collective-permute-start.35
  276.4 24.1 %copy-start.11 = (bf16[512,2048]{1,0:T(8,128)(2,1)}, bf16[512,2048]{1,0:T(8,128)(2,1)S(1)}, u32[]{:S(2)}) copy-start(bf16[512,2048]{1,0:T(8,128)(2,1)S(1)} %collective-permute-done.35.far) | copy-start | bytes 6291460
  318.6 10.8 %collective-permute-start.36 = (bf16[512,2048]{1,0:T(8,128)(2,1)}, bf16[512,2048]{1,0:T(8,128)(2,1)S(1)}, u32[]{:S(2)}, u32[]{:S(2)}) collective-permute-start(bf16[512,2048]{1,0:T(8,128)(2,1)} %shard_map.226), channel_id=1, source_target_pairs={{0,4},{4,0},{1,5},{5,1},{2,6},{6,2},{3,7},{7,3},{8,12},{12,8},{9,1... | collective-permute-start | bytes 6291464 | tf_op jit(solution)/shard_map/ppermute | solution.py:200
  318.6 48.4 %collective-permute-start.38 = (bf16[1024,1024]{1,0:T(8,128)(2,1)}, bf16[1024,1024]{1,0:T(8,128)(2,1)}, u32[]{:S(2)}, u32[]{:S(2)}) collective-permute-start(bf16[1024,1024]{1,0:T(8,128)(2,1)} %get-tuple-element.215), channel_id=1, source_target_pairs={{0,8},{8,0},{16,24},{24,16},{1,9},{9,1},{17,25},{25,17},{2,10},{10... | collective-permute-start | bytes 6291464 | tf_op jit(solution)/shard_map/ppermute | solution.py:200
  320.0 52.7 %collective-permute-start.40 = (bf16[1024,1024]{1,0:T(8,128)(2,1)}, bf16[1024,1024]{1,0:T(8,128)(2,1)}, u32[]{:S(2)}, u32[]{:S(2)}) collective-permute-start(bf16[1024,1024]{1,0:T(8,128)(2,1)} %get-tuple-element.217), channel_id=1, source_target_pairs={{0,16},{8,24},{16,0},{24,8},{1,17},{9,25},{17,1},{25,9},{2,18},{10... | collective-permute-start | bytes 6291464 | tf_op jit(solution)/shard_map/ppermute | solution.py:200
  333.3 75.2 %all-to-all-start.4 = ((bf16[4,128,2048]{2,1,0:T(8,128)(2,1)}), bf16[4,128,2048]{2,1,0:T(8,128)(2,1)}, u32[]{:S(2)}, u32[]{:S(2)}) async-start(bf16[4,128,2048]{2,1,0:T(8,128)(2,1)} %bitcast.63), calls=%async_computation.4 | async-start | bytes 4194304 | tf_op jit(solution)/shard_map/all_to_all | solution.py:286
  340.8 163.2 %reduce-scatter.4.cloned.1.call-start = ((), (), s32[]{:S(2)}) async-start(), calls=%async_computation.14 | async-start | bytes 2621440 | tf_op jit(solution)/shard_map/reduce_scatter | solution.py:744
  348.5 57.1 %collective-permute-start.37 = (bf16[512,2048]{1,0:T(8,128)(2,1)}, bf16[512,2048]{1,0:T(8,128)(2,1)S(1)}, u32[]{:S(2)}, u32[]{:S(2)}) collective-permute-start(bf16[512,2048]{1,0:T(8,128)(2,1)} %shard_map.228), channel_id=1, source_target_pairs={{0,4},{4,0},{1,5},{5,1},{2,6},{6,2},{3,7},{7,3},{8,12},{12,8},{9,1... | collective-permute-start | bytes 6291464 | tf_op jit(solution)/shard_map/ppermute | solution.py:200
  371.3 25.0 %collective-permute-start.39 = (bf16[512,1024]{1,0:T(8,128)(2,1)}, bf16[512,1024]{1,0:T(8,128)(2,1)S(1)}, u32[]{:S(2)}, u32[]{:S(2)}) collective-permute-start(bf16[512,1024]{1,0:T(8,128)(2,1)} %fusion.19), channel_id=1, source_target_pairs={{0,16},{8,24},{16,0},{24,8},{1,17},{9,25},{17,1},{25,9},{2,18},{10... | collective-permute-start | bytes 3145736 | tf_op jit(solution)/shard_map/ppermute | solution.py:200
  377.1 24.8 %collective-permute-start.41 = (bf16[512,1024]{1,0:T(8,128)(2,1)}, bf16[512,1024]{1,0:T(8,128)(2,1)}, u32[]{:S(2)}, u32[]{:S(2)}) collective-permute-start(bf16[512,1024]{1,0:T(8,128)(2,1)} %fusion.16), channel_id=1, source_target_pairs={{0,8},{8,0},{16,24},{24,16},{1,9},{9,1},{17,25},{25,17},{2,10},{10... | collective-permute-start | bytes 3145736 | tf_op jit(solution)/shard_map/ppermute | solution.py:200
  377.7 18.6 %copy-start.8 = (f32[1024,1024]{1,0:T(8,128)S(1)}, f32[1024,1024]{1,0:T(8,128)}, u32[]{:S(2)}) copy-start(f32[1024,1024]{1,0:T(8,128)} %copy-done.7) | copy-start | bytes 12582916
  383.8 18.1 %copy-start.10 = (f32[1024,1024]{1,0:T(8,128)S(1)}, f32[1024,1024]{1,0:T(8,128)}, u32[]{:S(2)}) copy-start(f32[1024,1024]{1,0:T(8,128)} %copy-done.9) | copy-start | bytes 12582916
  415.4 88.7 %all-to-all-start.5 = ((bf16[8,64,2048]{2,1,0:T(8,128)(2,1)}), bf16[8,64,2048]{2,1,0:T(8,128)(2,1)S(1)}, u32[]{:S(2)}, u32[]{:S(2)}) async-start(bf16[8,64,2048]{2,1,0:T(8,128)(2,1)} %bitcast.64), calls=%async_computation.6 | async-start | bytes 4194304 | tf_op jit(solution)/shard_map/all_to_all | solution.py:743
  421.6 153.6 %reduce-scatter.6.cloned.1.call-start = ((), (), s32[]{:S(2)}) async-start(), calls=%async_computation.15 | async-start | bytes 5242880 | tf_op jit(solution)/shard_map/reduce_scatter | solution.py:775
  421.8 15.1 %collective-permute-start.21 = (bf16[128,2048]{1,0:T(8,128)(2,1)}, bf16[128,2048]{1,0:T(8,128)(2,1)}, u32[]{:S(2)}, u32[]{:S(2)}) collective-permute-start(bf16[128,2048]{1,0:T(8,128)(2,1)} %get-tuple-element.109.refs_0_), channel_id=1, source_target_pairs={{0,8},{8,0},{16,24},{24,16},{1,9},{9,1},{17,25},{25,17},{2,10},{10... | collective-permute-start | bytes 1572872 | tf_op jit(solution)/shard_map/cond/branch_1_fun/ppermute | solution.py:200
  423.3 25.6 %collective-permute-start.22 = (bf16[128,2048]{1,0:T(8,128)(2,1)}, bf16[128,2048]{1,0:T(8,128)(2,1)}, u32[]{:S(2)}, u32[]{:S(2)}) collective-permute-start(bf16[128,2048]{1,0:T(8,128)(2,1)} %get-tuple-element.109.refs_0_), channel_id=1, source_target_pairs={{0,16},{8,24},{16,0},{24,8},{1,17},{9,25},{17,1},{25,9},{2,18},{10... | collective-permute-start | bytes 1572872 | tf_op jit(solution)/shard_map/cond/branch_1_fun/ppermute | solution.py:200
  424.0 24.9 %collective-permute-start.23 = (bf16[128,2048]{1,0:T(8,128)(2,1)}, bf16[128,2048]{1,0:T(8,128)(2,1)}, u32[]{:S(2)}, u32[]{:S(2)}) collective-permute-start(bf16[128,2048]{1,0:T(8,128)(2,1)} %get-tuple-element.109.refs_0_), channel_id=1, source_target_pairs={{0,24},{8,16},{16,8},{24,0},{1,25},{9,17},{17,9},{25,1},{2,26},{10... | collective-permute-start | bytes 1572872 | tf_op jit(solution)/shard_map/cond/branch_1_fun/ppermute | solution.py:200
  425.4 34.3 %collective-permute-start.24 = (bf16[128,2048]{1,0:T(8,128)(2,1)}, bf16[128,2048]{1,0:T(8,128)(2,1)}, u32[]{:S(2)}, u32[]{:S(2)}) collective-permute-start(bf16[128,2048]{1,0:T(8,128)(2,1)} %get-tuple-element.109.refs_0_), channel_id=1, source_target_pairs={{0,4},{4,0},{1,5},{5,1},{2,6},{6,2},{3,7},{7,3},{8,12},{12,8},{9,1... | collective-permute-start | bytes 1572872 | tf_op jit(solution)/shard_map/cond/branch_1_fun/ppermute | solution.py:200
  436.9 22.7 %collective-permute-start.25 = (bf16[128,2048]{1,0:T(8,128)(2,1)}, bf16[128,2048]{1,0:T(8,128)(2,1)}, u32[]{:S(2)}, u32[]{:S(2)}) collective-permute-start(bf16[128,2048]{1,0:T(8,128)(2,1)} %collective-permute-done.21.refs_1_), channel_id=1, source_target_pairs={{0,4},{4,0},{1,5},{5,1},{2,6},{6,2},{3,7},{7,3},{8,12},{12,8},{9,1... | collective-permute-start | bytes 1572872 | tf_op jit(solution)/shard_map/cond/branch_1_fun/ppermute | solution.py:200
  448.9 10.7 %collective-permute-start.26 = (bf16[128,2048]{1,0:T(8,128)(2,1)}, bf16[128,2048]{1,0:T(8,128)(2,1)}, u32[]{:S(2)}, u32[]{:S(2)}) collective-permute-start(bf16[128,2048]{1,0:T(8,128)(2,1)} %collective-permute-done.22.refs_2_), channel_id=1, source_target_pairs={{0,4},{4,0},{1,5},{5,1},{2,6},{6,2},{3,7},{7,3},{8,12},{12,8},{9,1... | collective-permute-start | bytes 1572872 | tf_op jit(solution)/shard_map/cond/branch_1_fun/ppermute | solution.py:200
  448.9 10.7 %collective-permute-start.27 = (bf16[128,2048]{1,0:T(8,128)(2,1)}, bf16[128,2048]{1,0:T(8,128)(2,1)}, u32[]{:S(2)}, u32[]{:S(2)}) collective-permute-start(bf16[128,2048]{1,0:T(8,128)(2,1)} %collective-permute-done.23.refs_3_), channel_id=1, source_target_pairs={{0,4},{4,0},{1,5},{5,1},{2,6},{6,2},{3,7},{7,3},{8,12},{12,8},{9,1... | collective-permute-start | bytes 1572872 | tf_op jit(solution)/shard_map/cond/branch_1_fun/ppermute | solution.py:200
  508.0 76.3 %all-to-all-start.6 = ((bf16[4,8,64,768]{3,2,1,0:T(8,128)(2,1)}), bf16[4,8,64,768]{3,2,1,0:T(8,128)(2,1)}, u32[]{:S(2)}, u32[]{:S(2)}) async-start(bf16[4,8,64,768]{3,2,1,0:T(8,128)(2,1)} %bitcast.61), calls=%async_computation.7 | async-start | bytes 6291456 | tf_op jit(solution)/shard_map/all_to_all | solution.py:773
  513.0 93.8 %reduce-scatter.8.cloned.1.call-start = ((), (), s32[]{:S(2)}) async-start(), calls=%async_computation.16 | async-start | bytes 1310720 | tf_op jit(solution)/shard_map/reduce_scatter | solution.py:801
  517.2 4.2 collective-permute-start.28
  526.6 4.1 collective-permute-start.32
  530.7 4.8 collective-permute-start.33
  532.1 18.0 %collective-permute-start.29 = (bf16[128,2048]{1,0:T(8,128)(2,1)}, bf16[128,2048]{1,0:T(8,128)(2,1)S(1)}, u32[]{:S(2)}, u32[]{:S(2)}) collective-permute-start(bf16[128,2048]{1,0:T(8,128)(2,1)} %get-tuple-element.293), channel_id=1, source_target_pairs={{0,8},{8,0},{16,24},{24,16},{1,9},{9,1},{17,25},{25,17},{2,10},{10... | collective-permute-start | bytes 1572872 | tf_op jit(solution)/shard_map/cond/branch_1_fun/ppermute | solution.py:200
  533.8 19.6 %collective-permute-start.30 = (bf16[128,2048]{1,0:T(8,128)(2,1)}, bf16[128,2048]{1,0:T(8,128)(2,1)S(1)}, u32[]{:S(2)}, u32[]{:S(2)}) collective-permute-start(bf16[128,2048]{1,0:T(8,128)(2,1)} %get-tuple-element.295), channel_id=1, source_target_pairs={{0,16},{8,24},{16,0},{24,8},{1,17},{9,25},{17,1},{25,9},{2,18},{10... | collective-permute-start | bytes 1572872 | tf_op jit(solution)/shard_map/cond/branch_1_fun/ppermute | solution.py:200
  535.3 34.9 %collective-permute-start.31 = (bf16[128,2048]{1,0:T(8,128)(2,1)}, bf16[128,2048]{1,0:T(8,128)(2,1)}, u32[]{:S(2)}, u32[]{:S(2)}) collective-permute-start(bf16[128,2048]{1,0:T(8,128)(2,1)} %get-tuple-element.294), channel_id=1, source_target_pairs={{0,24},{8,16},{16,8},{24,0},{1,25},{9,17},{17,9},{25,1},{2,26},{10... | collective-permute-start | bytes 1572872 | tf_op jit(solution)/shard_map/cond/branch_1_fun/ppermute | solution.py:200
  535.6 1.2 collective-permute-start.34
  587.8 17.4 %copy-start.24 = (bf16[256,2048]{1,0:T(8,128)(2,1)S(1)}, bf16[256,2048]{1,0:T(8,128)(2,1)}, u32[]{:S(2)}) copy-start(bf16[256,2048]{1,0:T(8,128)(2,1)} %reduce-scatter.6.cloned.1.call-done) | copy-start | bytes 3145732
  587.8 16.2 %all-to-all-start.7 = ((bf16[8,64,768]{2,1,0:T(8,128)(2,1)}), bf16[8,64,768]{2,1,0:T(8,128)(2,1)S(1)}, u32[]{:S(2)}, u32[]{:S(2)}) async-start(bf16[8,64,768]{2,1,0:T(8,128)(2,1)} %reduce_sum.88), calls=%async_computation.8 | async-start | bytes 1572864 | tf_op jit(solution)/shard_map/all_to_all | solution.py:804
  593.6 4.5 collective-permute-start.4
  598.1 5.1 collective-permute-start.5
  (20 other events, 84.3 us)
Sparse Core Ops, SparseCore 0:
  9.6 30.6 all-gather.3
  42.1 67.5 all-gather.5
  190.2 81.6 all-gather.7
  415.5 85.2 reduce-scatter.3
  504.2 64.7 reduce-scatter.5
  577.6 26.9 reduce-scatter.7

commit v4 on v3

--- a/solution.py
+++ b/solution.py
@@ -717,11 +717,10 @@
     if chips == 4:
         gate20, up10 = pair_products(mlp_in, gate_low, up_low, chip, chips, ((2, 0), (1, 0)))
         rows = gate20.shape[0] // 2
-        gate_in, up_in = gate_in.astype(FULL), up_in.astype(FULL)
-        gate2 = (gate20[:rows].astype(FULL) + gate_in[:rows]).astype(LOW)
-        gate0 = gate20[rows:].astype(FULL) + gate_in[rows:]
-        up1 = (up10[:rows].astype(FULL) + up_in[rows:]).astype(LOW)
-        up0 = up10[rows:].astype(FULL) + up_in[:rows]
+        gate2 = (gate20[:rows].astype(FULL) + gate_in[:rows].astype(FULL)).astype(LOW)
+        up1 = (up10[:rows].astype(FULL) + up_in[rows:].astype(FULL)).astype(LOW)
+        gate0 = gate20[rows:].astype(FULL) + gate_in[rows:].astype(FULL)
+        up0 = up10[rows:].astype(FULL) + up_in[:rows].astype(FULL)
         gate_sum = (gate0 + swap_with(gate2, "chip", 2).astype(FULL)).astype(LOW)
         up_sum = (up0 + swap_with(up1, "chip", 1).astype(FULL)).astype(LOW)
     else:

time: 623 us -> 621 us (level)
  transfers between devices with their start and end apart: 55 -> 55, of which waited for: 34 -> 34; matrix products, arithmetic and copies ran while one was open for 16% -> 15% of each run, Pallas kernels for 13% -> 13%
where the time goes in v4:
time: 621 us; the launch traced here: 614 us
  waiting for transfers between devices  279 us (45%)
  Pallas kernels  116 us (19%)
  starting transfers between devices  73.6 us (12%)
  other arithmetic  56.2 us (9%)
  matrix products  31.5 us (5%)
  local copies, waits for them, and re-layouts  25.9 us (4%)
  blocking collectives  15.6 us (3%)
  between operations  14.9 us (2%)
    ppermute x40, waiting for transfers between devices, swap_with(): return lax.ppermute(value, axis, [(i, i ^ code) for i in range(count)])  224 us
    dot_general x8, matrix products, matmul(): lax.dot_general(left, right, (((left_dim,), (right_dim,)), ((), ())), pre...  31.5 us
    ppermute x40, starting transfers between devices, swap_with(): return lax.ppermute(value, axis, [(i, i ^ code) for i in range(count)])  28.3 us
    pallas_call x1, Pallas kernels, expand(): pl.pallas_call(expand_kernel, grid=(hidden // tile,), in_specs=[once] * 4...  20.3 us
    pallas_call x2, Pallas kernels, pair_products(): pl.pallas_call(pair_kernel, grid_spec=pltpu.PrefetchScalarGridSpec(num_sc...  18.6 us
    pallas_call x2, Pallas kernels, contract(): pl.pallas_call(contract_kernel, grid=(width // tile,), in_specs=[rows, ro...  17.6 us
    all_to_all x1, blocking collectives, local(): lax.all_to_all(after(packed_heads, spread), RANKS, 0, 0, tiled=True)  15.6 us
    all_to_all x1, waiting for transfers between devices, local(): column_sum = lax.all_to_all(column_sum, ('core', 'fsdp'), 0, 0, tiled=True)  15.2 us
  transfers between devices with their start and end apart: 55, of which 34 were waited for; matrix products, arithmetic and copies ran while one was open for 15% of the time, Pallas kernels for 13%

profile of v4, /device:TPU:0, one launch (start us, length us, event | category | flops | bytes accessed | tf_op | source)
XLA Modules:
  0.0 613.8 jit_solution(3917017893261363966)
XLA Ops:
  9.3 7.3 %all-to-all-start = ((f32[32,1,128]{2,1,0:T(1,128)}), f32[32,1,128]{2,1,0:T(1,128)S(1)}, u32[]{:S(2)}, u32[]{:S(2)}) async-start(f32[32,1,128]{2,1,0:T(1,128)} %broadcast_in_dim.15), calls=%async_computation | async-start | bytes 32768 | tf_op jit(solution)/shard_map/all_to_all | solution.py:294
  19.8 3.9 all-to-all-done
  23.7 15.6 %all_to_all.44 = bf16[8,64,768]{2,1,0:T(8,128)(2,1)} all-to-all(bf16[8,64,768]{2,1,0:T(8,128)(2,1)S(1)} %shard_map.221), channel_id=1, replica_groups=mesh['chip'=4,'core'=2,'fsdp'=4] {'chip','core'}, dimensions={0} | all-to-all | bytes 1572864 | tf_op jit(solution)/shard_map/all_to_all | solution.py:656
  42.0 63.3 %conditional.6 = (bf16[2048,768]{1,0:T(8,128)(2,1)}, bf16[1024,2048]{1,0:T(8,128)(2,1)}, bf16[512,2048]{1,0:T(8,128)(2,1)}, f32[512,1]{0,1:T(1,128)S(1)}) conditional(s32[]{:T(128)} %bitcast.11, () %tuple.81, (s32[]{:T(128)}, bf16[8,64,768]{2,1,0:T(8,128)(2,1)}, bf16[128,2048]{1,0:T(8,128)(2,1)}, f32[32,64]{1,0:T(8,128)S(1)}) %tuple.84), branch_computations={%region_0.0_spmd, %region_1.3_spmd} | conditional | flops 15074309 | bytes 46445056 | solution.py:195
  47.9 17.1 %collective-permute-done.10.refs_1_ = bf16[128,2048]{1,0:T(8,128)(2,1)S(1)} collective-permute-done((bf16[128,2048]{1,0:T(8,128)(2,1)}, bf16[128,2048]{1,0:T(8,128)(2,1)S(1)}, u32[]{:S(2)}, u32[]{:S(2)}) %collective-permute-start.10) | collective-permute-done | bytes 524320 | tf_op jit(solution)/shard_map/cond/branch_1_fun/ppermute | solution.py:200
  65.0 4.6 collective-permute-done.11.refs_2_
  69.5 10.7 %collective-permute-done.12.refs_3_ = bf16[128,2048]{1,0:T(8,128)(2,1)S(1)} collective-permute-done((bf16[128,2048]{1,0:T(8,128)(2,1)}, bf16[128,2048]{1,0:T(8,128)(2,1)S(1)}, u32[]{:S(2)}, u32[]{:S(2)}) %collective-permute-start.12) | collective-permute-done | bytes 524320 | tf_op jit(solution)/shard_map/cond/branch_1_fun/ppermute | solution.py:200
  89.6 3.1 fusion.2
  92.7 9.5 %collective-permute-done.9 = bf16[8,64,768]{2,1,0:T(8,128)(2,1)S(1)} collective-permute-done((bf16[8,64,768]{2,1,0:T(8,128)(2,1)S(1)}, bf16[8,64,768]{2,1,0:T(8,128)(2,1)S(1)}, u32[]{:S(2)}, u32[]{:S(2)}) %collective-permute-start.9) | collective-permute-done | bytes 786464 | tf_op jit(solution)/shard_map/cond/branch_1_fun/ppermute | solution.py:204
  102.3 3.0 branch_1_fun.7
  105.3 4.4 all-gather.6.cloned.1.call-done.down_rows.refs_0_
  109.7 4.6 all-to-all-start.2
  117.5 56.9 %conditional.7 = (bf16[1024,256]{1,0:T(8,128)(2,1)}, bf16[1024,256]{1,0:T(8,128)(2,1)}, bf16[1024,256]{1,0:T(8,128)(2,1)}, bf16[1024,256]{1,0:T(8,128)(2,1)}, f3...) conditional(s32[]{:T(128)} %bitcast.11, () %tuple.80, ...), branch_computations={%region_5.6_spmd, %region_6.8_spmd} | conditional | flops 4302569984 | bytes 49311492 | solution.py:195
  118.1 6.1 %fusion.29.qkv = f32[1024,768]{1,0:T(8,128)S(1)} fusion(bf16[1024,2048]{1,0:T(8,128)(2,1)} %get-tuple-element.91, bf16[2048,768]{1,0:T(8,128)(2,1)} %get-tuple-element.92), kind=kOutput, calls=%fused_computation.90 | convolution fusion | flops 3221225472 | bytes 10485760 | tf_op jit(solution)/shard_map/cond/branch_1_fun/dot_general | solution.py:41
  124.3 9.4 %branch_1_fun.9 = (bf16[1024,256]{1,0:T(8,128)(2,1)}, bf16[1024,256]{1,0:T(8,128)(2,1)}, bf16[1024,256]{1,0:T(8,128)(2,1)}, bf16[1024,256]{1,0:T(8,128)(2,1)}, f32[2,8,1024]{2,1,0:T(8,128)S(1)}) custom-call(s32[16]{0:T(128)S(1)} %get-tuple-element.90.offsets, f32[1024,768]{1,0:T(8,128)S(1)} %fusion.29.qkv, f32[1024,128]{1,0:T(8,128)S(1)} %copy.32.cosine, ...), custom_call_target="tpu_custom_call" | custom-call | tf_op jit(solution)/shard_map/cond/branch_1_fun/pallas_call | solution.py:551
  136.0 3.8 collective-permute-done.17
  146.6 11.5 %collective-permute-done.18 = bf16[128,2048]{1,0:T(8,128)(2,1)} collective-permute-done((bf16[128,2048]{1,0:T(8,128)(2,1)}, bf16[128,2048]{1,0:T(8,128)(2,1)}, u32[]{:S(2)}, u32[]{:S(2)}) %collective-permute-start.18) | collective-permute-done | bytes 524320 | tf_op jit(solution)/shard_map/cond/branch_1_fun/ppermute | solution.py:200
  158.1 11.9 %collective-permute-done.19 = bf16[128,2048]{1,0:T(8,128)(2,1)} collective-permute-done((bf16[128,2048]{1,0:T(8,128)(2,1)}, bf16[128,2048]{1,0:T(8,128)(2,1)}, u32[]{:S(2)}, u32[]{:S(2)}) %collective-permute-start.19) | collective-permute-done | bytes 524320 | tf_op jit(solution)/shard_map/cond/branch_1_fun/ppermute | solution.py:200
  169.9 3.0 multiply_reduce_fusion
  174.4 6.0 broadcast_in_dim.18
  180.4 5.6 all-to-all-start.3
  186.8 69.8 %conditional.8 = (bf16[512,2048]{1,0:T(8,128)(2,1)}, bf16[512,2048]{1,0:T(8,128)(2,1)}) conditional(s32[]{:T(128)} %bitcast.11, () %tuple.88, (s32[]{:T(128)}, bf16[128,2048]{1,0:T(8,128)(2,1)S(1)}) %tuple.91), branch_computations={%region_8.9_spmd, %region_9.10_spmd} | conditional | bytes 16777420 | solution.py:195
  192.0 36.0 %collective-permute-done.refs_1_ = bf16[128,2048]{1,0:T(8,128)(2,1)S(1)} collective-permute-done((bf16[128,2048]{1,0:T(8,128)(2,1)}, bf16[128,2048]{1,0:T(8,128)(2,1)S(1)}, u32[]{:S(2)}, u32[]{:S(2)}) %collective-permute-start) | collective-permute-done | bytes 524320 | tf_op jit(solution)/shard_map/cond/branch_1_fun/ppermute | solution.py:200
  229.3 19.8 %collective-permute-done.2.refs_3_ = bf16[128,2048]{1,0:T(8,128)(2,1)S(1)} collective-permute-done((bf16[128,2048]{1,0:T(8,128)(2,1)}, bf16[128,2048]{1,0:T(8,128)(2,1)S(1)}, u32[]{:S(2)}, u32[]{:S(2)}) %collective-permute-start.2) | collective-permute-done | bytes 524320 | tf_op jit(solution)/shard_map/cond/branch_1_fun/ppermute | solution.py:200
  251.6 4.5 collective-permute-done.3
  256.6 14.3 %all-gather.8.cloned.1.call-done.near = bf16[512,2048]{1,0:T(8,128)(2,1)} async-done(((bf16[128,2048]{1,0:T(8,128)(2,1)}), bf16[512,2048]{1,0:T(8,128)(2,1)}) %all-gather.8.cloned.1.call-update) | async-done | bytes 2097168 | tf_op jit(solution)/shard_map/all_gather | solution.py:689
  271.4 3.8 collective-permute-done.35.far
  275.2 2.9 all-to-all-done.3
  278.1 20.3 %shard_map.223 = (bf16[1024,2048]{1,0:T(8,128)(2,1)}, bf16[1024,1024]{1,0:T(8,128)(2,1)}, bf16[1024,1024]{1,0:T(8,128)(2,1)}, bf16[1024,1024]{1,0:T(8,128)(2,1)}) custom-call(bf16[512,2048]{1,0:T(8,128)(2,1)} %get-tuple-element.206.near_in, bf16[512,2048]{1,0:T(8,128)(2,1)} %get-tuple-element.207.far_in, ...), custom_call_target="tpu_custom_call" | custom-call | tf_op jit(solution)/shard_map/pallas_call | solution.py:126
  298.5 9.3 %shard_map.224 = (bf16[1024,1024]{1,0:T(8,128)(2,1)}, bf16[1024,1024]{1,0:T(8,128)(2,1)}) custom-call(s32[4]{0:T(128)} %get-tuple-element.311.order, bf16[1024,2048]{1,0:T(8,128)(2,1)} %get-tuple-element.213.left.right, bf16[1024,2048]{1,0:T(8,128)(2,1)} %get-tuple-element.213.left.right, bf16[1024,1024]{1,0:T(8,128)(2,1)} %get-tuple-element.221.gate_low.left, ...), custom_call_target="tpu_custom_call" | custom-call | tf_op jit(solution)/shard_map/pallas_call | solution.py:150
  307.8 8.8 %shard_map.226 = bf16[512,2048]{1,0:T(8,128)(2,1)} custom-call(bf16[1024,1024]{1,0:T(8,128)(2,1)} %get-tuple-element.221.gate_low.left, bf16[1024,1024]{1,0:T(8,128)(2,1)} %get-tuple-element.222.up_low.right, bf16[2048,2048]{1,0:T(8,128)(2,1)} %bitcast.20.gate_cols.up_cols.cols), custom_call_target="tpu_custom_call" | custom-call | tf_op jit(solution)/shard_map/pallas_call | solution.py:179
  318.5 8.8 %shard_map.225 = bf16[512,2048]{1,0:T(8,128)(2,1)} custom-call(bf16[1024,1024]{1,0:T(8,128)(2,1)} %get-tuple-element.221.gate_low.left, bf16[1024,1024]{1,0:T(8,128)(2,1)} %get-tuple-element.222.up_low.right, bf16[2048,2048]{1,0:T(8,128)(2,1)} %bitcast.20.gate_cols.up_cols.cols), custom_call_target="tpu_custom_call" | custom-call | tf_op jit(solution)/shard_map/pallas_call | solution.py:179
  327.3 3.8 add_convert_fusion.2
  331.2 9.0 %all-to-all-start.4 = ((bf16[4,128,2048]{2,1,0:T(8,128)(2,1)}), bf16[4,128,2048]{2,1,0:T(8,128)(2,1)}, u32[]{:S(2)}, u32[]{:S(2)}) async-start(bf16[4,128,2048]{2,1,0:T(8,128)(2,1)} %bitcast.62), calls=%async_computation.4 | async-start | bytes 4194304 | tf_op jit(solution)/shard_map/all_to_all | solution.py:286
  341.9 5.8 shard_map.228
  347.7 9.3 %shard_map.229 = (bf16[1024,1024]{1,0:T(8,128)(2,1)}, bf16[1024,1024]{1,0:T(8,128)(2,1)}) custom-call(s32[4]{0:T(128)} %get-tuple-element.310.order, bf16[1024,2048]{1,0:T(8,128)(2,1)} %get-tuple-element.213.left.right, bf16[1024,2048]{1,0:T(8,128)(2,1)} %get-tuple-element.213.left.right, bf16[1024,1024]{1,0:T(8,128)(2,1)} %get-tuple-element.221.gate_low.left, ...), custom_call_target="tpu_custom_call" | custom-call | tf_op jit(solution)/shard_map/pallas_call | solution.py:150
  357.1 7.9 %collective-permute-done.38 = bf16[1024,1024]{1,0:T(8,128)(2,1)} collective-permute-done((bf16[1024,1024]{1,0:T(8,128)(2,1)}, bf16[1024,1024]{1,0:T(8,128)(2,1)}, u32[]{:S(2)}, u32[]{:S(2)}) %collective-permute-start.38) | collective-permute-done | bytes 2097184 | tf_op jit(solution)/shard_map/ppermute | solution.py:200
  364.9 2.9 add_convert_fusion.6
  372.5 6.0 shard_map.227
  378.5 14.4 %collective-permute-done.39 = bf16[512,1024]{1,0:T(8,128)(2,1)} collective-permute-done((bf16[512,1024]{1,0:T(8,128)(2,1)}, bf16[512,1024]{1,0:T(8,128)(2,1)}, u32[]{:S(2)}, u32[]{:S(2)}) %collective-permute-start.39) | collective-permute-done | bytes 1048608 | tf_op jit(solution)/shard_map/ppermute | solution.py:200
  401.3 3.8 add_convert_fusion.1
  411.8 7.6 %all-to-all-start.5 = ((bf16[8,64,2048]{2,1,0:T(8,128)(2,1)}), bf16[8,64,2048]{2,1,0:T(8,128)(2,1)S(1)}, u32[]{:S(2)}, u32[]{:S(2)}) async-start(bf16[8,64,2048]{2,1,0:T(8,128)(2,1)} %bitcast.63), calls=%async_computation.6 | async-start | bytes 4194304 | tf_op jit(solution)/shard_map/all_to_all | solution.py:742
  419.5 59.3 %conditional.9 = (bf16[1024,2048]{1,0:T(8,128)(2,1)}, bf16[256,2048]{0,1:T(8,128)(2,1)}, bf16[1024,768]{1,0:T(8,128)(2,1)}) conditional(s32[]{:T(128)} %bitcast.11, () %tuple.103, (bf16[1024,1024]{1,0:T(8,128)(2,1)}, bf16[512,2048]{1,0:T(8,128)(2,1)}, bf16[512,2048]{1,0:T(8,128)(2,1)}, bf16[128,2048]{1,0:T(8,128)(2,1)}, ...), branch_computations={%region_13.14_spmd, %region_14.15_spmd} | conditional | flops 2148270080 | bytes 36700548 | solution.py:195
  423.3 11.6 %collective-permute-done.21.refs_1_ = bf16[128,2048]{1,0:T(8,128)(2,1)} collective-permute-done((bf16[128,2048]{1,0:T(8,128)(2,1)}, bf16[128,2048]{1,0:T(8,128)(2,1)}, u32[]{:S(2)}, u32[]{:S(2)}) %collective-permute-start.21) | collective-permute-done | bytes 524320 | tf_op jit(solution)/shard_map/cond/branch_1_fun/ppermute | solution.py:200
  434.8 12.0 %collective-permute-done.22.refs_2_ = bf16[128,2048]{1,0:T(8,128)(2,1)} collective-permute-done((bf16[128,2048]{1,0:T(8,128)(2,1)}, bf16[128,2048]{1,0:T(8,128)(2,1)}, u32[]{:S(2)}, u32[]{:S(2)}) %collective-permute-start.22) | collective-permute-done | bytes 524320 | tf_op jit(solution)/shard_map/cond/branch_1_fun/ppermute | solution.py:200
  448.7 8.8 %branch_1_fun.11 = bf16[1024,2048]{1,0:T(8,128)(2,1)} custom-call(bf16[1024,1024]{1,0:T(8,128)(2,1)} %get-tuple-element.106.left, bf16[512,2048]{1,0:T(8,128)(2,1)} %get-tuple-element.107.near, bf16[512,2048]{1,0:T(8,128)(2,1)} %get-tuple-element.108.far), custom_call_target="tpu_custom_call" | custom-call | tf_op jit(solution)/shard_map/cond/branch_1_fun/pallas_call | solution.py:83
  461.3 3.4 fusion.9
  464.6 13.9 %branch_1_fun.13 = bf16[1024,768]{1,0:T(8,128)(2,1)} custom-call(s32[16]{0:T(128)S(1)} %get-tuple-element.111.offsets, bf16[1024,256]{1,0:T(8,128)(2,1)S(1)} %convolution_convert_fusion.2.upstream, bf16[1024,256]{1,0:T(8,128)(2,1)} %get-tuple-element.113.query_in, bf16[1024,256]{1,0:T(8,128)(2,1)} %get-tuple-element.114.key_in, ...), custom_call_target="tpu_custom_call" | custom-call | tf_op jit(solution)/shard_map/cond/branch_1_fun/pallas_call | solution.py:579
  478.8 7.9 %convolution_convert_fusion.4 = bf16[2048,768]{1,0:T(8,128)(2,1)} fusion(bf16[1024,2048]{1,0:T(8,128)(2,1)} %get-tuple-element.198, bf16[1024,768]{1,0:T(8,128)(2,1)} %get-tuple-element.235), kind=kOutput, calls=%fused_computation.40 | convolution fusion | flops 3222798336 | bytes 8912896 | tf_op jit(solution)/shard_map/dot_general | solution.py:41
  486.7 15.2 %all-to-all-done.5.packed = bf16[8,64,2048]{2,1,0:T(8,128)(2,1)S(1)} async-done(((bf16[8,64,2048]{2,1,0:T(8,128)(2,1)}), bf16[8,64,2048]{2,1,0:T(8,128)(2,1)S(1)}, u32[]{:S(2)}, u32[]{:S(2)}) %all-to-all-start.5) | async-done | bytes 2097184 | tf_op jit(solution)/shard_map/all_to_all | solution.py:742
  501.9 3.9 copy.39
  505.8 5.1 all-to-all-start.6
  511.1 61.8 %conditional.10 = (f32[128,2048]{1,0:T(8,128)}, f32[2,2048]{1,0:T(2,128)S(1)}) conditional(s32[]{:T(128)} %bitcast.11, () %tuple.102, (f32[512,1]{0,1:T(1,128)S(1)}, bf16[1024,768]{1,0:T(8,128)(2,1)}, bf16[2048,768]{1,0:T(8,128)(2,1)}, f32[32,64]{1,0:T(8,128)S(1)}, f32[128,2048]{1,0:T(8,128)}, /*index=5*/bf16[512,2048]{1,0:T(8,128)(2,1)}, ...), branch_computations={%region_15.16_spmd, %region_16.20_spmd} | conditional | flops 3236192512 | bytes 53402436 | solution.py:195
  511.2 4.0 convolution_convert_fusion.3
  519.4 5.1 multiply_reduce_fusion.1
  534.8 13.1 %collective-permute-done.29 = bf16[128,2048]{1,0:T(8,128)(2,1)S(1)} collective-permute-done((bf16[128,2048]{1,0:T(8,128)(2,1)}, bf16[128,2048]{1,0:T(8,128)(2,1)S(1)}, u32[]{:S(2)}, u32[]{:S(2)}) %collective-permute-start.29) | collective-permute-done | bytes 524320 | tf_op jit(solution)/shard_map/cond/branch_1_fun/ppermute | solution.py:200
  547.9 4.3 collective-permute-done.30
  552.1 15.9 %collective-permute-done.31 = bf16[128,2048]{1,0:T(8,128)(2,1)} collective-permute-done((bf16[128,2048]{1,0:T(8,128)(2,1)}, bf16[128,2048]{1,0:T(8,128)(2,1)}, u32[]{:S(2)}, u32[]{:S(2)}) %collective-permute-start.31) | collective-permute-done | bytes 524320 | tf_op jit(solution)/shard_map/cond/branch_1_fun/ppermute | solution.py:200
  570.0 3.0 multiply_subtract_fusion
  582.2 3.5 reduce_sum.88
  585.7 3.7 all-to-all-start.7
  591.6 9.7 %conditional.11 = (f32[2,2048]{1,0:T(2,128)S(1)}) conditional(s32[]{:T(128)} %bitcast.11, () %tuple.108, f32[2,2048]{1,0:T(2,128)S(1)} %get-tuple-element.241), branch_computations={%region_21.22_spmd, %region_22.23_spmd} | conditional | flops 8192 | bytes 229464 | solution.py:195
  591.6 4.5 collective-permute-done.4
  596.2 5.1 collective-permute-done.5
  (206 shorter events, 113.1 us)
Async XLA Ops:
  7.2 33.1 %all-gather.4.cloned.1.call-start = ((), (), s32[]{:S(2)}) async-start(), calls=%async_computation.11 | async-start | bytes 1310720 | tf_op jit(solution)/shard_map/all_gather | solution.py:653
  9.3 14.4 %all-to-all-start = ((f32[32,1,128]{2,1,0:T(1,128)}), f32[32,1,128]{2,1,0:T(1,128)S(1)}, u32[]{:S(2)}, u32[]{:S(2)}) async-start(f32[32,1,128]{2,1,0:T(1,128)} %broadcast_in_dim.15), calls=%async_computation | async-start | bytes 32768 | tf_op jit(solution)/shard_map/all_to_all | solution.py:294
  16.6 23.7 %copy-start = (bf16[64,8192]{1,0:T(8,128)(2,1)S(1)}, bf16[64,8192]{1,0:T(8,128)(2,1)}, u32[]{:S(2)}) copy-start(bf16[64,8192]{1,0:T(8,128)(2,1)} %gate.1) | copy-start | bytes 3145732
  16.6 23.7 %copy-start.1 = (bf16[64,8192]{1,0:T(8,128)(2,1)S(1)}, bf16[64,8192]{1,0:T(8,128)(2,1)}, u32[]{:S(2)}) copy-start(bf16[64,8192]{1,0:T(8,128)(2,1)} %up.1) | copy-start | bytes 3145732
  16.6 93.1 %all-gather.6.cloned.1.call-start = ((), (), s32[]{:S(2)}) async-start(), calls=%async_computation.12 | async-start | bytes 5242880 | tf_op jit(solution)/shard_map/all_gather | solution.py:659
  19.7 20.6 %copy-start.25 = (s32[1,4]{1,0:T(1,128)S(1)}, s32[1,4]{1,0:T(1,128)}, u32[]{:S(2)}) copy-start(s32[1,4]{1,0:T(1,128)} %param.27) | copy-start | bytes 52
  42.0 38.3 %collective-permute-start.6 = (bf16[8,64,768]{2,1,0:T(8,128)(2,1)}, bf16[8,64,768]{2,1,0:T(8,128)(2,1)S(1)}, u32[]{:S(2)}, u32[]{:S(2)}) collective-permute-start(bf16[8,64,768]{2,1,0:T(8,128)(2,1)} %get-tuple-element.87.refs_0_), channel_id=1, source_target_pairs={{0,1},{1,0},{2,3},{3,2},{4,5},{5,4},{6,7},{7,6},{8,9},{9,8},{10,11... | collective-permute-start | bytes 2359304 | tf_op jit(solution)/shard_map/cond/branch_1_fun/ppermute | solution.py:200
  43.4 21.6 %collective-permute-start.10 = (bf16[128,2048]{1,0:T(8,128)(2,1)}, bf16[128,2048]{1,0:T(8,128)(2,1)S(1)}, u32[]{:S(2)}, u32[]{:S(2)}) collective-permute-start(bf16[128,2048]{1,0:T(8,128)(2,1)} %get-tuple-element.88.refs_0_), channel_id=1, source_target_pairs={{0,8},{8,0},{16,24},{24,16},{1,9},{9,1},{17,25},{25,17},{2,10},{10... | collective-permute-start | bytes 1572872 | tf_op jit(solution)/shard_map/cond/branch_1_fun/ppermute | solution.py:200
  44.9 24.7 %collective-permute-start.11 = (bf16[128,2048]{1,0:T(8,128)(2,1)}, bf16[128,2048]{1,0:T(8,128)(2,1)S(1)}, u32[]{:S(2)}, u32[]{:S(2)}) collective-permute-start(bf16[128,2048]{1,0:T(8,128)(2,1)} %get-tuple-element.88.refs_0_), channel_id=1, source_target_pairs={{0,16},{8,24},{16,0},{24,8},{1,17},{9,25},{17,1},{25,9},{2,18},{10... | collective-permute-start | bytes 1572872 | tf_op jit(solution)/shard_map/cond/branch_1_fun/ppermute | solution.py:200
  46.4 33.9 %collective-permute-start.12 = (bf16[128,2048]{1,0:T(8,128)(2,1)}, bf16[128,2048]{1,0:T(8,128)(2,1)S(1)}, u32[]{:S(2)}, u32[]{:S(2)}) collective-permute-start(bf16[128,2048]{1,0:T(8,128)(2,1)} %get-tuple-element.88.refs_0_), channel_id=1, source_target_pairs={{0,24},{8,16},{16,8},{24,0},{1,25},{9,17},{17,9},{25,1},{2,26},{10... | collective-permute-start | bytes 1572872 | tf_op jit(solution)/shard_map/cond/branch_1_fun/ppermute | solution.py:200
  46.9 35.9 %collective-permute-start.7 = (bf16[8,64,768]{2,1,0:T(8,128)(2,1)}, bf16[8,64,768]{2,1,0:T(8,128)(2,1)S(1)}, u32[]{:S(2)}, u32[]{:S(2)}) collective-permute-start(bf16[8,64,768]{2,1,0:T(8,128)(2,1)} %get-tuple-element.87.refs_0_), channel_id=1, source_target_pairs={{0,2},{1,3},{2,0},{3,1},{4,6},{5,7},{6,4},{7,5},{8,10},{9,11},{10,... | collective-permute-start | bytes 2359304 | tf_op jit(solution)/shard_map/cond/branch_1_fun/ppermute | solution.py:200
  65.0 19.2 %collective-permute-start.13 = (bf16[128,2048]{1,0:T(8,128)(2,1)}, bf16[128,2048]{1,0:T(8,128)(2,1)}, u32[]{:S(2)}, u32[]{:S(2)}) collective-permute-start(bf16[128,2048]{1,0:T(8,128)(2,1)} %get-tuple-element.88.refs_0_), channel_id=1, source_target_pairs={{0,4},{4,0},{1,5},{5,1},{2,6},{6,2},{3,7},{7,3},{8,12},{12,8},{9,1... | collective-permute-start | bytes 1572872 | tf_op jit(solution)/shard_map/cond/branch_1_fun/ppermute | solution.py:200
  69.5 15.3 %collective-permute-start.14 = (bf16[128,2048]{1,0:T(8,128)(2,1)S(1)}, bf16[128,2048]{1,0:T(8,128)(2,1)}, u32[]{:S(2)}, u32[]{:S(2)}) collective-permute-start(bf16[128,2048]{1,0:T(8,128)(2,1)S(1)} %collective-permute-done.10.refs_1_), channel_id=1, source_target_pairs={{0,4},{4,0},{1,5},{5,1},{2,6},{6,2},{3,7},{7,3},{8,12},{12,8},{9,1... | collective-permute-start | bytes 1572872 | tf_op jit(solution)/shard_map/cond/branch_1_fun/ppermute | solution.py:200
  80.3 4.6 collective-permute-start.15
  80.3 4.6 collective-permute-start.16
  82.8 19.3 %collective-permute-start.9 = (bf16[8,64,768]{2,1,0:T(8,128)(2,1)S(1)}, bf16[8,64,768]{2,1,0:T(8,128)(2,1)S(1)}, u32[]{:S(2)}, u32[]{:S(2)}) collective-permute-start(bf16[8,64,768]{2,1,0:T(8,128)(2,1)S(1)} %collective-permute-done.7.refs_2_), channel_id=1, source_target_pairs={{2,3},{1,0},{6,7},{5,4},{10,11},{9,8},{14,15},{13,12},{18,19},{17,... | collective-permute-start | bytes 2359304 | tf_op jit(solution)/shard_map/cond/branch_1_fun/ppermute | solution.py:204
  84.1 8.5 %collective-permute-start.8 = (bf16[8,64,768]{2,1,0:T(8,128)(2,1)}, bf16[8,64,768]{2,1,0:T(8,128)(2,1)S(1)}, u32[]{:S(2)}, u32[]{:S(2)}) collective-permute-start(bf16[8,64,768]{2,1,0:T(8,128)(2,1)} %get-tuple-element.87.refs_0_), channel_id=1, source_target_pairs={{1,2},{2,1},{5,6},{6,5},{9,10},{10,9},{13,14},{14,13},{17,18},{18,... | collective-permute-start | bytes 2359304 | tf_op jit(solution)/shard_map/cond/branch_1_fun/ppermute | solution.py:204
  109.7 64.7 %all-to-all-start.2 = ((bf16[8,64,2048]{2,1,0:T(8,128)(2,1)}), bf16[8,64,2048]{2,1,0:T(8,128)(2,1)}, u32[]{:S(2)}, u32[]{:S(2)}) async-start(bf16[8,64,2048]{2,1,0:T(8,128)(2,1)} %shard_map.222), calls=%async_computation.2 | async-start | bytes 4194304 | tf_op jit(solution)/shard_map/all_to_all | solution.py:673
  135.4 4.3 collective-permute-start.17
  143.0 15.1 %collective-permute-start.18 = (bf16[128,2048]{1,0:T(8,128)(2,1)}, bf16[128,2048]{1,0:T(8,128)(2,1)}, u32[]{:S(2)}, u32[]{:S(2)}) collective-permute-start(bf16[128,2048]{1,0:T(8,128)(2,1)} %get-tuple-element.298), channel_id=1, source_target_pairs={{0,8},{8,0},{16,24},{24,16},{1,9},{9,1},{17,25},{25,17},{2,10},{10... | collective-permute-start | bytes 1572872 | tf_op jit(solution)/shard_map/cond/branch_1_fun/ppermute | solution.py:200
  144.5 25.5 %collective-permute-start.19 = (bf16[128,2048]{1,0:T(8,128)(2,1)}, bf16[128,2048]{1,0:T(8,128)(2,1)}, u32[]{:S(2)}, u32[]{:S(2)}) collective-permute-start(bf16[128,2048]{1,0:T(8,128)(2,1)} %get-tuple-element.300), channel_id=1, source_target_pairs={{0,16},{8,24},{16,0},{24,8},{1,17},{9,25},{17,1},{25,9},{2,18},{10... | collective-permute-start | bytes 1572872 | tf_op jit(solution)/shard_map/cond/branch_1_fun/ppermute | solution.py:200
  145.0 24.9 %collective-permute-start.20 = (bf16[128,2048]{1,0:T(8,128)(2,1)}, bf16[128,2048]{1,0:T(8,128)(2,1)}, u32[]{:S(2)}, u32[]{:S(2)}) collective-permute-start(bf16[128,2048]{1,0:T(8,128)(2,1)} %get-tuple-element.299), channel_id=1, source_target_pairs={{0,24},{8,16},{16,8},{24,0},{1,25},{9,17},{17,9},{25,1},{2,26},{10... | collective-permute-start | bytes 1572872 | tf_op jit(solution)/shard_map/cond/branch_1_fun/ppermute | solution.py:200
  180.4 97.7 %all-to-all-start.3 = ((bf16[4,512,2048]{2,1,0:T(8,128)(2,1)}), bf16[4,512,2048]{2,1,0:T(8,128)(2,1)}, u32[]{:S(2)}, u32[]{:S(2)}) async-start(bf16[4,512,2048]{2,1,0:T(8,128)(2,1)} %broadcast_in_dim.18), calls=%async_computation.3 | async-start | bytes 16777216 | tf_op jit(solution)/shard_map/all_to_all | solution.py:280
  186.0 84.8 %all-gather.8.cloned.1.call-start = ((), (), s32[]{:S(2)}) async-start(), calls=%async_computation.13 | async-start | bytes 2621440 | tf_op jit(solution)/shard_map/all_gather | solution.py:689
  186.8 84.1 %copy-start.23 = (s32[4]{0:T(128)S(1)}, s32[4]{0:T(128)}, u32[]{:S(2)}) copy-start(s32[4]{0:T(128)} %constant.128.clone) | copy-start | bytes 52
  186.8 84.1 %copy-start.24 = (s32[4]{0:T(128)S(1)}, s32[4]{0:T(128)}, u32[]{:S(2)}) copy-start(s32[4]{0:T(128)} %constant.129.clone) | copy-start | bytes 52
  187.6 40.4 %collective-permute-start = (bf16[128,2048]{1,0:T(8,128)(2,1)}, bf16[128,2048]{1,0:T(8,128)(2,1)S(1)}, u32[]{:S(2)}, u32[]{:S(2)}) collective-permute-start(bf16[128,2048]{1,0:T(8,128)(2,1)} %copy-done.18), channel_id=1, source_target_pairs={{0,1},{1,0},{2,3},{3,2},{4,5},{5,4},{6,7},{7,6},{8,9},{9,8},{10,11... | collective-permute-start | bytes 1572872 | tf_op jit(solution)/shard_map/cond/branch_1_fun/ppermute | solution.py:200
  189.3 40.0 %collective-permute-start.1 = (bf16[128,2048]{1,0:T(8,128)(2,1)}, bf16[128,2048]{1,0:T(8,128)(2,1)S(1)}, u32[]{:S(2)}, u32[]{:S(2)}) collective-permute-start(bf16[128,2048]{1,0:T(8,128)(2,1)} %copy-done.18), channel_id=1, source_target_pairs={{0,2},{1,3},{2,0},{3,1},{4,6},{5,7},{6,4},{7,5},{8,10},{9,11},{10,... | collective-permute-start | bytes 1572872 | tf_op jit(solution)/shard_map/cond/branch_1_fun/ppermute | solution.py:200
  191.6 57.4 %collective-permute-start.2 = (bf16[128,2048]{1,0:T(8,128)(2,1)}, bf16[128,2048]{1,0:T(8,128)(2,1)S(1)}, u32[]{:S(2)}, u32[]{:S(2)}) collective-permute-start(bf16[128,2048]{1,0:T(8,128)(2,1)} %copy-done.18), channel_id=1, source_target_pairs={{0,3},{1,2},{2,1},{3,0},{4,7},{5,6},{6,5},{7,4},{8,11},{9,10},{10,... | collective-permute-start | bytes 1572872 | tf_op jit(solution)/shard_map/cond/branch_1_fun/ppermute | solution.py:200
  251.6 4.5 collective-permute-start.3
  270.9 4.4 collective-permute-start.35
  275.2 23.2 %copy-start.7 = (bf16[512,2048]{1,0:T(8,128)(2,1)}, bf16[512,2048]{1,0:T(8,128)(2,1)S(1)}, u32[]{:S(2)}) copy-start(bf16[512,2048]{1,0:T(8,128)(2,1)S(1)} %collective-permute-done.35.far) | copy-start | bytes 6291460
  316.6 10.8 %collective-permute-start.36 = (bf16[512,2048]{1,0:T(8,128)(2,1)}, bf16[512,2048]{1,0:T(8,128)(2,1)S(1)}, u32[]{:S(2)}, u32[]{:S(2)}) collective-permute-start(bf16[512,2048]{1,0:T(8,128)(2,1)} %shard_map.226), channel_id=1, source_target_pairs={{0,4},{4,0},{1,5},{5,1},{2,6},{6,2},{3,7},{7,3},{8,12},{12,8},{9,1... | collective-permute-start | bytes 6291464 | tf_op jit(solution)/shard_map/ppermute | solution.py:200
  316.6 48.4 %collective-permute-start.38 = (bf16[1024,1024]{1,0:T(8,128)(2,1)}, bf16[1024,1024]{1,0:T(8,128)(2,1)}, u32[]{:S(2)}, u32[]{:S(2)}) collective-permute-start(bf16[1024,1024]{1,0:T(8,128)(2,1)} %get-tuple-element.215), channel_id=1, source_target_pairs={{0,8},{8,0},{16,24},{24,16},{1,9},{9,1},{17,25},{25,17},{2,10},{10... | collective-permute-start | bytes 6291464 | tf_op jit(solution)/shard_map/ppermute | solution.py:200
  318.0 51.3 %collective-permute-start.40 = (bf16[1024,1024]{1,0:T(8,128)(2,1)}, bf16[1024,1024]{1,0:T(8,128)(2,1)}, u32[]{:S(2)}, u32[]{:S(2)}) collective-permute-start(bf16[1024,1024]{1,0:T(8,128)(2,1)} %get-tuple-element.217), channel_id=1, source_target_pairs={{0,16},{8,24},{16,0},{24,8},{1,17},{9,25},{17,1},{25,9},{2,18},{10... | collective-permute-start | bytes 6291464 | tf_op jit(solution)/shard_map/ppermute | solution.py:200
  331.2 73.9 %all-to-all-start.4 = ((bf16[4,128,2048]{2,1,0:T(8,128)(2,1)}), bf16[4,128,2048]{2,1,0:T(8,128)(2,1)}, u32[]{:S(2)}, u32[]{:S(2)}) async-start(bf16[4,128,2048]{2,1,0:T(8,128)(2,1)} %bitcast.62), calls=%async_computation.4 | async-start | bytes 4194304 | tf_op jit(solution)/shard_map/all_to_all | solution.py:286
  340.2 161.7 %reduce-scatter.4.cloned.1.call-start = ((), (), s32[]{:S(2)}) async-start(), calls=%async_computation.14 | async-start | bytes 2621440 | tf_op jit(solution)/shard_map/reduce_scatter | solution.py:743
  347.7 52.7 %collective-permute-start.37 = (bf16[512,2048]{1,0:T(8,128)(2,1)}, bf16[512,2048]{1,0:T(8,128)(2,1)}, u32[]{:S(2)}, u32[]{:S(2)}) collective-permute-start(bf16[512,2048]{1,0:T(8,128)(2,1)} %shard_map.228), channel_id=1, source_target_pairs={{0,4},{4,0},{1,5},{5,1},{2,6},{6,2},{3,7},{7,3},{8,12},{12,8},{9,1... | collective-permute-start | bytes 6291464 | tf_op jit(solution)/shard_map/ppermute | solution.py:200
  367.8 25.1 %collective-permute-start.39 = (bf16[512,1024]{1,0:T(8,128)(2,1)}, bf16[512,1024]{1,0:T(8,128)(2,1)}, u32[]{:S(2)}, u32[]{:S(2)}) collective-permute-start(bf16[512,1024]{1,0:T(8,128)(2,1)} %add_convert_fusion.6), channel_id=1, source_target_pairs={{0,16},{8,24},{16,0},{24,8},{1,17},{9,25},{17,1},{25,9},{2,18},{10... | collective-permute-start | bytes 3145736 | tf_op jit(solution)/shard_map/ppermute | solution.py:200
  371.9 24.8 %collective-permute-start.41 = (bf16[512,1024]{1,0:T(8,128)(2,1)}, bf16[512,1024]{1,0:T(8,128)(2,1)}, u32[]{:S(2)}, u32[]{:S(2)}) collective-permute-start(bf16[512,1024]{1,0:T(8,128)(2,1)} %add_convert_fusion.4), channel_id=1, source_target_pairs={{0,8},{8,0},{16,24},{24,16},{1,9},{9,1},{17,25},{25,17},{2,10},{10... | collective-permute-start | bytes 3145736 | tf_op jit(solution)/shard_map/ppermute | solution.py:200
  372.5 20.4 %copy-start.20 = (bf16[1024,1024]{1,0:T(8,128)(2,1)S(1)}, bf16[1024,1024]{1,0:T(8,128)(2,1)}, u32[]{:S(2)}) copy-start(bf16[1024,1024]{1,0:T(8,128)(2,1)} %get-tuple-element.223) | copy-start | bytes 6291460
  411.8 90.1 %all-to-all-start.5 = ((bf16[8,64,2048]{2,1,0:T(8,128)(2,1)}), bf16[8,64,2048]{2,1,0:T(8,128)(2,1)S(1)}, u32[]{:S(2)}, u32[]{:S(2)}) async-start(bf16[8,64,2048]{2,1,0:T(8,128)(2,1)} %bitcast.63), calls=%async_computation.6 | async-start | bytes 4194304 | tf_op jit(solution)/shard_map/all_to_all | solution.py:742
  419.4 153.5 %reduce-scatter.6.cloned.1.call-start = ((), (), s32[]{:S(2)}) async-start(), calls=%async_computation.15 | async-start | bytes 5242880 | tf_op jit(solution)/shard_map/reduce_scatter | solution.py:774
  419.7 27.6 %copy-start.10 = (f32[1024,128]{0,1:T(8,128)}, f32[1024,128]{0,1:T(8,128)S(1)}, u32[]{:S(2)}) copy-start(f32[1024,128]{0,1:T(8,128)S(1)} %get-tuple-element.282) | copy-start | bytes 1572868 | tf_op jit(solution)/shard_map/cond
  419.7 15.1 %collective-permute-start.21 = (bf16[128,2048]{1,0:T(8,128)(2,1)}, bf16[128,2048]{1,0:T(8,128)(2,1)}, u32[]{:S(2)}, u32[]{:S(2)}) collective-permute-start(bf16[128,2048]{1,0:T(8,128)(2,1)} %get-tuple-element.109.refs_0_), channel_id=1, source_target_pairs={{0,8},{8,0},{16,24},{24,16},{1,9},{9,1},{17,25},{25,17},{2,10},{10... | collective-permute-start | bytes 1572872 | tf_op jit(solution)/shard_map/cond/branch_1_fun/ppermute | solution.py:200
  421.2 25.5 %collective-permute-start.22 = (bf16[128,2048]{1,0:T(8,128)(2,1)}, bf16[128,2048]{1,0:T(8,128)(2,1)}, u32[]{:S(2)}, u32[]{:S(2)}) collective-permute-start(bf16[128,2048]{1,0:T(8,128)(2,1)} %get-tuple-element.109.refs_0_), channel_id=1, source_target_pairs={{0,16},{8,24},{16,0},{24,8},{1,17},{9,25},{17,1},{25,9},{2,18},{10... | collective-permute-start | bytes 1572872 | tf_op jit(solution)/shard_map/cond/branch_1_fun/ppermute | solution.py:200
  421.8 25.0 %collective-permute-start.23 = (bf16[128,2048]{1,0:T(8,128)(2,1)}, bf16[128,2048]{1,0:T(8,128)(2,1)}, u32[]{:S(2)}, u32[]{:S(2)}) collective-permute-start(bf16[128,2048]{1,0:T(8,128)(2,1)} %get-tuple-element.109.refs_0_), channel_id=1, source_target_pairs={{0,24},{8,16},{16,8},{24,0},{1,25},{9,17},{17,9},{25,1},{2,26},{10... | collective-permute-start | bytes 1572872 | tf_op jit(solution)/shard_map/cond/branch_1_fun/ppermute | solution.py:200
  423.3 34.3 %collective-permute-start.24 = (bf16[128,2048]{1,0:T(8,128)(2,1)}, bf16[128,2048]{1,0:T(8,128)(2,1)}, u32[]{:S(2)}, u32[]{:S(2)}) collective-permute-start(bf16[128,2048]{1,0:T(8,128)(2,1)} %get-tuple-element.109.refs_0_), channel_id=1, source_target_pairs={{0,4},{4,0},{1,5},{5,1},{2,6},{6,2},{3,7},{7,3},{8,12},{12,8},{9,1... | collective-permute-start | bytes 1572872 | tf_op jit(solution)/shard_map/cond/branch_1_fun/ppermute | solution.py:200
  434.8 22.8 %collective-permute-start.25 = (bf16[128,2048]{1,0:T(8,128)(2,1)}, bf16[128,2048]{1,0:T(8,128)(2,1)}, u32[]{:S(2)}, u32[]{:S(2)}) collective-permute-start(bf16[128,2048]{1,0:T(8,128)(2,1)} %collective-permute-done.21.refs_1_), channel_id=1, source_target_pairs={{0,4},{4,0},{1,5},{5,1},{2,6},{6,2},{3,7},{7,3},{8,12},{12,8},{9,1... | collective-permute-start | bytes 1572872 | tf_op jit(solution)/shard_map/cond/branch_1_fun/ppermute | solution.py:200
  446.8 10.8 %collective-permute-start.26 = (bf16[128,2048]{1,0:T(8,128)(2,1)}, bf16[128,2048]{1,0:T(8,128)(2,1)}, u32[]{:S(2)}, u32[]{:S(2)}) collective-permute-start(bf16[128,2048]{1,0:T(8,128)(2,1)} %collective-permute-done.22.refs_2_), channel_id=1, source_target_pairs={{0,4},{4,0},{1,5},{5,1},{2,6},{6,2},{3,7},{7,3},{8,12},{12,8},{9,1... | collective-permute-start | bytes 1572872 | tf_op jit(solution)/shard_map/cond/branch_1_fun/ppermute | solution.py:200
  446.8 10.8 %collective-permute-start.27 = (bf16[128,2048]{1,0:T(8,128)(2,1)}, bf16[128,2048]{1,0:T(8,128)(2,1)}, u32[]{:S(2)}, u32[]{:S(2)}) collective-permute-start(bf16[128,2048]{1,0:T(8,128)(2,1)} %collective-permute-done.23.refs_3_), channel_id=1, source_target_pairs={{0,4},{4,0},{1,5},{5,1},{2,6},{6,2},{3,7},{7,3},{8,12},{12,8},{9,1... | collective-permute-start | bytes 1572872 | tf_op jit(solution)/shard_map/cond/branch_1_fun/ppermute | solution.py:200
  505.8 76.4 %all-to-all-start.6 = ((bf16[4,8,64,768]{3,2,1,0:T(8,128)(2,1)}), bf16[4,8,64,768]{3,2,1,0:T(8,128)(2,1)}, u32[]{:S(2)}, u32[]{:S(2)}) async-start(bf16[4,8,64,768]{3,2,1,0:T(8,128)(2,1)} %bitcast.61), calls=%async_computation.7 | async-start | bytes 6291456 | tf_op jit(solution)/shard_map/all_to_all | solution.py:772
  510.9 93.8 %reduce-scatter.8.cloned.1.call-start = ((), (), s32[]{:S(2)}) async-start(), calls=%async_computation.16 | async-start | bytes 1310720 | tf_op jit(solution)/shard_map/reduce_scatter | solution.py:800
  515.1 4.2 collective-permute-start.28
  524.5 4.1 collective-permute-start.32
  528.7 4.8 collective-permute-start.33
  530.0 17.9 %collective-permute-start.29 = (bf16[128,2048]{1,0:T(8,128)(2,1)}, bf16[128,2048]{1,0:T(8,128)(2,1)S(1)}, u32[]{:S(2)}, u32[]{:S(2)}) collective-permute-start(bf16[128,2048]{1,0:T(8,128)(2,1)} %get-tuple-element.293), channel_id=1, source_target_pairs={{0,8},{8,0},{16,24},{24,16},{1,9},{9,1},{17,25},{25,17},{2,10},{10... | collective-permute-start | bytes 1572872 | tf_op jit(solution)/shard_map/cond/branch_1_fun/ppermute | solution.py:200
  531.6 20.6 %collective-permute-start.30 = (bf16[128,2048]{1,0:T(8,128)(2,1)}, bf16[128,2048]{1,0:T(8,128)(2,1)S(1)}, u32[]{:S(2)}, u32[]{:S(2)}) collective-permute-start(bf16[128,2048]{1,0:T(8,128)(2,1)} %get-tuple-element.295), channel_id=1, source_target_pairs={{0,16},{8,24},{16,0},{24,8},{1,17},{9,25},{17,1},{25,9},{2,18},{10... | collective-permute-start | bytes 1572872 | tf_op jit(solution)/shard_map/cond/branch_1_fun/ppermute | solution.py:200
  533.4 34.7 %collective-permute-start.31 = (bf16[128,2048]{1,0:T(8,128)(2,1)}, bf16[128,2048]{1,0:T(8,128)(2,1)}, u32[]{:S(2)}, u32[]{:S(2)}) collective-permute-start(bf16[128,2048]{1,0:T(8,128)(2,1)} %get-tuple-element.294), channel_id=1, source_target_pairs={{0,24},{8,16},{16,8},{24,0},{1,25},{9,17},{17,9},{25,1},{2,26},{10... | collective-permute-start | bytes 1572872 | tf_op jit(solution)/shard_map/cond/branch_1_fun/ppermute | solution.py:200
  533.5 1.2 collective-permute-start.34
  585.7 17.4 %copy-start.21 = (bf16[256,2048]{1,0:T(8,128)(2,1)S(1)}, bf16[256,2048]{1,0:T(8,128)(2,1)}, u32[]{:S(2)}) copy-start(bf16[256,2048]{1,0:T(8,128)(2,1)} %reduce-scatter.6.cloned.1.call-done) | copy-start | bytes 3145732
  585.7 16.2 %all-to-all-start.7 = ((bf16[8,64,768]{2,1,0:T(8,128)(2,1)}), bf16[8,64,768]{2,1,0:T(8,128)(2,1)S(1)}, u32[]{:S(2)}, u32[]{:S(2)}) async-start(bf16[8,64,768]{2,1,0:T(8,128)(2,1)} %reduce_sum.88), calls=%async_computation.8 | async-start | bytes 1572864 | tf_op jit(solution)/shard_map/all_to_all | solution.py:803
  591.6 4.5 collective-permute-start.4
  596.1 5.1 collective-permute-start.5
  (17 other events, 88.0 us)
Sparse Core Ops, SparseCore 0:
  9.6 30.6 all-gather.3
  42.1 67.5 all-gather.5
  188.4 82.3 all-gather.7
  411.9 86.6 reduce-scatter.3
  502.0 64.5 reduce-scatter.5
  575.4 27.1 reduce-scatter.7
